TPU v7x, 32 devices: a whole 2x2x4 slice. The times are simulated.
32 devices in a mesh: row: 8 (over z, y), col: 4 (over x, core).
Axes of the slice: x: 2, y: 2, z: 4, core: 2. Of those that a mesh axis runs over, the one named last changes fastest.
Arguments:
- init_mean: float32 [256], replicated, may hold values from -6 to 6
- init_var: float32 [256], replicated, may hold values from 0.1 to 2
- decay: float32 [1024, 256], P(('row', 'col')), may hold values from 0 to 1
- coupling: bfloat16 [1024, 256, 256], P(('row', 'col')), may hold values from -0.0234375 to 0.0234375
- obs_map: bfloat16 [1024, 64, 256], P(('row', 'col')), may hold values from -0.375 to 0.375
- gain: bfloat16 [1024, 64, 256], P(('row', 'col')), may hold values from -0.0625 to 0.0625
- noise_factor: bfloat16 [256, 256], replicated, may hold values from -0.02734375 to 0.02734375
- obs_var: float32 [64], replicated, may hold values from 0.25 to 4
- observed: float32 [1024, 64], P(('row', 'col')), may hold values from -6 to 6
Outputs:
- means: float32 [1024, 256], P(('row', 'col'))
- variances: float32 [1024, 256], P(('row', 'col'))
All inputs are finite; a program needn't handle non-finite values.
Results may differ from a plain program's by a relative error of at most 0.00037.
Values sent between devices are 32-bit elements; how exact they have to be, the bound alone decides.
No kernel may reach another device: no remote copies, remote signals or barrier semaphores. Data moves between devices by JAX's collectives and lax.ppermute only.
A program may use at most 128 MiB of HBM per device.

v0:
```python
import jax
import jax.numpy as jnp
from jax import lax
from jax.sharding import PartitionSpec as P

highest = lax.Precision.HIGHEST


def entering(shard, axis, combine, identity):
    size, place = (lax.axis_size(axis), lax.axis_index(axis))
    everything = jax.tree.map(lambda part: lax.all_gather(part, axis), shard)
    start = jax.tree.map(
        lambda part, zero: jnp.broadcast_to(jnp.asarray(zero, part.dtype), part.shape),
        shard,
        identity,
    )

    def hop(k, before):
        reached = k < place
        new = combine(before, jax.tree.map(lambda part: part[k], everything))
        return jax.tree.map(lambda a, b: jnp.where(reached, a, b), new, before)

    return lax.fori_loop(0, size, hop, start)


def broadcast(block, axis, holder):
    block = jnp.where(lax.axis_index(axis) == holder, block, jnp.zeros_like(block))
    return lax.psum(block, axis)


def combine(earlier, later):
    earlier_map, earlier_shift, earlier_noise = earlier
    later_map, later_shift, later_noise = later
    joined_map = jnp.matmul(later_map, earlier_map, precision=highest)
    joined_shift = (
        jnp.einsum("...ij,...j->...i", later_map, earlier_shift, precision=highest) + later_shift
    )
    moved = jnp.matmul(later_map, earlier_noise, precision=highest)
    joined_noise = (
        jnp.matmul(moved, jnp.swapaxes(later_map, -1, -2), precision=highest) + later_noise
    )
    return (joined_map, joined_shift, joined_noise)


def build_steps(decay, coupling, obs_map, gain, noise_factor, obs_var, observed):
    width = decay.shape[1]
    unit = jnp.eye(width, dtype=jnp.float32)
    trans = unit[None] * decay[:, None, :] + coupling.astype(jnp.float32)
    obs_f = obs_map.astype(jnp.float32) * decay[:, None, :] + jnp.einsum(
        "tms,tsr->tmr", obs_map, coupling, preferred_element_type=jnp.float32
    )
    obs_f = obs_f.astype(jnp.bfloat16)
    step_map = trans - jnp.einsum("tms,tmr->tsr", gain, obs_f, preferred_element_type=jnp.float32)
    obs_g = jnp.einsum(
        "tms,sr->tmr", obs_map, noise_factor, preferred_element_type=jnp.float32
    ).astype(jnp.bfloat16)
    shaped = noise_factor.astype(jnp.float32)[None] - jnp.einsum(
        "tms,tmr->tsr", gain, obs_g, preferred_element_type=jnp.float32
    )
    shaped = shaped.astype(jnp.bfloat16)
    weighted = (gain.astype(jnp.float32) * obs_var[None, :, None]).astype(jnp.bfloat16)
    noise = jnp.einsum("tsr,tqr->tsq", shaped, shaped, preferred_element_type=jnp.float32)
    noise = noise + jnp.einsum("tms,tmq->tsq", gain, weighted, preferred_element_type=jnp.float32)
    shift = jnp.einsum("tm,tms->ts", observed, gain.astype(jnp.float32), precision=highest)
    return (step_map, shift, noise)


def per_device(
    init_mean, init_var, decay, coupling, obs_map, gain, noise_factor, obs_var, observed
):
    width = decay.shape[1]
    step_map, shift, noise = build_steps(
        decay, coupling, obs_map, gain, noise_factor, obs_var, observed
    )
    neutral = (
        jnp.eye(width, dtype=jnp.float32),
        jnp.zeros((width,), jnp.float32),
        jnp.zeros((width, width), jnp.float32),
    )

    def accumulate(carry, element):
        merged = combine(carry, element)
        return (merged, merged)

    total, prefixes = lax.scan(accumulate, neutral, (step_map, shift, noise))
    inner = entering(total, "col", combine, neutral)
    row_whole = combine(inner, total)
    row_total = (
        broadcast(row_whole[0], "col", lax.axis_size("col") - 1),
        broadcast(row_whole[1], "col", lax.axis_size("col") - 1),
        broadcast(row_whole[2], "col", lax.axis_size("col") - 1),
    )
    outer = entering(row_total, "row", combine, neutral)
    before = combine(outer, inner)
    carry_map, carry_shift, carry_noise = before
    entry_mean = jnp.dot(carry_map, init_mean, precision=highest) + carry_shift
    entry_cov = jnp.dot(carry_map * init_var[None, :], carry_map.T, precision=highest) + carry_noise
    prefix_maps, prefix_shifts, prefix_noises = prefixes
    means = jnp.einsum("tij,j->ti", prefix_maps, entry_mean, precision=highest) + prefix_shifts
    moved = jnp.einsum("tij,jk->tik", prefix_maps, entry_cov, precision=highest)
    variances = jnp.sum(moved * prefix_maps, axis=2) + jnp.diagonal(prefix_noises, axis1=1, axis2=2)
    return (means, variances)


def solution(mesh):
    return jax.shard_map(
        per_device,
        mesh=mesh,
        in_specs=(
            P(),
            P(),
            P(("row", "col"), None),
            P(("row", "col"), None, None),
            P(("row", "col"), None, None),
            P(("row", "col"), None, None),
            P(),
            P(),
            P(("row", "col"), None),
        ),
        out_specs=(P(("row", "col"), None), P(("row", "col"), None)),
        check_vma=False,
    )
```

profile of v0, /device:TPU:0, one launch (start us, length us, event | category | flops | bytes accessed | tf_op | source)
XLA Modules:
  0.0 555.4 jit_solution(13868768000205400363)
XLA Ops:
  7.5 6.6 %copy.28 = bf16[32,256,256]{1,2,0:T(8,128)(2,1)} copy(bf16[32,256,256]{2,1,0:T(8,128)(2,1)} %param.18) | data formatting | bytes 8388608 | tf_op args[3]
  15.7 5.2 fusion.65
  21.4 6.7 %bitcast_subtract_fusion.1 = f32[32,256,256]{1,2,0:T(8,128)} fusion(bf16[32,256,256]{1,2,0:T(8,128)(2,1)} %copy.28, f32[32,256]{1,0:T(8,128)S(1)} %copy-done.10, f32[256,256]{0,1:T(8,128)S(1)} %copy.27, bf16[32,64,256]{2,1,0:T(8,128)(2,1)S(1)} %copy-done.4, bf16[32,64,256]{2,1,0:T(8,128)(2,1)S(1)} %copy-done.7, bf16[32,256,256]{2,1,0:T(8,128)(2,1)} %param.18), kind=kOutput, calls=%fused_computation.76 | convolution fusion | flops 547356672 | bytes 19169280 | tf_op jit(solution)/shard_map/tms,tmr->tsr/dot_general | solution.py:53
  28.1 11.0 %bitcast_add_fusion = f32[32,256,256]{2,1,0:T(8,128)} fusion(f32[32,256,256]{1,2,0:T(8,128)} %fusion.65, f32[256,256]{0,1:T(8,128)S(1)} %copy.29, bf16[32,64,256]{2,1,0:T(8,128)(2,1)} %convolution_convert_fusion, bf16[32,64,256]{2,1,0:T(8,128)(2,1)S(1)} %copy-done.4), kind=kOutput, calls=%fused_computation.73 | convolution fusion | flops 1348468736 | bytes 19136512 | tf_op jit(solution)/shard_map/tsr,tqr->tsq/dot_general | solution.py:62
  39.1 231.4 %while.57 = (s32[]{:T(128)}, f32[256,256]{1,0:T(8,128)S(1)}, f32[256]{0:T(256)S(1)}, f32[256,256]{1,0:T(8,128)S(1)}, f32[32,256,256]{2,1,0:T(8,128)}, /*index=5*...) while((s32[]{:T(128)}, f32[256,256]{1,0:T(8,128)S(1)}, ...), condition=%wide.region_1.2_spmd.clone, body=%wide.region_0.1_spmd.clone.sunk | while | flops 604897792 | bytes 3946632 | solution.py:85
  44.1 2.3 bitcast_dynamic-update-slice_fusion.4
  51.3 2.3 bitcast_dynamic-update-slice_fusion.4
  58.6 2.3 bitcast_dynamic-update-slice_fusion.4
  65.8 2.3 bitcast_dynamic-update-slice_fusion.4
  73.1 2.3 bitcast_dynamic-update-slice_fusion.4
  80.3 2.2 bitcast_dynamic-update-slice_fusion.4
  87.5 2.2 bitcast_dynamic-update-slice_fusion.4
  94.7 2.3 bitcast_dynamic-update-slice_fusion.4
  102.0 2.3 bitcast_dynamic-update-slice_fusion.4
  109.2 2.2 bitcast_dynamic-update-slice_fusion.4
  116.5 2.2 bitcast_dynamic-update-slice_fusion.4
  123.7 2.3 bitcast_dynamic-update-slice_fusion.4
  130.9 2.3 bitcast_dynamic-update-slice_fusion.4
  138.2 2.3 bitcast_dynamic-update-slice_fusion.4
  145.4 2.3 bitcast_dynamic-update-slice_fusion.4
  152.6 2.3 bitcast_dynamic-update-slice_fusion.4
  167.1 2.3 bitcast_dynamic-update-slice_fusion.4
  174.3 2.3 bitcast_dynamic-update-slice_fusion.4
  181.6 2.2 bitcast_dynamic-update-slice_fusion.4
  188.8 2.3 bitcast_dynamic-update-slice_fusion.4
  203.2 2.3 bitcast_dynamic-update-slice_fusion.4
  210.5 2.3 bitcast_dynamic-update-slice_fusion.4
  217.7 2.2 bitcast_dynamic-update-slice_fusion.4
  225.0 2.2 bitcast_dynamic-update-slice_fusion.4
  239.4 2.3 bitcast_dynamic-update-slice_fusion.4
  246.6 2.3 bitcast_dynamic-update-slice_fusion.4
  253.8 2.3 bitcast_dynamic-update-slice_fusion.4
  261.1 2.3 bitcast_dynamic-update-slice_fusion.4
  268.3 2.3 bitcast_dynamic-update-slice_fusion.4
  272.1 6.2 %all-gather.3 = f32[4,1,256]{2,1,0:T(1,128)S(1)} all-gather(f32[1,1,256]{2,1,0:T(1,128)S(1)} %bitcast.221), channel_id=3, replica_groups=mesh['row'=8,'col'=4] {'col'}, dimensions={0}, use_global_device_ids=true | all-gather | bytes 5120 | tf_op jit(solution)/shard_map/all_gather | solution.py:11
  278.3 12.6 %all-gather.14.cloned.1.call-done = f32[1024,256]{1,0:T(8,128)} async-done(((f32[256,256]{1,0:T(8,128)}), f32[1024,256]{1,0:T(8,128)}) %all-gather.14.cloned.1.call-update) | async-done | bytes 1048592 | tf_op jit(solution)/shard_map/all_gather | solution.py:11
  290.9 18.3 %all-gather.16.cloned.1.call-done = f32[1024,256]{1,0:T(8,128)} async-done(((f32[256,256]{1,0:T(8,128)}), f32[1024,256]{1,0:T(8,128)}) %all-gather.16.cloned.1.call-update) | async-done | bytes 1048592 | tf_op jit(solution)/shard_map/all_gather | solution.py:11
  309.2 22.2 %while.58 = (s32[]{:T(128)}, f32[256,256]{1,0:T(8,128)S(1)}, f32[256]{0:T(256)S(1)}, f32[256,256]{1,0:T(8,128)S(1)}, s32[]{:T(128)}, /*index=5*/f32[4,256,256]{2...) while((s32[]{:T(128)}, f32[256,256]{1,0:T(8,128)S(1)}, ...), condition=%wide.region_3.4_spmd.clone, body=%wide.region_2.3_spmd.clone.sunk | while | flops 605094912 | bytes 3945090 | solution.py:23
  334.1 33.3 %all-reduce.3.cloned.1.call-done = (f32[1,256,256]{2,1,0:T(8,128)}, f32[1,256,256]{2,1,0:T(8,128)}) async-done(((f32[1,256,256]{2,1,0:T(8,128)}, f32[1,256,256]{2,1,0:T(8,128)}), (f32[1,256,256]{2,1,0:T(8,128)}, f32[1,256,256]{2,1,0:T(8,128)})) %all-reduce.3.cloned.1.call-update) | async-done | bytes 524304 | tf_op jit(solution)/shard_map/psum | solution.py:28
  368.1 9.0 %copy.35 = f32[32,256,256]{1,2,0:T(8,128)} copy(f32[32,256,256]{2,1,0:T(8,128)} %get-tuple-element.341) | data formatting | bytes 16777216 | tf_op jit(solution)/shard_map/while | solution.py:85
  377.0 19.8 %copy.36 = f32[32,256,256]{0,2,1:T(8,128)} copy(f32[32,256,256]{2,1,0:T(8,128)} %get-tuple-element.352) | data formatting | bytes 16777216 | tf_op jit(solution)/shard_map/while | solution.py:85
  396.8 2.3 gather_fusion
  399.5 6.1 %psum.22 = f32[1,256]{1,0:T(1,128)S(1)} all-reduce(f32[1,256]{1,0:T(1,128)S(1)} %bitcast.239), channel_id=1, replica_groups=mesh['row'=8,'col'=4] {'col'}, use_global_device_ids=true, to_apply=%region_5.6 | all-reduce | flops 256 | bytes 2048 | tf_op jit(solution)/shard_map/psum | solution.py:28
  405.5 20.5 %all-gather.4 = f32[8,1,256]{2,1,0:T(1,128)S(1)} all-gather(f32[1,1,256]{2,1,0:T(1,128)S(1)} %bitcast.240), channel_id=1, replica_groups=mesh['row'=8,'col'=4] {'row'}, dimensions={0}, use_global_device_ids=true | all-gather | bytes 9216 | tf_op jit(solution)/shard_map/all_gather | solution.py:11
  426.1 42.7 %all-gather.12.cloned.1.call-done = f32[8,256,256]{2,1,0:T(8,128)} async-done(((f32[1,256,256]{2,1,0:T(8,128)}), f32[8,256,256]{2,1,0:T(8,128)}) %all-gather.12.cloned.1.call-update) | async-done | bytes 2097168 | tf_op jit(solution)/shard_map/all_gather | solution.py:11
  468.8 44.4 %while.59 = (s32[]{:T(128)}, f32[256,256]{1,0:T(8,128)S(1)}, f32[256]{0:T(256)S(1)}, f32[256,256]{1,0:T(8,128)S(1)}, s32[]{:T(128)}, /*index=5*/f32[8,256,256]{2...) while((s32[]{:T(128)}, f32[256,256]{1,0:T(8,128)S(1)}, ...), condition=%wide.region_8.9_spmd.clone, body=%wide.region_7.8_spmd.clone.sunk | while | flops 605094912 | bytes 3945090 | solution.py:23
  514.8 22.3 %multiply_reduce_fusion = f32[32,256]{1,0:T(8,128)S(1)} fusion(f32[32,256,256]{1,2,0:T(8,128)} %copy.35, f32[32,256,256]{2,1,0:T(8,128)} %get-tuple-element.341, f32[256,256,1]{1,0,2:T(8,128)S(1)} %fusion.67), kind=kOutput, calls=%fused_computation.77 | convolution fusion | flops 6446637056 | bytes 17072128 | tf_op jit(solution)/shard_map/tij,jk->tik/dot_general | solution.py:100
  538.6 9.7 %fusion.84 = f32[1,32,256]{2,0,1:T(1,128)S(1)} fusion(f32[32,256,256]{2,1,0:T(8,128)} %get-tuple-element.341, f32[256,1,1]{0,1,2:T(1,128)S(1)} %bitcast.237), kind=kOutput, calls=%fused_computation.115 | convolution fusion | flops 25165824 | bytes 8422400 | tf_op jit(solution)/shard_map/tij,j->ti/dot_general | solution.py:99
  (430 shorter events, 241.6 us)
Async XLA Ops:
  7.2 13.7 %copy-start = (f32[32,64]{1,0:T(8,128)S(1)}, f32[32,64]{1,0:T(8,128)}, u32[]{:S(2)}) copy-start(f32[32,64]{1,0:T(8,128)} %param.23) | copy-start | bytes 24580
  7.2 7.0 %copy-start.8 = (bf16[256,256]{1,0:T(8,128)(2,1)S(1)}, bf16[256,256]{1,0:T(8,128)(2,1)}, u32[]{:S(2)}) copy-start(bf16[256,256]{1,0:T(8,128)(2,1)} %param.21) | copy-start | bytes 393220
  7.2 7.0 %copy-start.7 = (bf16[32,64,256]{2,1,0:T(8,128)(2,1)S(1)}, bf16[32,64,256]{2,1,0:T(8,128)(2,1)}, u32[]{:S(2)}) copy-start(bf16[32,64,256]{2,1,0:T(8,128)(2,1)} %param.19) | copy-start | bytes 3145732
  7.2 8.5 %copy-start.4 = (bf16[32,64,256]{2,1,0:T(8,128)(2,1)S(1)}, bf16[32,64,256]{2,1,0:T(8,128)(2,1)}, u32[]{:S(2)}) copy-start(bf16[32,64,256]{2,1,0:T(8,128)(2,1)} %param.20) | copy-start | bytes 3145732
  7.2 283.7 %all-gather.14.cloned.1.call-start = ((), (), s32[]{:S(2)}) async-start(), calls=%async_computation.2 | async-start | bytes 1310720 | tf_op jit(solution)/shard_map/all_gather | solution.py:11
  15.7 5.7 %copy-start.10 = (f32[32,256]{1,0:T(8,128)S(1)}, f32[32,256]{1,0:T(8,128)}, u32[]{:S(2)}) copy-start(f32[32,256]{1,0:T(8,128)} %param.17) | copy-start | bytes 98308
  28.1 11.0 %copy-start.9 = (f32[256]{0:T(256)S(1)}, f32[256]{0:T(256)}, u32[]{:S(2)}) copy-start(f32[256]{0:T(256)} %custom-call.2) | copy-start | bytes 3076
  28.1 11.0 %copy-start.11 = (f32[32,256]{1,0:T(8,128)S(1)}, f32[32,256]{1,0:T(8,128)}, u32[]{:S(2)}) copy-start(f32[32,256]{1,0:T(8,128)} %custom-call.9) | copy-start | bytes 98308
  270.6 0.7 copy-start.2
  270.6 0.8 copy-start.5
  271.3 37.9 %all-gather.16.cloned.1.call-start = ((), (), s32[]{:S(2)}) async-start(), calls=%async_computation.3 | async-start | bytes 1310720 | tf_op jit(solution)/shard_map/all_gather | solution.py:11
  272.0 95.4 %all-reduce.3.cloned.1.call-start = ((), (), s32[]{:S(2)}) async-start(), calls=%async_computation.4 | async-start | bytes 1048576 | tf_op jit(solution)/shard_map/psum | solution.py:28
  309.2 22.3 %copy-start.3 = (f32[256,256]{1,0:T(8,128)S(1)}, f32[256,256]{1,0:T(8,128)}, u32[]{:S(2)}) copy-start(f32[256,256]{1,0:T(8,128)} %copy-done.2) | copy-start | bytes 786436
  309.2 22.6 %copy-start.6 = (f32[256,256]{1,0:T(8,128)S(1)}, f32[256,256]{1,0:T(8,128)}, u32[]{:S(2)}) copy-start(f32[256,256]{1,0:T(8,128)} %copy-done.5) | copy-start | bytes 786436
  334.1 92.0 %all-gather.10.cloned.1.call-start = ((), (), s32[]{:S(2)}) async-start(), calls=%async_computation | async-start | bytes 2359296 | tf_op jit(solution)/shard_map/all_gather | solution.py:11
  367.5 101.3 %all-gather.12.cloned.1.call-start = ((), (), s32[]{:S(2)}) async-start(), calls=%async_computation.1 | async-start | bytes 2359296 | tf_op jit(solution)/shard_map/all_gather | solution.py:11
  468.8 45.2 %copy-start.12 = (f32[256]{0:T(256)S(1)}, f32[256]{0:T(256)}, u32[]{:S(2)}) copy-start(f32[256]{0:T(256)} %param.16) | copy-start | bytes 3076
  514.8 23.4 %copy-start.13 = (f32[256]{0:T(256)S(1)}, f32[256]{0:T(256)}, u32[]{:S(2)}) copy-start(f32[256]{0:T(256)} %param.15) | copy-start | bytes 3076
  514.8 34.1 %copy-start.1 = (f32[32,64]{1,0:T(8,128)S(1)}, f32[32,64]{1,0:T(8,128)}, u32[]{:S(2)}) copy-start(f32[32,64]{1,0:T(8,128)} %param.23) | copy-start | bytes 24580
Sparse Core Ops, SparseCore 0:
  271.4 19.4 all-gather.13
  292.4 16.7 all-gather.15
  334.2 33.1 all-reduce.2
  369.4 49.5 all-gather.9
  421.0 47.7 all-gather.11
where the time goes:
time: 561 us; the launch traced here: 555 us
  matrix products  353 us (63%)
  waiting for transfers between devices  108 us (19%)
  local copies, waits for them, and re-layouts  43.6 us (8%)
  blocking collectives  32.7 us (6%)
  between operations  14.1 us (3%)
    dot_general x46, matrix products, combine(): joined_map = jnp.matmul(later_map, earlier_map, precision=highest)  89.8 us
    dot_general x46, matrix products, combine(): jnp.matmul(moved, jnp.swapaxes(later_map, -1, -2), precision=highest)  87.4 us
    all_gather x4, waiting for transfers between devices, entering(): everything = jax.tree.map(lambda part: lax.all_gather(part, axis), shard)  73.6 us
    dot_general x46, matrix products, combine(): moved = jnp.matmul(later_map, earlier_noise, precision=highest)  66.4 us
    dot_general x46, matrix products, combine(): jnp.einsum('...ij,...j->...i', later_map, earlier_shift, precision=highest)  52.3 us
    psum x1, waiting for transfers between devices, broadcast(): return lax.psum(block, axis)  33.3 us
    while x2, local copies, waits for them, and re-layouts, per_device(): total, prefixes = lax.scan(accumulate, neutral, (step_map, shift, noise))  28.7 us
    all_gather x2, blocking collectives, entering(): everything = jax.tree.map(lambda part: lax.all_gather(part, axis), shard)  26.7 us
  transfers between devices with their start and end apart: 5, of which 4 were waited for; matrix products, arithmetic and copies ran while one was open for 6% of the time, Pallas kernels for 0%

commit v1 on v0

v1 whole, which is shorter than its diff:
```python
import functools
import jax
import jax.numpy as jnp
from jax import lax
from jax.experimental import pallas as pl
from jax.experimental.pallas import tpu as pltpu
from jax.sharding import PartitionSpec as P

f32, bf16 = jnp.float32, jnp.bfloat16
VMEM_LIMIT = 56 * 1024 * 1024


def nn(a, b):
    return jnp.dot(a, b, preferred_element_type=f32)


def nt(a, b):
    return lax.dot_general(a, b, (((1,), (1,)), ((), ())), preferred_element_type=f32)


def halves(x):
    high = x.astype(bf16)
    return high, (x - high.astype(f32)).astype(bf16)


def nn3(a, b):
    ah, al = halves(a)
    bh, bl = halves(b)
    return nn(ah, bh) + (nn(al, bh) + nn(ah, bl))


def nt3(a, b):
    ah, al = halves(a)
    bh, bl = halves(b)
    return nt(ah, bh) + (nt(al, bh) + nt(ah, bl))


def eye_mask(n):
    return lax.broadcasted_iota(jnp.int32, (n, n), 0) == lax.broadcasted_iota(jnp.int32, (n, n), 1)


def column(row):
    n = row.shape[1]
    out = []
    for k in range(0, n, 128):
        m = min(128, n - k)
        out.append(jnp.sum(jnp.where(eye_mask(m), row[:, k:k + m], 0.0), axis=1, keepdims=True))
    return out[0] if len(out) == 1 else jnp.concatenate(out, axis=0)


def diag_row(x):
    n = x.shape[1]
    out = []
    for k in range(0, n, 128):
        out.append(jnp.sum(jnp.where(eye_mask(128), x[k:k + 128, k:k + 128], 0.0), axis=0, keepdims=True))
    return jnp.concatenate(out, axis=1)


def joined(early, late):
    em, en, es = early
    lm, ln, ls = late
    n = em.shape[1]
    lh, ll = halves(lm)
    eh, el = halves(jnp.concatenate([em, en], axis=1))
    both = nn(lh, eh) + (nn(ll, eh) + nn(lh, el))
    xh, xl = halves(jnp.concatenate([both[:, n:], es], axis=0))
    out = nt(xh, lh) + (nt(xl, lh) + nt(xh, ll))
    return both[:, :n], out[:n] + ln, out[n:] + ls


def rank_of(axes):
    rank = 0
    for name, size in axes:
        rank = rank * size + lax.axis_index(name)
    return rank


def load(x):
    n = x.shape[1]
    return x[:n], x[n:2 * n], x[2 * n:]


def store(ref, at, element):
    n = ref.shape[-1]
    em, en, es = element
    ref[(*at, pl.ds(0, n), slice(None))] = em
    ref[(*at, pl.ds(n, n), slice(None))] = en
    ref[(*at, pl.ds(2 * n, es.shape[0]), slice(None))] = es


def choose(flag, a, b):
    return tuple(jnp.where(flag, x, y) for x, y in zip(a, b))


def identity(n):
    return jnp.where(eye_mask(n), 1.0, 0.0), jnp.zeros((n, n), f32), jnp.zeros((16, n), f32)


def local_kernel(subs, axes, mean_ref, init_ref, decay_ref, coup_ref, omap_ref, gain_ref, nf_ref, var_ref, seen_ref,
                 g_ref, delta_ref, shift_ref, diag_ref, sub_ref, total_ref, g_s, q_s, d_s, b_s):
    j = pl.program_id(0)
    steps = pl.num_programs(0)
    n = nf_ref.shape[0]
    m = omap_ref.shape[2]

    @pl.when(j == 0)
    def _():
        g_s[...] = jnp.zeros_like(g_s)
        q_s[...] = jnp.zeros_like(q_s)
        b_s[...] = jnp.zeros_like(b_s)
        d_s[...] = jnp.ones_like(d_s)

    @pl.when((j == 0) & (rank_of(axes) == 0))
    def _():
        q_s[0] = jnp.where(eye_mask(n), init_ref[...], 0.0)
        b_s[0] = jnp.broadcast_to(mean_ref[...], b_s.shape[1:])
        d_s[0] = jnp.zeros_like(d_s[0])

    nf = nf_ref[...]
    var_col = column(var_ref[...])
    obs_g = nn(omap_ref[...].reshape(subs * m, n), nf).astype(bf16)
    for s in range(subs):
        t = s * steps + j
        d_row = decay_ref[pl.ds(t, 1), :]
        d_col = column(d_row)
        coup = coup_ref[s, 0]
        gain = gain_ref[s, 0]
        omap = omap_ref[s, 0]
        gain32 = gain.astype(f32)
        obs_f = (omap.astype(f32) * d_row + nn(omap, coup)).astype(bf16)
        weighted = (gain32 * var_col).astype(bf16)
        gain_t = gain.T
        e = coup.astype(f32) - nn(gain_t, obs_f)
        shaped = (nf.astype(f32) - nn(gain_t, obs_g[s * m:(s + 1) * m])).astype(bf16)
        noise = nt(shaped, shaped) + nn(gain_t, weighted)
        shift = jnp.sum(gain32 * column(seen_ref[pl.ds(t, 1), :]), axis=0, keepdims=True)
        e_h, e_l = halves(e)
        g = g_s[s]
        q = q_s[s]
        delta = d_s[s, 0:1, :]
        b = b_s[s]
        g_new = d_col * g + e * delta + nn(e_h, g.astype(bf16))
        x = d_col * q + nn(e_h, q.astype(bf16))
        b_h, b_l = halves(b)
        y = nt(jnp.concatenate([x.astype(bf16), b_h, b_l], axis=0), e_h)
        q_new = x * d_row + y[:n] + noise
        b_new = d_row * b + (y[n:n + 16] + y[n + 16:] + nt(b_h, e_l)) + shift
        delta = delta * d_row
        g_s[s] = g_new
        q_s[s] = q_new
        b_s[s] = b_new
        d_s[s] = jnp.broadcast_to(delta, d_s.shape[1:])
        g_ref[s, 0] = g_new
        delta_ref[pl.ds(t, 1), :] = delta
        shift_ref[pl.ds(t, 1), :] = b_new[0:1, :]
        diag_ref[pl.ds(t, 1), :] = diag_row(q_new)

    @pl.when(j == steps - 1)
    def _():
        eye = eye_mask(n)
        for s in range(subs):
            sub_ref[s, 0:n, :] = g_s[s] + jnp.where(eye, d_s[s, 0:1, :], 0.0)
            sub_ref[s, n:2 * n, :] = q_s[s]
            sub_ref[s, 2 * n:, :] = b_s[s]
        pairs = [joined(load(sub_ref[s]), load(sub_ref[s + 1])) for s in (0, 2)]
        store(sub_ref, (subs,), pairs[0])
        store(total_ref, (), joined(*pairs))


def local_call(axes, init_mean, init_var, decay, coupling, obs_map, gain, noise_factor, obs_var, observed, subs=4):
    T, n = decay.shape
    m = obs_map.shape[1]
    steps = T // subs
    blk = lambda a, b: pl.BlockSpec((subs, 1, a, b), lambda j: (0, j, 0, 0))
    full = lambda *sh: pl.BlockSpec(sh, lambda j: (0,) * len(sh))
    return pl.pallas_call(
        functools.partial(local_kernel, subs, axes),
        grid=(steps,),
        in_specs=[full(1, n), full(1, n), full(T, n), blk(n, n), blk(m, n), blk(m, n), full(n, n), full(1, m), full(T, m)],
        out_specs=[blk(n, n), full(T, n), full(T, n), full(T, n),
                   full(subs + 1, 2 * n + 16, n), full(2 * n + 16, n)],
        out_shape=[
            jax.ShapeDtypeStruct((subs, steps, n, n), f32),
            jax.ShapeDtypeStruct((T, n), f32),
            jax.ShapeDtypeStruct((T, n), f32),
            jax.ShapeDtypeStruct((T, n), f32),
            jax.ShapeDtypeStruct((subs + 1, 2 * n + 16, n), f32),
            jax.ShapeDtypeStruct((2 * n + 16, n), f32),
        ],
        scratch_shapes=[
            pltpu.VMEM((subs, n, n), f32),
            pltpu.VMEM((subs, n, n), f32),
            pltpu.VMEM((subs, 8, n), f32),
            pltpu.VMEM((subs, 16, n), f32),
        ],
        compiler_params=pltpu.CompilerParams(vmem_limit_bytes=VMEM_LIMIT),
        name="local_steps",
    )(init_mean.reshape(1, n), init_var.reshape(1, n), decay, coupling.reshape(subs, steps, n, n), obs_map.reshape(subs, steps, m, n),
      gain.reshape(subs, steps, m, n), noise_factor, obs_var.reshape(1, m), observed)


def core_kernel(axes, own_ref, other_ref, total_ref, half_ref):
    upper = rank_of(axes) % 2 == 1
    own, other = load(own_ref[...]), load(other_ref[...])
    store(total_ref, (), joined(choose(upper, other, own), choose(upper, own, other)))
    put_half(half_ref, total_ref, upper)


def put_half(half_ref, total_ref, upper):
    rows = half_ref.shape[0]
    skip = total_ref.shape[0] - 2 * rows
    half_ref[...] = jnp.where(upper, total_ref[skip + rows:], total_ref[skip:skip + rows])


def whole(upper, mine_ref, others_ref):
    mine, others = mine_ref[...], others_ref[...]
    return jnp.concatenate([jnp.where(upper, others, mine), jnp.where(upper, mine, others)], axis=0)


def plane_kernel(axes, own_ref, r2, x2, r4, x4, r6, x6, token_ref, total_ref, half_ref, other_ref, first_ref):
    rank = rank_of(axes)
    upper, xbit, ybit = rank % 2 == 1, (rank // 2) % 2 == 1, (rank // 4) % 2 == 1
    own = load(own_ref[...])
    near = load(whole(upper, r2, x2))
    far = load(whole(upper, r4, x4))
    cross = load(whole(upper, r6, x6))
    first = choose(xbit, near, own)
    mine = joined(first, choose(xbit, own, near))
    other = joined(choose(xbit, cross, far), choose(xbit, far, cross))
    store(first_ref, (), first)
    store(other_ref, (), other)
    store(total_ref, (), joined(choose(ybit, other, mine), choose(ybit, mine, other)))
    put_half(half_ref, total_ref, upper)


def prefix_kernel(axes, first_ref, other_ref, core_ref, out_ref):
    rank = rank_of(axes)
    upper, xbit, ybit = rank % 2 == 1, (rank // 2) % 2 == 1, (rank // 4) % 2 == 1
    n = out_ref.shape[1]
    first = choose(xbit, load(first_ref[...]), identity(n))
    other = choose(ybit, load(other_ref[...]), identity(n))
    before = joined(other, first)
    store(out_ref, (), choose(upper, joined(before, load(core_ref[...])), before))


def level_kernel(axes, bit, own_ref, prefix_ref, r_ref, x_ref, total_ref, half_ref, out_ref):
    rank = rank_of(axes)
    upper, high = rank % 2 == 1, (rank // bit) % 2 == 1
    n = own_ref.shape[1]
    other = load(whole(upper, r_ref, x_ref))
    own = load(own_ref[...])
    store(total_ref, (), joined(choose(high, other, own), choose(high, own, other)))
    store(out_ref, (), choose(high, joined(other, load(prefix_ref[...])), load(prefix_ref[...])))
    put_half(half_ref, total_ref, upper)


def carry(element, noise, shift):
    em, en, es = element
    n = em.shape[1]
    lh, ll = halves(em)
    eh, el = halves(noise)
    x = nn(lh, eh) + (nn(ll, eh) + nn(lh, el))
    xh, xl = halves(jnp.concatenate([x, shift], axis=0))
    out = nt(xh, lh) + (nt(xl, lh) + nt(xh, ll))
    return out[:n] + en, out[n:] + es


def compose_kernel(per, g_ref, delta_ref, shift_ref, diag_ref, sub_ref, after_ref, out_ref, var_ref, mean_ref,
                   stack_s, col_s):
    s, i = pl.program_id(0), pl.program_id(1)
    n = g_ref.shape[-1]

    def use(element):
        stack_s[0:n, :] = element[0].T
        stack_s[n:2 * n, :] = element[1]
        col_s[...] = jnp.broadcast_to(column(element[2][0:1, :]), (n, 128))

    @pl.when((i == 0) & (s == 0))
    def _():
        use(identity(n))

    @pl.when((i == 0) & (s == 1))
    def _():
        use(load(sub_ref[0]))

    @pl.when((i == 0) & (s == 2))
    def _():
        use(load(sub_ref[4]))

    @pl.when((i == 0) & (s == 3))
    def _():
        use(joined(load(sub_ref[4]), load(sub_ref[2])))

    eye = eye_mask(n)
    lh, ll = halves(stack_s[...])
    col = jnp.concatenate([col_s[...], col_s[...]], axis=1)
    for k in range(per):
        t = (s * pl.num_programs(1) + i) * per + k
        phi = (g_ref[k] + jnp.where(eye, delta_ref[pl.ds(t, 1), :], 0.0)).T
        ph, plo = halves(phi)
        both = nn(lh, ph) + (nn(ll, ph) + nn(lh, plo))
        out_ref[k] = both[:n]
        var_ref[pl.ds(t, 1), :] = diag_ref[pl.ds(t, 1), :] + jnp.sum(phi * both[n:], axis=0, keepdims=True)
        mean_ref[pl.ds(t, 1), :] = shift_ref[pl.ds(t, 1), :] + jnp.sum(phi * col, axis=0, keepdims=True)


def finish_kernel(axes, bit, per, psi_ref, var_ref, mean_ref, place_ref, prefix_ref, r_ref, x_ref, means_ref, vars_ref,
                  p_s, col_s):
    i = pl.program_id(0)
    n = psi_ref.shape[-1]

    @pl.when(i == 0)
    def _():
        rank = rank_of(axes)
        upper, high = rank % 2 == 1, (rank // bit) % 2 == 1
        state = whole(upper, r_ref, x_ref)
        prefix = load(prefix_ref[...])
        noise, shift = carry(prefix, state[:n], state[n:])
        noise, shift = jnp.where(high, noise, prefix[1]), jnp.where(high, shift, prefix[2])
        noise, shift = carry(load(place_ref[...]), noise, shift)
        p_s[...] = noise
        col_s[...] = jnp.broadcast_to(column(shift[0:1, :]), (n, 128))

    eye = eye_mask(n)
    p = p_s[...]
    ph = p.astype(bf16)
    col = jnp.concatenate([col_s[...], col_s[...]], axis=1)
    for k in range(per):
        t = i * per + k
        psi = psi_ref[k]
        w = nn(ph, jnp.where(eye, 0.0, psi).astype(bf16)) + p * diag_row(psi)
        vars_ref[pl.ds(t, 1), :] = var_ref[pl.ds(t, 1), :] + jnp.sum(psi * w, axis=0, keepdims=True)
        means_ref[pl.ds(t, 1), :] = mean_ref[pl.ds(t, 1), :] + jnp.sum(psi * col, axis=0, keepdims=True)


PARAMS = pltpu.CompilerParams(vmem_limit_bytes=VMEM_LIMIT)


def call(kernel, name, shapes, *args):
    return pl.pallas_call(
        kernel,
        in_specs=[pl.BlockSpec(memory_space=pltpu.VMEM)] * len(args),
        out_specs=[pl.BlockSpec(memory_space=pltpu.VMEM)] * len(shapes),
        out_shape=[jax.ShapeDtypeStruct(s, f32) for s in shapes],
        compiler_params=PARAMS,
        name=name,
    )(*args)


def compose_call(g, delta, shift, diag, sub, after, per=4):
    subs, steps, n, _ = g.shape
    T = subs * steps
    full = lambda *sh: pl.BlockSpec(sh, lambda s, i: (0,) * len(sh))
    blk = pl.BlockSpec((per, n, n), lambda s, i: (s * (steps // per) + i, 0, 0))
    return pl.pallas_call(
        functools.partial(compose_kernel, per),
        grid=(subs, steps // per),
        in_specs=[blk, full(T, n), full(T, n), full(T, n), full(*sub.shape), pl.BlockSpec(memory_space=pl.ANY)],
        out_specs=[blk, full(T, n), full(T, n)],
        out_shape=[jax.ShapeDtypeStruct((T, n, n), f32), jax.ShapeDtypeStruct((T, n), f32),
                   jax.ShapeDtypeStruct((T, n), f32)],
        scratch_shapes=[pltpu.VMEM((2 * n, n), f32), pltpu.VMEM((n, 128), f32)],
        compiler_params=PARAMS,
        name="compose_steps",
    )(g.reshape(T, n, n), delta, shift, diag, sub, after)


def finish_call(axes, bit, psi, var, mean, place, prefix, r, x, per=4):
    T, n, _ = psi.shape
    full = lambda *sh: pl.BlockSpec(sh, lambda i: (0,) * len(sh))
    return pl.pallas_call(
        functools.partial(finish_kernel, axes, bit, per),
        grid=(T // per,),
        in_specs=[pl.BlockSpec((per, n, n), lambda i: (i, 0, 0)), full(T, n), full(T, n), full(*place.shape),
                  full(*prefix.shape), full(*r.shape), full(*x.shape)],
        out_specs=[full(T, n), full(T, n)],
        out_shape=[jax.ShapeDtypeStruct((T, n), f32)] * 2,
        scratch_shapes=[pltpu.VMEM((n, n), f32), pltpu.VMEM((n, 128), f32)],
        compiler_params=PARAMS,
        name="finish_steps",
    )(psi, var, mean, place, prefix, r, x)


def per_device(axes, init_mean, init_var, decay, coupling, obs_map, gain, noise_factor, obs_var, observed):
    n = decay.shape[1]
    count = 1
    for _, size in axes:
        count *= size
    names = tuple(name for name, _ in axes)

    def swap(x, bit):
        return lax.ppermute(x, names, [(k, k ^ bit) for k in range(count)])

    rows = 2 * n + 16
    part = rows // 2
    g, delta, shift, diag, sub, own = local_call(
        axes, init_mean, init_var, decay, coupling, obs_map, gain, noise_factor, obs_var, observed)
    other = swap(own, 1)
    chip, half = call(functools.partial(core_kernel, axes), "core_join", [(rows, n), (part, n)], own, other)
    got = [swap(half, bit) for bit in (2, 4, 6)]
    psi, var, mean = compose_call(g, delta, shift, diag, sub, chip)
    both = [x for r in got for x in (r, swap(r, 1))]
    bits = []
    bit = 8
    while bit < count:
        bits.append(bit)
        bit *= 2
    small = (n + 16) // 2
    total, half, second, first = call(
        functools.partial(plane_kernel, axes), "plane_join",
        [(rows, n), (part if len(bits) > 1 else small, n), (rows, n), (rows, n)], chip, *both, var)
    (place,) = call(functools.partial(prefix_kernel, axes), "place_join", [(rows, n)], first, second, other)
    prefix = jnp.concatenate([jnp.eye(n, dtype=f32), jnp.zeros((rows - n, n), f32)], axis=0)
    for k, bit in enumerate(bits[:-1]):
        r = swap(half, bit)
        total, half, prefix = call(
            functools.partial(level_kernel, axes, bit), "level_join",
            [(rows, n), (part if k < len(bits) - 2 else small, n), (rows, n)], total, prefix, r, swap(r, 1))
    r = swap(half, bits[-1])
    return tuple(finish_call(axes, bits[-1], psi, var, mean, place, prefix, r, swap(r, 1)))


def solution(mesh):
    axes = tuple((name, mesh.shape[name]) for name in mesh.axis_names)
    time = P(tuple(mesh.axis_names))
    return jax.shard_map(
        functools.partial(per_device, axes),
        mesh=mesh,
        in_specs=(P(), P(), time, time, time, time, P(), P(), time),
        out_specs=(time, time),
        check_vma=False,
    )
```

time: 561 us -> 104 us (0.19)
  matrix products: 353 us -> 0 us
  waiting for transfers between devices: 108 us -> 29.5 us
  Pallas kernels: 0 us -> 59.9 us
  local copies, waits for them, and re-layouts: 43.6 us -> 2.98 us
  blocking collectives: 32.7 us -> 0 us
  between operations: 14.1 us -> 0.74 us
  starting transfers between devices: 0.2 us -> 9.55 us
    dot_general x193 -> x0, matrix products: 353 us -> none  [the longest x46 89.8 us: combine(): joined_map = jnp.matmul(later_map, earlier_map, precision=highest)]
    all_gather x4 -> x0, waiting for transfers between devices: 73.6 us -> none  [entering(): everything = jax.tree.map(lambda part: lax.all_gather(part, axis), shard)]
    pallas_call x0 -> x7, Pallas kernels: none -> 59.9 us  [the longest x1 21.2 us: local_call(): pl.pallas_call(functools.partial(local_kernel, subs, axes), grid=(steps,)...]
    psum x1 -> x0, waiting for transfers between devices: 33.3 us -> none  [broadcast(): return lax.psum(block, axis)]
    while x46 -> x0, local copies, waits for them, and re-layouts: 29.5 us -> none  [the longest x2 28.7 us: per_device(): total, prefixes = lax.scan(accumulate, neutral, (step_map, shift, noise))]
    ppermute x0 -> x11, waiting for transfers between devices: none -> 29.5 us  [swap(): return lax.ppermute(x, names, [(k, k ^ bit) for k in range(count)])]
    all_gather x2 -> x0, blocking collectives: 26.7 us -> none  [entering(): everything = jax.tree.map(lambda part: lax.all_gather(part, axis), shard)]
    ppermute x0 -> x11, starting transfers between devices: none -> 9.55 us  [swap(): return lax.ppermute(x, names, [(k, k ^ bit) for k in range(count)])]
  transfers between devices with their start and end apart: 5 -> 11, of which waited for: 4 -> 6; matrix products, arithmetic and copies ran while one was open for 6% -> 1% of each run, Pallas kernels for 0% -> 18%
where the time goes in v1:
time: 104 us
  Pallas kernels  59.9 us (58%)
  waiting for transfers between devices  29.5 us (28%)
  starting transfers between devices  9.55 us (9%)
  local copies, waits for them, and re-layouts  2.98 us (3%)
    ppermute x11, waiting for transfers between devices, swap(): return lax.ppermute(x, names, [(k, k ^ bit) for k in range(count)])  29.5 us
    pallas_call x1, Pallas kernels, local_call(): pl.pallas_call(functools.partial(local_kernel, subs, axes), grid=(steps,)...  21.2 us
    pallas_call x1, Pallas kernels, compose_call(): pl.pallas_call(functools.partial(compose_kernel, per), grid=(subs, steps...  15.2 us
    pallas_call x4, Pallas kernels, call(): pl.pallas_call(kernel, in_specs=[pl.BlockSpec(memory_space=pltpu.VMEM)] *...  14 us
    ppermute x11, starting transfers between devices, swap(): return lax.ppermute(x, names, [(k, k ^ bit) for k in range(count)])  9.55 us
    pallas_call x1, Pallas kernels, finish_call(): pl.pallas_call(functools.partial(finish_kernel, axes, bit, per), grid=(T...  9.45 us
    unnamed x22, local copies, waits for them, and re-layouts  2.98 us
  transfers between devices with their start and end apart: 11, of which 6 were waited for; matrix products, arithmetic and copies ran while one was open for 1% of the time, Pallas kernels for 18%

profile of v1, /device:TPU:0, one launch (start us, length us, event | category | flops | bytes accessed | tf_op | source)
XLA Modules:
  0.0 103.5 jit_solution(6935657666346008001)
XLA Ops:
  0.6 21.2 %local_steps.1 = (f32[4,8,256,256]{3,2,1,0:T(8,128)}, f32[32,256]{1,0:T(8,128)}, f32[32,256]{1,0:T(8,128)}, f32[32,256]{1,0:T(8,128)}, f32[5,528,256]{2,1,0:T(8,128)}, /*index=5*/f32[528,256]{1,0:T(8,128)}) custom-call(f32[1,256]{1,0:T(1,128)} %bitcast.11, f32[1,256]{1,0:T(1,128)} %bitcast.12, f32[32,256]{1,0:T(8,128)} %decay_ref.1, ...), custom_call_target="tpu_custom_call" | custom-call | tf_op jit(solution)/shard_map/local_steps/pallas_call | solution.py:176
  21.9 0.5 collective-permute-start
  22.4 1.8 %collective-permute-done.other_ref.core_ref = f32[528,256]{1,0:T(8,128)S(1)} collective-permute-done((f32[528,256]{1,0:T(8,128)}, f32[528,256]{1,0:T(8,128)S(1)}, u32[]{:S(2)}, u32[]{:S(2)}) %collective-permute-start) | collective-permute-done | bytes 540704 | tf_op jit(solution)/shard_map/ppermute | solution.py:392
  24.1 0.0 copy-start
  24.1 0.8 copy-done
  24.9 2.8 %core_join.1 = (f32[528,256]{1,0:T(8,128)}, f32[264,256]{1,0:T(8,128)}) custom-call(f32[528,256]{1,0:T(8,128)} %get-tuple-element.24.own_ref, f32[528,256]{1,0:T(8,128)} %copy-done), custom_call_target="tpu_custom_call" | custom-call | tf_op jit(solution)/shard_map/core_join/pallas_call | solution.py:340
  27.7 2.8 %collective-permute-start.1 = (f32[264,256]{1,0:T(8,128)}, f32[264,256]{1,0:T(8,128)S(1)}, u32[]{:S(2)}, u32[]{:S(2)}) collective-permute-start(f32[264,256]{1,0:T(8,128)} %get-tuple-element.29), channel_id=1, source_target_pairs={{0,2},{1,3},{2,0},{3,1},{4,6},{5,7},{6,4},{7,5},{8,10},{9,11},{10,... | collective-permute-start | bytes 811016 | tf_op jit(solution)/shard_map/ppermute | solution.py:392
  30.5 1.5 %collective-permute-start.3 = (f32[264,256]{1,0:T(8,128)}, f32[264,256]{1,0:T(8,128)S(1)}, u32[]{:S(2)}, u32[]{:S(2)}) collective-permute-start(f32[264,256]{1,0:T(8,128)} %get-tuple-element.29), channel_id=1, source_target_pairs={{0,4},{1,5},{2,6},{3,7},{4,0},{5,1},{6,2},{7,3},{8,12},{9,13},{10,... | collective-permute-start | bytes 811016 | tf_op jit(solution)/shard_map/ppermute | solution.py:392
  32.1 0.0 collective-permute-start.5
  32.1 6.0 %collective-permute-done.1.r2 = f32[264,256]{1,0:T(8,128)S(1)} collective-permute-done((f32[264,256]{1,0:T(8,128)}, f32[264,256]{1,0:T(8,128)S(1)}, u32[]{:S(2)}, u32[]{:S(2)}) %collective-permute-start.1) | collective-permute-done | bytes 270368 | tf_op jit(solution)/shard_map/ppermute | solution.py:392
  38.0 0.0 collective-permute-start.2
  38.0 6.8 %collective-permute-done.3.r4 = f32[264,256]{1,0:T(8,128)S(1)} collective-permute-done((f32[264,256]{1,0:T(8,128)}, f32[264,256]{1,0:T(8,128)S(1)}, u32[]{:S(2)}, u32[]{:S(2)}) %collective-permute-start.3) | collective-permute-done | bytes 270368 | tf_op jit(solution)/shard_map/ppermute | solution.py:392
  44.8 0.0 copy-start.2
  44.8 0.0 collective-permute-start.4
  44.8 0.0 collective-permute-done.5.r6
  44.8 0.0 copy-start.3
  44.8 0.5 collective-permute-start.6
  45.3 15.2 %compose_steps.1 = (f32[32,256,256]{2,1,0:T(8,128)}, f32[32,256]{1,0:T(8,128)}, f32[32,256]{1,0:T(8,128)}) custom-call(f32[32,256,256]{2,1,0:T(8,128)} %bitcast.7, f32[32,256]{1,0:T(8,128)} %get-tuple-element.20.delta_ref, f32[32,256]{1,0:T(8,128)} %get-tuple-element.21.shift_ref, f32[32,256]{1,0:T(8,128)} %get-tuple-element.22.diag_ref, ...), custom_call_target="tpu_custom_call" | custom-call | tf_op jit(solution)/shard_map/compose_steps/pallas_call | solution.py:355
  60.5 0.0 collective-permute-done.2.x2
  60.5 0.0 copy-start.4
  60.5 0.0 collective-permute-done.4.x4
  60.5 0.0 copy-start.5
  60.6 0.0 collective-permute-done.6.x6
  60.6 0.0 copy-start.6
  60.6 0.0 copy-done.1
  60.6 0.0 copy-done.2
  60.6 0.0 copy-done.3
  60.6 0.6 copy-done.4
  61.2 0.1 copy-done.5
  61.4 0.1 copy-done.6
  61.4 4.4 %plane_join.1 = (f32[528,256]{1,0:T(8,128)}, f32[264,256]{1,0:T(8,128)}, f32[528,256]{1,0:T(8,128)}, f32[528,256]{1,0:T(8,128)}) custom-call(f32[528,256]{1,0:T(8,128)} %get-tuple-element.25.after_ref.own_ref, f32[264,256]{1,0:T(8,128)} %copy-done.1, f32[264,256]{1,0:T(8,128)} %copy-done.4, f32[264,256]{1,0:T(8,128)} %copy-done.2, f32[264,256]{1,0:T(8,128)} %copy-done.5, ...), custom_call_target="tpu_custom_call" | custom-call | tf_op jit(solution)/shard_map/plane_join/pallas_call | solution.py:340
  65.8 1.6 %collective-permute-start.7 = (f32[264,256]{1,0:T(8,128)}, f32[264,256]{1,0:T(8,128)S(1)}, u32[]{:S(2)}, u32[]{:S(2)}) collective-permute-start(f32[264,256]{1,0:T(8,128)} %get-tuple-element.33), channel_id=1, source_target_pairs={{0,8},{1,9},{2,10},{3,11},{4,12},{5,13},{6,14},{7,15},{8,0},{9,1},... | collective-permute-start | bytes 811016 | tf_op jit(solution)/shard_map/ppermute | solution.py:392
  67.4 7.1 %collective-permute-done.7.r_ref = f32[264,256]{1,0:T(8,128)S(1)} collective-permute-done((f32[264,256]{1,0:T(8,128)}, f32[264,256]{1,0:T(8,128)S(1)}, u32[]{:S(2)}, u32[]{:S(2)}) %collective-permute-start.7) | collective-permute-done | bytes 270368 | tf_op jit(solution)/shard_map/ppermute | solution.py:392
  74.5 0.0 copy-start.7
  74.5 0.0 collective-permute-start.8
  74.5 0.9 pad_convert_fusion.prefix_ref
  75.4 0.6 collective-permute-done.8.x_ref
  76.0 0.0 copy-done.7
  76.0 0.7 copy-done.8
  76.7 3.3 %level_join.1 = (f32[528,256]{1,0:T(8,128)}, f32[136,256]{1,0:T(8,128)}, f32[528,256]{1,0:T(8,128)}) custom-call(f32[528,256]{1,0:T(8,128)} %get-tuple-element.32.own_ref, f32[528,256]{1,0:T(8,128)} %pad_convert_fusion.prefix_ref, f32[264,256]{1,0:T(8,128)} %copy-done.7, f32[264,256]{1,0:T(8,128)} %copy-done.8), custom_call_target="tpu_custom_call" | custom-call | tf_op jit(solution)/shard_map/level_join/pallas_call | solution.py:340
  80.0 2.6 %collective-permute-start.9 = (f32[136,256]{1,0:T(8,128)}, f32[136,256]{1,0:T(8,128)S(1)}, u32[]{:S(2)}, u32[]{:S(2)}) collective-permute-start(f32[136,256]{1,0:T(8,128)} %get-tuple-element.35), channel_id=1, source_target_pairs={{0,16},{1,17},{2,18},{3,19},{4,20},{5,21},{6,22},{7,23},{8,24},{9,... | collective-permute-start | bytes 417800 | tf_op jit(solution)/shard_map/ppermute | solution.py:392
  82.6 7.2 %collective-permute-done.9.r_ref = f32[136,256]{1,0:T(8,128)S(1)} collective-permute-done((f32[136,256]{1,0:T(8,128)}, f32[136,256]{1,0:T(8,128)S(1)}, u32[]{:S(2)}, u32[]{:S(2)}) %collective-permute-start.9) | collective-permute-done | bytes 139296 | tf_op jit(solution)/shard_map/ppermute | solution.py:392
  89.8 0.0 collective-permute-start.10
  89.8 3.6 %place_join.1.place_ref = f32[528,256]{1,0:T(8,128)} custom-call(f32[528,256]{1,0:T(8,128)} %get-tuple-element.30.first_ref, f32[528,256]{1,0:T(8,128)} %get-tuple-element.31.other_ref, f32[528,256]{1,0:T(8,128)} %copy-done), custom_call_target="tpu_custom_call" | custom-call | tf_op jit(solution)/shard_map/place_join/pallas_call | solution.py:340
  93.4 0.0 collective-permute-done.10.x_ref
  93.4 0.0 copy-done.9
  93.4 0.6 copy-done.10
  94.1 9.4 %finish_steps.1 = (f32[32,256]{1,0:T(8,128)}, f32[32,256]{1,0:T(8,128)}) custom-call(f32[32,256,256]{2,1,0:T(8,128)} %get-tuple-element.26.psi_ref, f32[32,256]{1,0:T(8,128)} %get-tuple-element.27.token_ref.var_ref, f32[32,256]{1,0:T(8,128)} %get-tuple-element.28.mean_ref, f32[528,256]{1,0:T(8,128)} %place_join.1.place_ref, ...), custom_call_target="tpu_custom_call" | custom-call | tf_op jit(solution)/shard_map/finish_steps/pallas_call | solution.py:371
  (5 shorter events, 0.0 us)
Async XLA Ops:
  21.9 2.3 %collective-permute-start = (f32[528,256]{1,0:T(8,128)}, f32[528,256]{1,0:T(8,128)S(1)}, u32[]{:S(2)}, u32[]{:S(2)}) collective-permute-start(f32[528,256]{1,0:T(8,128)} %get-tuple-element.24.own_ref), channel_id=1, source_target_pairs={{0,1},{1,0},{2,3},{3,2},{4,5},{5,4},{6,7},{7,6},{8,9},{9,8},{10,11... | collective-permute-start | bytes 1622024 | tf_op jit(solution)/shard_map/ppermute | solution.py:392
  24.1 0.8 copy-start
  27.7 10.3 %collective-permute-start.1 = (f32[264,256]{1,0:T(8,128)}, f32[264,256]{1,0:T(8,128)S(1)}, u32[]{:S(2)}, u32[]{:S(2)}) collective-permute-start(f32[264,256]{1,0:T(8,128)} %get-tuple-element.29), channel_id=1, source_target_pairs={{0,2},{1,3},{2,0},{3,1},{4,6},{5,7},{6,4},{7,5},{8,10},{9,11},{10,... | collective-permute-start | bytes 811016 | tf_op jit(solution)/shard_map/ppermute | solution.py:392
  30.5 14.2 %collective-permute-start.3 = (f32[264,256]{1,0:T(8,128)}, f32[264,256]{1,0:T(8,128)S(1)}, u32[]{:S(2)}, u32[]{:S(2)}) collective-permute-start(f32[264,256]{1,0:T(8,128)} %get-tuple-element.29), channel_id=1, source_target_pairs={{0,4},{1,5},{2,6},{3,7},{4,0},{5,1},{6,2},{7,3},{8,12},{9,13},{10,... | collective-permute-start | bytes 811016 | tf_op jit(solution)/shard_map/ppermute | solution.py:392
  32.1 12.7 %collective-permute-start.5 = (f32[264,256]{1,0:T(8,128)}, f32[264,256]{1,0:T(8,128)S(1)}, u32[]{:S(2)}, u32[]{:S(2)}) collective-permute-start(f32[264,256]{1,0:T(8,128)} %get-tuple-element.29), channel_id=1, source_target_pairs={{0,6},{1,7},{2,4},{3,5},{4,2},{5,3},{6,0},{7,1},{8,14},{9,15},{10,... | collective-permute-start | bytes 811016 | tf_op jit(solution)/shard_map/ppermute | solution.py:392
  38.0 22.6 %copy-start.1 = (f32[264,256]{1,0:T(8,128)}, f32[264,256]{1,0:T(8,128)S(1)}, u32[]{:S(2)}) copy-start(f32[264,256]{1,0:T(8,128)S(1)} %collective-permute-done.1.r2) | copy-start | bytes 811012
  38.0 22.5 %collective-permute-start.2 = (f32[264,256]{1,0:T(8,128)S(1)}, f32[264,256]{1,0:T(8,128)S(1)}, u32[]{:S(2)}, u32[]{:S(2)}) collective-permute-start(f32[264,256]{1,0:T(8,128)S(1)} %collective-permute-done.1.r2), channel_id=1, source_target_pairs={{0,1},{1,0},{2,3},{3,2},{4,5},{5,4},{6,7},{7,6},{8,9},{9,8},{10,11... | collective-permute-start | bytes 811016 | tf_op jit(solution)/shard_map/ppermute | solution.py:392
  44.8 15.8 %copy-start.2 = (f32[264,256]{1,0:T(8,128)}, f32[264,256]{1,0:T(8,128)S(1)}, u32[]{:S(2)}) copy-start(f32[264,256]{1,0:T(8,128)S(1)} %collective-permute-done.3.r4) | copy-start | bytes 811012
  44.8 15.7 %collective-permute-start.4 = (f32[264,256]{1,0:T(8,128)S(1)}, f32[264,256]{1,0:T(8,128)S(1)}, u32[]{:S(2)}, u32[]{:S(2)}) collective-permute-start(f32[264,256]{1,0:T(8,128)S(1)} %collective-permute-done.3.r4), channel_id=1, source_target_pairs={{0,1},{1,0},{2,3},{3,2},{4,5},{5,4},{6,7},{7,6},{8,9},{9,8},{10,11... | collective-permute-start | bytes 811016 | tf_op jit(solution)/shard_map/ppermute | solution.py:392
  44.8 15.8 %copy-start.3 = (f32[264,256]{1,0:T(8,128)}, f32[264,256]{1,0:T(8,128)S(1)}, u32[]{:S(2)}) copy-start(f32[264,256]{1,0:T(8,128)S(1)} %collective-permute-done.5.r6) | copy-start | bytes 811012
  44.8 15.7 %collective-permute-start.6 = (f32[264,256]{1,0:T(8,128)S(1)}, f32[264,256]{1,0:T(8,128)S(1)}, u32[]{:S(2)}, u32[]{:S(2)}) collective-permute-start(f32[264,256]{1,0:T(8,128)S(1)} %collective-permute-done.5.r6), channel_id=1, source_target_pairs={{0,1},{1,0},{2,3},{3,2},{4,5},{5,4},{6,7},{7,6},{8,9},{9,8},{10,11... | collective-permute-start | bytes 811016 | tf_op jit(solution)/shard_map/ppermute | solution.py:392
  60.5 0.7 copy-start.4
  60.5 0.8 copy-start.5
  60.6 0.9 copy-start.6
  65.8 8.7 %collective-permute-start.7 = (f32[264,256]{1,0:T(8,128)}, f32[264,256]{1,0:T(8,128)S(1)}, u32[]{:S(2)}, u32[]{:S(2)}) collective-permute-start(f32[264,256]{1,0:T(8,128)} %get-tuple-element.33), channel_id=1, source_target_pairs={{0,8},{1,9},{2,10},{3,11},{4,12},{5,13},{6,14},{7,15},{8,0},{9,1},... | collective-permute-start | bytes 811016 | tf_op jit(solution)/shard_map/ppermute | solution.py:392
  74.5 1.6 %copy-start.7 = (f32[264,256]{1,0:T(8,128)}, f32[264,256]{1,0:T(8,128)S(1)}, u32[]{:S(2)}) copy-start(f32[264,256]{1,0:T(8,128)S(1)} %collective-permute-done.7.r_ref) | copy-start | bytes 811012
  74.5 1.5 %collective-permute-start.8 = (f32[264,256]{1,0:T(8,128)S(1)}, f32[264,256]{1,0:T(8,128)S(1)}, u32[]{:S(2)}, u32[]{:S(2)}) collective-permute-start(f32[264,256]{1,0:T(8,128)S(1)} %collective-permute-done.7.r_ref), channel_id=1, source_target_pairs={{0,1},{1,0},{2,3},{3,2},{4,5},{5,4},{6,7},{7,6},{8,9},{9,8},{10,11... | collective-permute-start | bytes 811016 | tf_op jit(solution)/shard_map/ppermute | solution.py:392
  76.0 0.7 copy-start.8
  80.0 9.8 %collective-permute-start.9 = (f32[136,256]{1,0:T(8,128)}, f32[136,256]{1,0:T(8,128)S(1)}, u32[]{:S(2)}, u32[]{:S(2)}) collective-permute-start(f32[136,256]{1,0:T(8,128)} %get-tuple-element.35), channel_id=1, source_target_pairs={{0,16},{1,17},{2,18},{3,19},{4,20},{5,21},{6,22},{7,23},{8,24},{9,... | collective-permute-start | bytes 417800 | tf_op jit(solution)/shard_map/ppermute | solution.py:392
  89.8 3.7 %copy-start.9 = (f32[136,256]{1,0:T(8,128)}, f32[136,256]{1,0:T(8,128)S(1)}, u32[]{:S(2)}) copy-start(f32[136,256]{1,0:T(8,128)S(1)} %collective-permute-done.9.r_ref) | copy-start | bytes 417796
  89.8 3.6 %collective-permute-start.10 = (f32[136,256]{1,0:T(8,128)S(1)}, f32[136,256]{1,0:T(8,128)S(1)}, u32[]{:S(2)}, u32[]{:S(2)}) collective-permute-start(f32[136,256]{1,0:T(8,128)S(1)} %collective-permute-done.9.r_ref), channel_id=1, source_target_pairs={{0,1},{1,0},{2,3},{3,2},{4,5},{5,4},{6,7},{7,6},{8,9},{9,8},{10,11... | collective-permute-start | bytes 417800 | tf_op jit(solution)/shard_map/ppermute | solution.py:392
  93.4 0.7 copy-start.10

commit v2 on v0

v2 whole, which is shorter than its diff:
```python
import functools

import jax
import jax.numpy as jnp
from jax import lax
from jax.experimental import pallas as pl
from jax.experimental.pallas import tpu as pltpu
from jax.sharding import PartitionSpec as P

f32, bf16 = jnp.float32, jnp.bfloat16
PLANE = 8


def nn(a, b):
    return jnp.dot(a, b, preferred_element_type=f32)


def nt(a, b):
    return lax.dot_general(a, b, (((1,), (1,)), ((), ())), preferred_element_type=f32)


def halves(x):
    high = x.astype(bf16)
    return high, (x - high.astype(f32)).astype(bf16)


def times(late, early):
    (lh, ll), (eh, el) = late, early
    return nn(lh, eh) + (nn(ll, eh) + nn(lh, el))


def advance(late, noise, shift):
    n = noise.shape[1]
    lh, ll = late
    xh, xl = halves(jnp.concatenate([times(late, halves(noise)), shift], axis=0))
    out = nt(xh, lh) + (nt(xl, lh) + nt(xh, ll))
    return out[:n], out[n:]


def joined(early, late):
    parts = halves(late[0])
    noise, shift = advance(parts, early[1], early[2])
    return times(parts, halves(early[0])), noise + late[1], shift + late[2]


def eye_mask(n):
    return lax.broadcasted_iota(jnp.int32, (n, n), 0) == lax.broadcasted_iota(jnp.int32, (n, n), 1)


def column(row):
    n = row.shape[1]
    out = []
    for k in range(0, n, 128):
        m = min(128, n - k)
        out.append(jnp.sum(jnp.where(eye_mask(m), row[:, k:k + m], 0.0), axis=1, keepdims=True))
    return out[0] if len(out) == 1 else jnp.concatenate(out, axis=0)


def row_of(col):
    n = col.shape[0]
    out = [jnp.sum(jnp.where(eye_mask(128), col[k:k + 128], 0.0), axis=0, keepdims=True) for k in range(0, n, 128)]
    return jnp.concatenate(out, axis=1)


def diag_row(x):
    n = x.shape[1]
    out = [jnp.sum(jnp.where(eye_mask(128), x[k:k + 128, k:k + 128], 0.0), axis=0, keepdims=True)
           for k in range(0, n, 128)]
    return jnp.concatenate(out, axis=1)


def rows16(row):
    return jnp.broadcast_to(row, (16, row.shape[1]))


def pack(noise, shift):
    n = noise.shape[1]
    h = n // 2
    lower = lax.broadcasted_iota(jnp.int32, (h, h), 0) >= lax.broadcasted_iota(jnp.int32, (h, h), 1)
    a, b, c = noise[:h, :h], noise[:h, h:], noise[h:, h:]
    body = jnp.concatenate([jnp.where(lower, a, c), b], axis=1)
    extra = jnp.concatenate([jnp.zeros((1, h), f32), diag_row(noise)[:, h:]], axis=1)
    return jnp.concatenate([body, shift[0:1], extra, jnp.zeros((6, n), f32)], axis=0)


def unpack(x):
    n = x.shape[1]
    h = n // 2
    i = lax.broadcasted_iota(jnp.int32, (h, h), 0)
    j = lax.broadcasted_iota(jnp.int32, (h, h), 1)
    body, b = x[:h, :h], x[:h, h:]
    turned = body.T
    a = jnp.where(i >= j, body, turned)
    c = jnp.where(i == j, x[h + 1:h + 2, h:], jnp.where(i < j, body, turned))
    noise = jnp.concatenate([jnp.concatenate([a, b], axis=1), jnp.concatenate([b.T, c], axis=1)], axis=0)
    return noise, rows16(x[h:h + 1])


def rank_of(axes):
    rank = 0
    for name, size in axes:
        rank = rank * size + lax.axis_index(name)
    return rank


def bit_of(rank, bit):
    return (rank // bit) % 2


def whole(upper, mine_ref, others_ref):
    mine, others = mine_ref[...], others_ref[...]
    return jnp.concatenate([jnp.where(upper, others, mine), jnp.where(upper, mine, others)], axis=0)


def identity(n):
    return jnp.where(eye_mask(n), 1.0, 0.0), jnp.zeros((n, n), f32), jnp.zeros((16, n), f32)


def maps_kernel(subs, axes, mean_hbm, decay_hbm, coup_hbm, omap_hbm, gain_hbm, seen_hbm,
                g_ref, e_ref, dcol_ref, delta_ref, shift_ref, maps_ref, total_ref,
                mean_ref, decay_ref, coup_ref, omap_ref, gain_ref, seen_ref, small_sem, sem):
    n = decay_ref.shape[1]
    steps = coup_ref.shape[1]
    small = [pltpu.make_async_copy(x, y, small_sem.at[k]) for k, (x, y) in enumerate(
        [(mean_hbm, mean_ref), (decay_hbm, decay_ref), (seen_hbm, seen_ref)])]

    def chunk(j):
        return [pltpu.make_async_copy(x.at[:, j], y.at[:, j], sem.at[k, j]) for k, (x, y) in enumerate(
            [(coup_hbm, coup_ref), (omap_hbm, omap_ref), (gain_hbm, gain_ref)])]

    for c in small + chunk(0):
        c.start()
    for j in range(1, steps):
        for c in chunk(j):
            c.start()
    for c in small:
        c.wait()
    begins = rank_of(axes) == 0

    def step(j, first):
        for c in chunk(j):
            c.wait()
        for s in range(subs):
            t = s * steps + j
            d_row = decay_ref[pl.ds(t, 1), :]
            d_col = jnp.broadcast_to(column(d_row), (n, 128))
            dcol_ref[s, j] = d_col
            coup = coup_ref[s, j]
            gain = gain_ref[s, j]
            omap = omap_ref[s, j]
            obs_f = (omap.astype(f32) * d_row + nn(omap, coup)).astype(bf16)
            e = coup.astype(f32) - nn(gain.T, obs_f)
            e_h = e.astype(bf16)
            e_ref[s, j] = e_h
            shift = jnp.sum(gain.astype(f32) * column(seen_ref[pl.ds(t, 1), :]), axis=0, keepdims=True)
            if first and s > 0:
                g_ref[s, j] = e
                delta = d_row
                b_new = shift
            else:
                if first:
                    delta = jnp.where(begins, 0.0, jnp.ones((1, n), f32))
                    b = jnp.where(begins, mean_ref[...], 0.0)
                    g_ref[s, j] = e * delta
                else:
                    delta = delta_ref[pl.ds(t - 1, 1), :]
                    b = shift_ref[pl.ds(t - 1, 1), :]
                    g = g_ref[s, j - 1]
                    both = jnp.concatenate([d_col, d_col], axis=1)
                    g_ref[s, j] = both * g + e * delta + nn(e_h, g.astype(bf16))
                b_new = d_row * b + row_of(jnp.sum(e * b, axis=1, keepdims=True)) + shift
                delta = delta * d_row
            delta_ref[pl.ds(t, 1), :] = delta
            shift_ref[pl.ds(t, 1), :] = b_new

    step(0, True)
    lax.fori_loop(1, steps, lambda j, c: (step(j, False), c)[1], 0)

    eye = eye_mask(n)
    maps = [g_ref[s, steps - 1] + jnp.where(eye, delta_ref[(s + 1) * steps - 1:(s + 1) * steps, :], 0.0)
            for s in range(subs)]
    for s in range(subs):
        maps_ref[s] = maps[s]
    parts = [halves(m) for m in maps]
    low, high = times(parts[1], parts[0]), times(parts[3], parts[2])
    maps_ref[subs] = low
    maps_ref[subs + 1] = high
    total_ref[...] = times(halves(high), halves(low))


def noises_kernel(subs, axes, init_ref, decay_ref, e_ref, dcol_ref, omap_ref, gain_ref, nf_ref, var_ref, shift_ref,
                  maps_ref, diag_ref, noises_ref, total_ref, q_s):
    n = nf_ref.shape[0]
    m = omap_ref.shape[2]
    steps = e_ref.shape[1]
    nf = nf_ref[...]
    var_col = column(var_ref[...])

    def moved(s, j, q, noise):
        d_row = decay_ref[pl.ds(s * steps + j, 1), :]
        d_col = jnp.concatenate([dcol_ref[s, j], dcol_ref[s, j]], axis=1)
        x = d_col * q + nn(e_ref[s, j], q.astype(bf16))
        return x * d_row + nt(x.astype(bf16), e_ref[s, j]) + noise

    def step(j, first):
        obs_g = nn(jnp.concatenate([omap_ref[s, j] for s in range(subs)], axis=0), nf).astype(bf16)
        for s in range(subs):
            gain = gain_ref[s, j]
            weighted = (gain.astype(f32) * var_col).astype(bf16)
            gain_t = gain.T
            shaped = (nf.astype(f32) - nn(gain_t, obs_g[s * m:(s + 1) * m])).astype(bf16)
            q_new = nt(shaped, shaped) + nn(gain_t, weighted)
            if not first:
                q_new = moved(s, j, q_s[s], q_new)
            q_s[s] = q_new
            if first and s == 0:
                @pl.when(rank_of(axes) == 0)
                def _():
                    q_s[0] = moved(0, 0, jnp.where(eye_mask(n), init_ref[...], 0.0), q_s[0])
            diag_ref[pl.ds(s * steps + j, 1), :] = diag_row(q_s[s] if first else q_new)

    step(0, True)
    lax.fori_loop(1, steps, lambda j, c: (step(j, False), c)[1], 0)

    shift = [rows16(shift_ref[(s + 1) * steps - 1:(s + 1) * steps, :]) for s in range(subs)]
    pairs = []
    for s in (0, 2):
        noise, along = advance(halves(maps_ref[s + 1]), q_s[s], shift[s])
        pairs.append((noise + q_s[s + 1], along + shift[s + 1]))
    for s in range(subs):
        noises_ref[s, 0:n, :] = q_s[s]
        noises_ref[s, n:, :] = shift[s]
    noises_ref[subs, 0:n, :] = pairs[0][0]
    noises_ref[subs, n:, :] = pairs[0][1]
    noise, along = advance(halves(maps_ref[subs + 1]), *pairs[0])
    total_ref[...] = pack(noise + pairs[1][0], along + pairs[1][1])


def core_kernel(axes, own_map_ref, other_map_ref, own_ref, other_ref, out_ref):
    upper = rank_of(axes) % 2 == 1
    own, other = unpack(own_ref[...]), unpack(other_ref[...])
    late = halves(jnp.where(upper, own_map_ref[...], other_map_ref[...]))
    noise, shift = advance(late, *(jnp.where(upper, a, b) for a, b in zip(other, own)))
    out_ref[...] = pack(noise + jnp.where(upper, own[0], other[0]), shift + jnp.where(upper, own[1], other[1]))


def fetch(rank, refs, dst, sem):
    place = (rank % PLANE) // (PLANE // len(refs))
    copies = [pltpu.make_async_copy(r, dst.at[place ^ k], sem.at[k]) for k, r in enumerate(refs)]
    for c in copies:
        c.start()
    for c in copies:
        c.wait()


def plane_maps_kernel(axes, *refs):
    ins, (_, _, late_ref, total_ref, half_ref, picks_ref, map_s, chip_s, sem) = refs[:PLANE], refs[PLANE:]
    rank = rank_of(axes)
    fetch(rank, ins, map_s, sem)
    place = rank % PLANE
    y = bit_of(rank, 4)
    chips = []
    for k in range(4):
        late = halves(map_s[2 * k + 1])
        late_ref[k, 0], late_ref[k, 1] = late
        chips.append(times(late, halves(map_s[2 * k])))
        chip_s[k] = chips[k]
    pairs = []
    for k in range(2):
        late = halves(chips[2 * k + 1])
        late_ref[4 + k, 0], late_ref[4 + k, 1] = late
        pairs.append(times(late, halves(chips[2 * k])))
    late = halves(pairs[1])
    late_ref[6, 0], late_ref[6, 1] = late
    total_ref[...] = times(late, halves(pairs[0]))
    h = half_ref.shape[0]
    half_ref[...] = jnp.where(rank % 2 == 1, total_ref[h:], total_ref[:h])
    picks_ref[0] = pairs[0]
    picks_ref[1] = chip_s[2 * y]
    picks_ref[2] = map_s[place - place % 2]


def plane_noises_kernel(axes, *refs):
    ins, (late_ref, core_ref, total_ref, picks_ref, in_s, sem) = refs[:4], refs[4:]
    rank = rank_of(axes)
    fetch(rank, ins, in_s, sem)
    n = late_ref.shape[-1]

    def join(k, early, late):
        noise, shift = advance((late_ref[k, 0], late_ref[k, 1]), *early)
        return noise + late[0], shift + late[1]

    chips = [unpack(in_s[k]) for k in range(4)]
    pairs = [join(4 + k, chips[2 * k], chips[2 * k + 1]) for k in range(2)]
    total_ref[...] = pack(*join(6, pairs[0], pairs[1]))
    picks_ref[0, 0:n], picks_ref[0, n:] = pairs[0]
    picks_ref[1, 0:n], picks_ref[1, n:] = unpack(in_s[2 * bit_of(rank, 4)])
    picks_ref[2, 0:n], picks_ref[2, n:] = unpack(core_ref[...])


def level_kernel(axes, bit, own_map_ref, own_ref, r_ref, x_ref, other_ref, *outs):
    rank = rank_of(axes)
    upper, high = rank % 2 == 1, bit_of(rank, bit) == 1
    other_map, own_map = whole(upper, r_ref, x_ref), own_map_ref[...]
    other, own = unpack(other_ref[...]), unpack(own_ref[...])
    late = halves(jnp.where(high, own_map, other_map))
    noise, shift = advance(late, *(jnp.where(high, a, b) for a, b in zip(other, own)))
    outs[0][...] = pack(noise + jnp.where(high, own[0], other[0]), shift + jnp.where(high, own[1], other[1]))
    if len(outs) > 1:
        outs[1][...] = times(late, halves(jnp.where(high, other_map, own_map)))
        h = outs[2].shape[0]
        outs[2][...] = jnp.where(upper, outs[1][h:], outs[1][:h])


def place_kernel(axes, bits, maps_ref, noises_ref, *refs):
    out_ref = refs[-1]
    rank = rank_of(axes)
    upper = rank % 2 == 1
    n = out_ref.shape[1]
    before = identity(n)
    for k, bit in enumerate(bits):
        r_ref, x_ref, other_ref = refs[3 * k:3 * k + 3]
        other = (whole(upper, r_ref, x_ref), *unpack(other_ref[...]))
        new = other if k == 0 else joined(other, before)
        before = tuple(jnp.where(bit_of(rank, bit) == 1, a, b) for a, b in zip(new, before))
    one = identity(n)
    parts = []
    for k, bit in enumerate((4, 2, 1)):
        element = (maps_ref[k], noises_ref[k, 0:n], noises_ref[k, n:])
        parts.append(tuple(jnp.where(bit_of(rank, bit) == 1, a, b) for a, b in zip(element, one)))
    em, en, es = joined(joined(before, parts[0]), joined(parts[1], parts[2]))
    out_ref[0:n, :], out_ref[n:2 * n, :], out_ref[2 * n:, :] = em, en, es


def compose_kernel(sub, g_ref, delta_ref, shift_ref, diag_ref, maps_ref, noises_ref, token_ref,
                   out_ref, var_ref, mean_ref, stack_s, col_s):
    steps, n = out_ref.shape[:2]
    eye = eye_mask(n)

    def element(k):
        return maps_ref[k], noises_ref[k, 0:n, :], noises_ref[k, n:, :]

    if sub:
        em, en, es = element(0) if sub == 1 else element(4) if sub == 2 else joined(element(4), element(2))
        turned = em.T
        stack_s[0:n, :] = turned
        stack_s[n:2 * n, :] = en
        col_s[0] = jnp.broadcast_to(column(es[0:1, :]), (n, 128))
        col_s[1] = jnp.broadcast_to(column(diag_row(turned)), (n, 128))

    def step(j, carry):
        t = sub * steps + j
        turned = g_ref[sub, j].T
        delta = delta_ref[pl.ds(t, 1), :]
        phi = turned + jnp.where(eye, delta, 0.0)
        if sub:
            mask = jnp.concatenate([eye, jnp.zeros((n, n), jnp.bool_)], axis=0)
            stack = stack_s[...]
            both = stack * delta + nn(jnp.where(mask, 0.0, stack).astype(bf16), turned.astype(bf16))
            out_ref[j] = both[:n] + jnp.concatenate([col_s[1], col_s[1]], axis=1) * turned
            var_ref[pl.ds(j, 1), :] = diag_ref[pl.ds(t, 1), :] + jnp.sum(phi * both[n:], axis=0, keepdims=True)
            mean_ref[pl.ds(j, 1), :] = shift_ref[pl.ds(t, 1), :] + jnp.sum(
                phi * jnp.concatenate([col_s[0], col_s[0]], axis=1), axis=0, keepdims=True)
        else:
            out_ref[j] = phi
            var_ref[pl.ds(j, 1), :] = diag_ref[pl.ds(t, 1), :]
            mean_ref[pl.ds(j, 1), :] = shift_ref[pl.ds(t, 1), :]
        return carry

    lax.fori_loop(0, steps, step, 0, unroll=2)


def finish_kernel(axes, bit, parts, *refs):
    psi = refs[:parts]
    var = refs[parts:2 * parts]
    mean = refs[2 * parts:3 * parts]
    place_ref, r_ref, means_ref, vars_ref, p_s, col_s = refs[3 * parts:]
    n = p_s.shape[1]
    high = bit_of(rank_of(axes), bit) == 1
    noise, shift = advance(halves(place_ref[0:n, :]), *unpack(r_ref[...]))
    p_s[...] = jnp.where(high, noise, 0.0) + place_ref[n:2 * n, :]
    shift = jnp.where(high, shift, 0.0) + place_ref[2 * n:, :]
    col_s[...] = jnp.broadcast_to(column(shift[0:1, :]), (n, 128))
    eye = eye_mask(n)
    steps = psi[0].shape[0]

    def step(j, carry):
        p = p_s[...]
        ph = p.astype(bf16)
        col = jnp.concatenate([col_s[...], col_s[...]], axis=1)
        for a in range(parts):
            to = a * steps + j
            x = psi[a][j]
            w = nn(ph, jnp.where(eye, 0.0, x).astype(bf16)) + p * diag_row(x)
            vars_ref[pl.ds(to, 1), :] = var[a][pl.ds(j, 1), :] + jnp.sum(x * w, axis=0, keepdims=True)
            means_ref[pl.ds(to, 1), :] = mean[a][pl.ds(j, 1), :] + jnp.sum(x * col, axis=0, keepdims=True)
        return carry

    lax.fori_loop(0, steps, step, 0)


def vmem():
    return pl.BlockSpec(memory_space=pltpu.VMEM)


def anywhere():
    return pl.BlockSpec(memory_space=pl.ANY)


def shape(*dims, dtype=f32):
    return jax.ShapeDtypeStruct(dims, dtype)


def call(kernel, name, outs, args, specs=None, scratch=(), limit=16, flops=10 ** 9):
    return pl.pallas_call(
        kernel,
        in_specs=specs or [vmem()] * len(args),
        out_specs=[vmem()] * len(outs),
        out_shape=outs,
        scratch_shapes=scratch,
        compiler_params=pltpu.CompilerParams(vmem_limit_bytes=limit * 1024 * 1024),
        cost_estimate=pl.CostEstimate(flops=flops, bytes_accessed=0, transcendentals=0),
        name=name,
    )(*args)


def hbm():
    return pl.BlockSpec(memory_space=pltpu.HBM)


def step_maps(axes, subs, init_mean, decay, coupling, obs_map, gain, observed):
    T, n = decay.shape
    m = obs_map.shape[1]
    steps = T // subs
    outs = [shape(subs, steps, n, n), shape(subs, steps, n, n, dtype=bf16), shape(subs, steps, n, 128),
            shape(T, n), shape(T, n), shape(subs + 2, n, n), shape(n, n)]
    args = [init_mean.reshape(1, n), decay, coupling.reshape(subs, steps, n, n), obs_map.reshape(subs, steps, m, n),
            gain.reshape(subs, steps, m, n), observed]
    scratch = [pltpu.VMEM(x.shape, x.dtype) for x in args]
    args = [pltpu.with_memory_space_constraint(x, pltpu.HBM) for x in args]
    scratch += [pltpu.SemaphoreType.DMA((3,)), pltpu.SemaphoreType.DMA((3, steps))]
    return call(functools.partial(maps_kernel, subs, axes), "step_maps", outs, args, [hbm()] * len(args), scratch,
                limit=20, flops=10 ** 10)


def step_noises(axes, subs, init_var, decay, e, dcol, obs_map, gain, noise_factor, obs_var, shift, maps):
    T, n = decay.shape
    m = obs_map.shape[1]
    steps = T // subs
    args = [init_var.reshape(1, n), decay, e, dcol, obs_map.reshape(subs, steps, m, n),
            gain.reshape(subs, steps, m, n), noise_factor, obs_var.reshape(1, m), shift, maps]
    return call(functools.partial(noises_kernel, subs, axes), "step_noises",
                [shape(T, n), shape(subs + 1, n + 16, n), shape(n // 2 + 8, n)], args,
                scratch=[pltpu.VMEM((subs, n, n), f32)])


def compose(sub, g, delta, shift, diag, maps, noises, token):
    _, steps, n, _ = g.shape
    return call(functools.partial(compose_kernel, sub), "compose",
                [shape(steps, n, n), shape(steps, n), shape(steps, n)],
                [g, delta, shift, diag, maps, noises, token], [vmem()] * 6 + [anywhere()],
                [pltpu.VMEM((2 * n, n), f32), pltpu.VMEM((2, n, 128), f32)], flops=4 * 10 ** 9)


def finish(axes, bit, composed, place, r):
    parts = len(composed)
    T, n, _ = composed[0][0].shape
    psi, var, mean = zip(*composed)
    return call(functools.partial(finish_kernel, axes, bit, parts), "finish", [shape(parts * T, n)] * 2,
                [*psi, *var, *mean, place, r], scratch=[pltpu.VMEM((n, n), f32), pltpu.VMEM((n, 128), f32)])


def per_device(axes, init_mean, init_var, decay, coupling, obs_map, gain, noise_factor, obs_var, observed):
    n = decay.shape[1]
    h = n // 2
    subs = 4
    count = 1
    for _, size in axes:
        count *= size
    names = tuple(name for name, _ in axes)

    def swap(x, bit):
        return lax.ppermute(x, names, [(k, k ^ bit) for k in range(count)])

    bits = []
    bit = PLANE
    while bit < count:
        bits.append(bit)
        bit *= 2

    g, e, dcol, delta, shift, maps, own = step_maps(axes, subs, init_mean, decay, coupling, obs_map, gain, observed)
    far = [swap(own, bit) for bit in (2, 4, 6)]
    other = swap(own, 1)
    diag, noises, packed = step_noises(
        axes, subs, init_var, decay, e, dcol, obs_map, gain, noise_factor, obs_var, shift, maps)
    other_packed = swap(packed, 1)
    (chip,) = call(functools.partial(core_kernel, axes), "core_noises", [shape(h + 8, n)],
                   [own, other, packed, other_packed])
    chips = [chip] + [swap(chip, bit) for bit in (2, 4, 6)]
    *far, token = lax.optimization_barrier((*far, chip))
    all_maps = [own, other] + [v for r in far for v in (r, swap(r, 1))]
    composed = [compose(k, g, delta, shift, diag, maps, noises, token) for k in (0, 1)]
    late, total, half, map_picks = call(
        functools.partial(plane_maps_kernel, axes), "plane_maps",
        [shape(PLANE - 1, 2, n, n, dtype=bf16), shape(n, n), shape(h, n), shape(3, n, n)],
        [*all_maps, composed[0][1], composed[1][1]], [anywhere()] * (PLANE + 2),
        [pltpu.VMEM((PLANE, n, n), f32), pltpu.VMEM((4, n, n), f32), pltpu.SemaphoreType.DMA((PLANE,))])
    packed, noise_picks = call(
        functools.partial(plane_noises_kernel, axes), "plane_noises",
        [shape(h + 8, n), shape(3, n + 16, n)],
        [*chips, late, other_packed], [anywhere()] * 4 + [vmem()] * 2,
        [pltpu.VMEM((4, h + 8, n), f32), pltpu.SemaphoreType.DMA((4,))])
    received = []
    for k, bit in enumerate(bits[:-1]):
        r = swap(half, bit)
        got = (r, swap(r, 1), swap(packed, bit))
        received += got
        more = k < len(bits) - 2
        new = call(functools.partial(level_kernel, axes, bit), "level",
                   [shape(h + 8, n)] + ([shape(n, n), shape(h, n)] if more else []), [total, packed, *got])
        if k == 0:
            composed.append(compose(2, g, delta, shift, diag, maps, noises, packed))
        packed = new[0]
        if more:
            total, half = new[1:]
    (place,) = call(functools.partial(place_kernel, axes, bits[:-1]), "place", [shape(2 * n + 16, n)],
                    [map_picks, noise_picks, *received], flops=10 ** 6)
    r = swap(packed, bits[-1])
    composed.append(compose(3, g, delta, shift, diag, maps, noises, packed))
    return tuple(finish(axes, bits[-1], composed, place, r))


def solution(mesh):
    axes = tuple((name, mesh.shape[name]) for name in mesh.axis_names)
    time = P(tuple(mesh.axis_names))
    return jax.shard_map(
        functools.partial(per_device, axes),
        mesh=mesh,
        in_specs=(P(), P(), time, time, time, time, P(), P(), time),
        out_specs=(time, time),
        check_vma=False,
    )
```

time: 561 us -> 65.9 us (0.12)
  matrix products: 353 us -> 0 us
  waiting for transfers between devices: 108 us -> 6.25 us
  Pallas kernels: 0 us -> 44.9 us
  local copies, waits for them, and re-layouts: 43.6 us -> 0.03 us
  blocking collectives: 32.7 us -> 0 us
  starting transfers between devices: 0.2 us -> 13.7 us
  between operations: 14.1 us -> 0.82 us
    dot_general x193 -> x0, matrix products: 353 us -> none  [the longest x46 89.8 us: combine(): joined_map = jnp.matmul(later_map, earlier_map, precision=highest)]
    all_gather x4 -> x0, waiting for transfers between devices: 73.6 us -> none  [entering(): everything = jax.tree.map(lambda part: lax.all_gather(part, axis), shard)]
    pallas_call x0 -> x12, Pallas kernels: none -> 44.9 us  [call(): pl.pallas_call(kernel, in_specs=specs or [vmem()] * len(args), out_specs=...]
    psum x1 -> x0, waiting for transfers between devices: 33.3 us -> none  [broadcast(): return lax.psum(block, axis)]
    while x46 -> x0, local copies, waits for them, and re-layouts: 29.5 us -> none  [the longest x2 28.7 us: per_device(): total, prefixes = lax.scan(accumulate, neutral, (step_map, shift, noise))]
    all_gather x2 -> x0, blocking collectives: 26.7 us -> none  [entering(): everything = jax.tree.map(lambda part: lax.all_gather(part, axis), shard)]
    ppermute x0 -> x15, starting transfers between devices: none -> 13.7 us  [swap(): return lax.ppermute(x, names, [(k, k ^ bit) for k in range(count)])]
    unnamed x34 -> x12, local copies, waits for them, and re-layouts: 8.15 us -> 0.03 us
  transfers between devices with their start and end apart: 5 -> 15, of which waited for: 4 -> 5; matrix products, arithmetic and copies ran while one was open for 6% -> 0% of each run, Pallas kernels for 0% -> 41%
where the time goes in v2:
time: 65.9 us; the launch traced here: 65.7 us
  Pallas kernels  44.9 us (68%)
  starting transfers between devices  13.7 us (21%)
  waiting for transfers between devices  6.25 us (9%)
  between operations  0.82 us (1%)
    pallas_call x12, Pallas kernels, call(): pl.pallas_call(kernel, in_specs=specs or [vmem()] * len(args), out_specs=...  44.9 us
    ppermute x15, starting transfers between devices, swap(): return lax.ppermute(x, names, [(k, k ^ bit) for k in range(count)])  13.7 us
    ppermute x15, waiting for transfers between devices, swap(): return lax.ppermute(x, names, [(k, k ^ bit) for k in range(count)])  6.25 us
  transfers between devices with their start and end apart: 15, of which 5 were waited for; matrix products, arithmetic and copies ran while one was open for 0% of the time, Pallas kernels for 41%

profile of v2, /device:TPU:0, one launch (start us, length us, event | category | flops | bytes accessed | tf_op | source)
XLA Modules:
  0.0 65.7 jit_solution(3329781189416540026)
XLA Ops:
  0.6 0.0 copy-start
  0.6 0.0 copy-start.1
  0.7 0.0 copy-start.2
  0.7 12.7 %step_maps.1 = (f32[4,8,256,256]{3,2,1,0:T(8,128)S(1)}, bf16[4,8,256,256]{3,2,1,0:T(8,128)(2,1)S(1)}, f32[4,8,256,128]{3,2,1,0:T(8,128)S(1)}, f32[32,256]{1,0:T(...) custom-call(f32[1,256]{1,0:T(1,128)} %bitcast.13, f32[32,256]{1,0:T(8,128)} %decay_ref.1, ...), custom_call_target="tpu_custom_call" | custom-call | flops 10000000000 | tf_op jit(solution)/shard_map/step_maps/pallas_call | solution.py:415
  13.4 0.5 collective-permute-start.3
  13.9 2.6 %collective-permute-start = (f32[256,256]{1,0:T(8,128)S(1)}, f32[256,256]{1,0:T(8,128)S(1)}, u32[]{:S(2)}, u32[]{:S(2)}) collective-permute-start(f32[256,256]{1,0:T(8,128)S(1)} %get-tuple-element.42.own_map_ref.refs_0_), channel_id=1, source_target_pairs={{0,2},{1,3},{2,0},{3,1},{4,6},{5,7},{6,4},{7,5},{8,10},{9,11},{10,... | collective-permute-start | bytes 786440 | tf_op jit(solution)/shard_map/ppermute | solution.py:483
  16.5 1.5 %collective-permute-start.1 = (f32[256,256]{1,0:T(8,128)S(1)}, f32[256,256]{1,0:T(8,128)S(1)}, u32[]{:S(2)}, u32[]{:S(2)}) collective-permute-start(f32[256,256]{1,0:T(8,128)S(1)} %get-tuple-element.42.own_map_ref.refs_0_), channel_id=1, source_target_pairs={{0,4},{1,5},{2,6},{3,7},{4,0},{5,1},{6,2},{7,3},{8,12},{9,13},{10,... | collective-permute-start | bytes 786440 | tf_op jit(solution)/shard_map/ppermute | solution.py:483
  18.0 0.0 collective-permute-start.2
  18.0 0.0 copy-done
  18.0 0.0 copy-done.4
  18.1 0.0 copy-done.5
  18.1 12.2 %step_noises.1 = (f32[32,256]{1,0:T(8,128)S(1)}, f32[5,272,256]{2,1,0:T(8,128)S(1)}, f32[136,256]{1,0:T(8,128)S(1)}) custom-call(f32[1,256]{1,0:T(1,128)S(1)} %bitcast.10, f32[32,256]{1,0:T(8,128)S(1)} %copy-done.3, bf16[4,8,256,256]{3,2,1,0:T(8,128)(2,1)S(1)} %get-tuple-element.37.e_ref, f32[4,8,256,128]{3,2,1,0:T(8,128)S(1)} %get-tuple-element.38.dcol_ref, ...), custom_call_target="tpu_custom_call" | custom-call | flops 1000000000 | tf_op jit(solution)/shard_map/step_noises/pallas_call | solution.py:415
  30.3 0.1 collective-permute-start.4
  30.4 1.3 %collective-permute-done.4.other_ref.refs_5_ = f32[136,256]{1,0:T(8,128)S(1)} collective-permute-done((f32[136,256]{1,0:T(8,128)S(1)}, f32[136,256]{1,0:T(8,128)S(1)}, u32[]{:S(2)}, u32[]{:S(2)}) %collective-permute-start.4) | collective-permute-done | bytes 139296 | tf_op jit(solution)/shard_map/ppermute | solution.py:483
  31.7 0.0 collective-permute-done.3.other_map_ref.refs_1_
  31.7 0.7 %core_noises.1.token_ref.refs_0_ = f32[136,256]{1,0:T(8,128)S(1)} custom-call(f32[256,256]{1,0:T(8,128)S(1)} %get-tuple-element.42.own_map_ref.refs_0_, f32[256,256]{1,0:T(8,128)S(1)} %collective-permute-done.3.other_map_ref.refs_1_, f32[136,256]{1,0:T(8,128)S(1)} %get-tuple-element.43.own_ref, f32[136,256]{1,0:T(8,128)S(1)} %collective-permute-done.4.other_ref.refs_5_), custom_call_target="tpu_custom_call" | custom-call | flops 1000000000 | tf_op jit(solution)/shard_map/core_noises/pallas_call | solution.py:415
  32.5 1.7 %collective-permute-start.5 = (f32[136,256]{1,0:T(8,128)S(1)}, f32[136,256]{1,0:T(8,128)S(1)}, u32[]{:S(2)}, u32[]{:S(2)}) collective-permute-start(f32[136,256]{1,0:T(8,128)S(1)} %core_noises.1.token_ref.refs_0_), channel_id=1, source_target_pairs={{0,2},{1,3},{2,0},{3,1},{4,6},{5,7},{6,4},{7,5},{8,10},{9,11},{10,... | collective-permute-start | bytes 417800 | tf_op jit(solution)/shard_map/ppermute | solution.py:483
  34.1 1.5 %collective-permute-start.6 = (f32[136,256]{1,0:T(8,128)S(1)}, f32[136,256]{1,0:T(8,128)S(1)}, u32[]{:S(2)}, u32[]{:S(2)}) collective-permute-start(f32[136,256]{1,0:T(8,128)S(1)} %core_noises.1.token_ref.refs_0_), channel_id=1, source_target_pairs={{0,4},{1,5},{2,6},{3,7},{4,0},{5,1},{6,2},{7,3},{8,12},{9,13},{10,... | collective-permute-start | bytes 417800 | tf_op jit(solution)/shard_map/ppermute | solution.py:483
  35.7 0.0 collective-permute-done.refs_2_
  35.7 0.4 collective-permute-start.7
  36.0 0.0 collective-permute-done.1.refs_4_
  36.0 0.0 collective-permute-done.2.refs_6_
  36.0 0.0 collective-permute-start.10
  36.0 0.5 collective-permute-start.8
  36.6 2.3 %compose.5 = (f32[8,256,256]{2,1,0:T(8,128)S(1)}, f32[8,256]{1,0:T(8,128)S(1)}, f32[8,256]{1,0:T(8,128)S(1)}) custom-call(f32[4,8,256,256]{3,2,1,0:T(8,128)S(1)} %get-tuple-element.34.g_ref, f32[32,256]{1,0:T(8,128)S(1)} %get-tuple-element.35.delta_ref, f32[32,256]{1,0:T(8,128)S(1)} %get-tuple-element.36.shift_ref, ...), custom_call_target="tpu_custom_call" | custom-call | flops 4000000000 | tf_op jit(solution)/shard_map/compose/pallas_call | solution.py:415
  38.8 0.0 collective-permute-done.10.refs_7_
  38.8 0.1 collective-permute-start.9
  39.0 0.8 %compose.4 = (f32[8,256,256]{2,1,0:T(8,128)S(1)}, f32[8,256]{1,0:T(8,128)S(1)}, f32[8,256]{1,0:T(8,128)S(1)}) custom-call(f32[4,8,256,256]{3,2,1,0:T(8,128)S(1)} %get-tuple-element.34.g_ref, f32[32,256]{1,0:T(8,128)S(1)} %get-tuple-element.35.delta_ref, f32[32,256]{1,0:T(8,128)S(1)} %get-tuple-element.36.shift_ref, ...), custom_call_target="tpu_custom_call" | custom-call | flops 4000000000 | tf_op jit(solution)/shard_map/compose/pallas_call | solution.py:415
  39.8 0.0 collective-permute-done.8.refs_3_
  39.8 0.6 collective-permute-done.9.refs_5_
  40.4 1.7 %plane_maps.1 = (bf16[7,2,256,256]{3,2,1,0:T(8,128)(2,1)S(1)}, f32[256,256]{1,0:T(8,128)S(1)}, f32[128,256]{1,0:T(8,128)S(1)}, f32[3,256,256]{2,1,0:T(8,128)S(1)}) custom-call(f32[256,256]{1,0:T(8,128)S(1)} %get-tuple-element.42.own_map_ref.refs_0_, f32[256,256]{1,0:T(8,128)S(1)} %collective-permute-done.3.other_map_ref.refs_1_, ...), custom_call_target="tpu_custom_call" | custom-call | flops 1000000000 | tf_op jit(solution)/shard_map/plane_maps/pallas_call | solution.py:415
  42.1 1.8 %collective-permute-start.11 = (f32[128,256]{1,0:T(8,128)S(1)}, f32[128,256]{1,0:T(8,128)S(1)}, u32[]{:S(2)}, u32[]{:S(2)}) collective-permute-start(f32[128,256]{1,0:T(8,128)S(1)} %get-tuple-element.56), channel_id=1, source_target_pairs={{0,8},{1,9},{2,10},{3,11},{4,12},{5,13},{6,14},{7,15},{8,0},{9,1},... | collective-permute-start | bytes 393224 | tf_op jit(solution)/shard_map/ppermute | solution.py:483
  43.8 0.0 collective-permute-done.5.refs_1_
  43.9 0.0 collective-permute-done.6.refs_2_
  43.9 0.0 collective-permute-done.7.refs_3_
  43.9 2.1 %plane_noises.1 = (f32[136,256]{1,0:T(8,128)S(1)}, f32[3,272,256]{2,1,0:T(8,128)S(1)}) custom-call(f32[136,256]{1,0:T(8,128)S(1)} %core_noises.1.token_ref.refs_0_, f32[136,256]{1,0:T(8,128)S(1)} %collective-permute-done.5.refs_1_, f32[136,256]{1,0:T(8,128)S(1)} %collective-permute-done.6.refs_2_, f32[136,256]{1,0:T(8,128)S(1)} %collective-permute-done.7.refs_3_, ...), custom_call_target="tpu_custom_call" | custom-call | flops 1000000000 | tf_op jit(solution)/shard_map/plane_noises/pallas_call | solution.py:415
  46.0 0.4 collective-permute-start.13
  46.4 1.3 %collective-permute-done.11.r_ref.refs_0_ = f32[128,256]{1,0:T(8,128)S(1)} collective-permute-done((f32[128,256]{1,0:T(8,128)S(1)}, f32[128,256]{1,0:T(8,128)S(1)}, u32[]{:S(2)}, u32[]{:S(2)}) %collective-permute-start.11) | collective-permute-done | bytes 131104 | tf_op jit(solution)/shard_map/ppermute | solution.py:483
  47.7 0.0 collective-permute-start.12
  47.7 2.3 %compose.6 = (f32[8,256,256]{2,1,0:T(8,128)S(1)}, f32[8,256]{1,0:T(8,128)S(1)}, f32[8,256]{1,0:T(8,128)S(1)}) custom-call(f32[4,8,256,256]{3,2,1,0:T(8,128)S(1)} %get-tuple-element.34.g_ref, f32[32,256]{1,0:T(8,128)S(1)} %get-tuple-element.35.delta_ref, f32[32,256]{1,0:T(8,128)S(1)} %get-tuple-element.36.shift_ref, ...), custom_call_target="tpu_custom_call" | custom-call | flops 4000000000 | tf_op jit(solution)/shard_map/compose/pallas_call | solution.py:415
  50.0 1.5 %collective-permute-done.13.other_ref.refs_2_ = f32[136,256]{1,0:T(8,128)S(1)} collective-permute-done((f32[136,256]{1,0:T(8,128)S(1)}, f32[136,256]{1,0:T(8,128)S(1)}, u32[]{:S(2)}, u32[]{:S(2)}) %collective-permute-start.13) | collective-permute-done | bytes 139296 | tf_op jit(solution)/shard_map/ppermute | solution.py:483
  51.5 0.0 collective-permute-done.12.x_ref.refs_1_
  51.5 0.7 %level.1.token_ref = f32[136,256]{1,0:T(8,128)S(1)} custom-call(f32[256,256]{1,0:T(8,128)S(1)} %get-tuple-element.55.own_map_ref, f32[136,256]{1,0:T(8,128)S(1)} %get-tuple-element.53.token_ref.own_ref, f32[128,256]{1,0:T(8,128)S(1)} %collective-permute-done.11.r_ref.refs_0_, f32[128,256]{1,0:T(8,128)S(1)} %collective-permute-done.12.x_ref.refs_1_, ...), custom_call_target="tpu_custom_call" | custom-call | flops 1000000000 | tf_op jit(solution)/shard_map/level/pallas_call | solution.py:415
  52.2 2.7 %collective-permute-start.14 = (f32[136,256]{1,0:T(8,128)S(1)}, f32[136,256]{1,0:T(8,128)S(1)}, u32[]{:S(2)}, u32[]{:S(2)}) collective-permute-start(f32[136,256]{1,0:T(8,128)S(1)} %level.1.token_ref), channel_id=1, source_target_pairs={{0,16},{1,17},{2,18},{3,19},{4,20},{5,21},{6,22},{7,23},{8,24},{9,... | collective-permute-start | bytes 417800 | tf_op jit(solution)/shard_map/ppermute | solution.py:483
  54.9 2.8 %compose.7 = (f32[8,256,256]{2,1,0:T(8,128)S(1)}, f32[8,256]{1,0:T(8,128)S(1)}, f32[8,256]{1,0:T(8,128)S(1)}) custom-call(f32[4,8,256,256]{3,2,1,0:T(8,128)S(1)} %get-tuple-element.34.g_ref, f32[32,256]{1,0:T(8,128)S(1)} %get-tuple-element.35.delta_ref, f32[32,256]{1,0:T(8,128)S(1)} %get-tuple-element.36.shift_ref, ...), custom_call_target="tpu_custom_call" | custom-call | flops 4000000000 | tf_op jit(solution)/shard_map/compose/pallas_call | solution.py:415
  57.7 1.8 %place.1.refs_12_ = f32[528,256]{1,0:T(8,128)S(1)} custom-call(f32[3,256,256]{2,1,0:T(8,128)S(1)} %get-tuple-element.64.maps_ref, f32[3,272,256]{2,1,0:T(8,128)S(1)} %get-tuple-element.65.noises_ref, f32[128,256]{1,0:T(8,128)S(1)} %collective-permute-done.11.r_ref.refs_0_, f32[128,256]{1,0:T(8,128)S(1)} %collective-permute-done.12.x_ref.refs_1_, ...), custom_call_target="tpu_custom_call" | custom-call | flops 1000000 | tf_op jit(solution)/shard_map/place/pallas_call | solution.py:415
  59.5 1.5 %collective-permute-done.14.refs_13_ = f32[136,256]{1,0:T(8,128)S(1)} collective-permute-done((f32[136,256]{1,0:T(8,128)S(1)}, f32[136,256]{1,0:T(8,128)S(1)}, u32[]{:S(2)}, u32[]{:S(2)}) %collective-permute-start.14) | collective-permute-done | bytes 139296 | tf_op jit(solution)/shard_map/ppermute | solution.py:483
  60.9 4.8 %finish.1 = (f32[32,256]{1,0:T(8,128)}, f32[32,256]{1,0:T(8,128)}) custom-call(f32[8,256,256]{2,1,0:T(8,128)S(1)} %get-tuple-element.45.refs_0_, f32[8,256,256]{2,1,0:T(8,128)S(1)} %get-tuple-element.46.refs_1_, f32[8,256,256]{2,1,0:T(8,128)S(1)} %get-tuple-element.54.refs_2_, f32[8,256,256]{2,1,0:T(8,128)S(1)} %get-tuple-element.57.refs_3_, ...), custom_call_target="tpu_custom_call" | custom-call | flops 1000000000 | tf_op jit(solution)/shard_map/finish/pallas_call | solution.py:415
  (6 shorter events, 0.0 us)
Async XLA Ops:
  0.6 17.4 %copy-start = (bf16[32,64,256]{2,1,0:T(8,128)(2,1)S(1)}, bf16[32,64,256]{2,1,0:T(8,128)(2,1)}, u32[]{:S(2)}) copy-start(bf16[32,64,256]{2,1,0:T(8,128)(2,1)} %param.13) | copy-start | bytes 3145732
  0.6 17.4 %copy-start.1 = (bf16[32,64,256]{2,1,0:T(8,128)(2,1)S(1)}, bf16[32,64,256]{2,1,0:T(8,128)(2,1)}, u32[]{:S(2)}) copy-start(bf16[32,64,256]{2,1,0:T(8,128)(2,1)} %param.14) | copy-start | bytes 3145732
  0.7 17.4 %copy-start.2 = (bf16[256,256]{1,0:T(8,128)(2,1)S(1)}, bf16[256,256]{1,0:T(8,128)(2,1)}, u32[]{:S(2)}) copy-start(bf16[256,256]{1,0:T(8,128)(2,1)} %nf_ref.1) | copy-start | bytes 393220
  0.7 17.4 %copy-start.3 = (f32[32,256]{1,0:T(8,128)S(1)}, f32[32,256]{1,0:T(8,128)}, u32[]{:S(2)}) copy-start(f32[32,256]{1,0:T(8,128)} %decay_ref.1) | copy-start | bytes 98308
  0.7 17.4 %copy-start.4 = (f32[256]{0:T(256)S(1)}, f32[256]{0:T(256)}, u32[]{:S(2)}) copy-start(f32[256]{0:T(256)} %param.10) | copy-start | bytes 3076
  0.7 17.4 %copy-start.5 = (f32[64]{0:T(128)S(1)}, f32[64]{0:T(128)}, u32[]{:S(2)}) copy-start(f32[64]{0:T(128)} %param.16) | copy-start | bytes 772
  13.4 18.3 %collective-permute-start.3 = (f32[256,256]{1,0:T(8,128)S(1)}, f32[256,256]{1,0:T(8,128)S(1)}, u32[]{:S(2)}, u32[]{:S(2)}) collective-permute-start(f32[256,256]{1,0:T(8,128)S(1)} %get-tuple-element.42.own_map_ref.refs_0_), channel_id=1, source_target_pairs={{0,1},{1,0},{2,3},{3,2},{4,5},{5,4},{6,7},{7,6},{8,9},{9,8},{10,11... | collective-permute-start | bytes 786440 | tf_op jit(solution)/shard_map/ppermute | solution.py:483
  13.9 21.7 %collective-permute-start = (f32[256,256]{1,0:T(8,128)S(1)}, f32[256,256]{1,0:T(8,128)S(1)}, u32[]{:S(2)}, u32[]{:S(2)}) collective-permute-start(f32[256,256]{1,0:T(8,128)S(1)} %get-tuple-element.42.own_map_ref.refs_0_), channel_id=1, source_target_pairs={{0,2},{1,3},{2,0},{3,1},{4,6},{5,7},{6,4},{7,5},{8,10},{9,11},{10,... | collective-permute-start | bytes 786440 | tf_op jit(solution)/shard_map/ppermute | solution.py:483
  16.5 19.5 %collective-permute-start.1 = (f32[256,256]{1,0:T(8,128)S(1)}, f32[256,256]{1,0:T(8,128)S(1)}, u32[]{:S(2)}, u32[]{:S(2)}) collective-permute-start(f32[256,256]{1,0:T(8,128)S(1)} %get-tuple-element.42.own_map_ref.refs_0_), channel_id=1, source_target_pairs={{0,4},{1,5},{2,6},{3,7},{4,0},{5,1},{6,2},{7,3},{8,12},{9,13},{10,... | collective-permute-start | bytes 786440 | tf_op jit(solution)/shard_map/ppermute | solution.py:483
  18.0 18.0 %collective-permute-start.2 = (f32[256,256]{1,0:T(8,128)S(1)}, f32[256,256]{1,0:T(8,128)S(1)}, u32[]{:S(2)}, u32[]{:S(2)}) collective-permute-start(f32[256,256]{1,0:T(8,128)S(1)} %get-tuple-element.42.own_map_ref.refs_0_), channel_id=1, source_target_pairs={{0,6},{1,7},{2,4},{3,5},{4,2},{5,3},{6,0},{7,1},{8,14},{9,15},{10,... | collective-permute-start | bytes 786440 | tf_op jit(solution)/shard_map/ppermute | solution.py:483
  30.3 1.4 %collective-permute-start.4 = (f32[136,256]{1,0:T(8,128)S(1)}, f32[136,256]{1,0:T(8,128)S(1)}, u32[]{:S(2)}, u32[]{:S(2)}) collective-permute-start(f32[136,256]{1,0:T(8,128)S(1)} %get-tuple-element.43.own_ref), channel_id=1, source_target_pairs={{0,1},{1,0},{2,3},{3,2},{4,5},{5,4},{6,7},{7,6},{8,9},{9,8},{10,11... | collective-permute-start | bytes 417800 | tf_op jit(solution)/shard_map/ppermute | solution.py:483
  32.5 11.4 %collective-permute-start.5 = (f32[136,256]{1,0:T(8,128)S(1)}, f32[136,256]{1,0:T(8,128)S(1)}, u32[]{:S(2)}, u32[]{:S(2)}) collective-permute-start(f32[136,256]{1,0:T(8,128)S(1)} %core_noises.1.token_ref.refs_0_), channel_id=1, source_target_pairs={{0,2},{1,3},{2,0},{3,1},{4,6},{5,7},{6,4},{7,5},{8,10},{9,11},{10,... | collective-permute-start | bytes 417800 | tf_op jit(solution)/shard_map/ppermute | solution.py:483
  34.1 9.7 %collective-permute-start.6 = (f32[136,256]{1,0:T(8,128)S(1)}, f32[136,256]{1,0:T(8,128)S(1)}, u32[]{:S(2)}, u32[]{:S(2)}) collective-permute-start(f32[136,256]{1,0:T(8,128)S(1)} %core_noises.1.token_ref.refs_0_), channel_id=1, source_target_pairs={{0,4},{1,5},{2,6},{3,7},{4,0},{5,1},{6,2},{7,3},{8,12},{9,13},{10,... | collective-permute-start | bytes 417800 | tf_op jit(solution)/shard_map/ppermute | solution.py:483
  35.7 8.2 %collective-permute-start.7 = (f32[136,256]{1,0:T(8,128)S(1)}, f32[136,256]{1,0:T(8,128)S(1)}, u32[]{:S(2)}, u32[]{:S(2)}) collective-permute-start(f32[136,256]{1,0:T(8,128)S(1)} %core_noises.1.token_ref.refs_0_), channel_id=1, source_target_pairs={{0,6},{1,7},{2,4},{3,5},{4,2},{5,3},{6,0},{7,1},{8,14},{9,15},{10,... | collective-permute-start | bytes 417800 | tf_op jit(solution)/shard_map/ppermute | solution.py:483
  36.0 2.8 %collective-permute-start.10 = (f32[256,256]{1,0:T(8,128)S(1)}, f32[256,256]{1,0:T(8,128)S(1)}, u32[]{:S(2)}, u32[]{:S(2)}) collective-permute-start(f32[256,256]{1,0:T(8,128)S(1)} %collective-permute-done.2.refs_6_), channel_id=1, source_target_pairs={{0,1},{1,0},{2,3},{3,2},{4,5},{5,4},{6,7},{7,6},{8,9},{9,8},{10,11... | collective-permute-start | bytes 786440 | tf_op jit(solution)/shard_map/ppermute | solution.py:483
  36.0 3.8 %collective-permute-start.8 = (f32[256,256]{1,0:T(8,128)S(1)}, f32[256,256]{1,0:T(8,128)S(1)}, u32[]{:S(2)}, u32[]{:S(2)}) collective-permute-start(f32[256,256]{1,0:T(8,128)S(1)} %collective-permute-done.refs_2_), channel_id=1, source_target_pairs={{0,1},{1,0},{2,3},{3,2},{4,5},{5,4},{6,7},{7,6},{8,9},{9,8},{10,11... | collective-permute-start | bytes 786440 | tf_op jit(solution)/shard_map/ppermute | solution.py:483
  38.8 1.6 %collective-permute-start.9 = (f32[256,256]{1,0:T(8,128)S(1)}, f32[256,256]{1,0:T(8,128)S(1)}, u32[]{:S(2)}, u32[]{:S(2)}) collective-permute-start(f32[256,256]{1,0:T(8,128)S(1)} %collective-permute-done.1.refs_4_), channel_id=1, source_target_pairs={{0,1},{1,0},{2,3},{3,2},{4,5},{5,4},{6,7},{7,6},{8,9},{9,8},{10,11... | collective-permute-start | bytes 786440 | tf_op jit(solution)/shard_map/ppermute | solution.py:483
  42.1 5.6 %collective-permute-start.11 = (f32[128,256]{1,0:T(8,128)S(1)}, f32[128,256]{1,0:T(8,128)S(1)}, u32[]{:S(2)}, u32[]{:S(2)}) collective-permute-start(f32[128,256]{1,0:T(8,128)S(1)} %get-tuple-element.56), channel_id=1, source_target_pairs={{0,8},{1,9},{2,10},{3,11},{4,12},{5,13},{6,14},{7,15},{8,0},{9,1},... | collective-permute-start | bytes 393224 | tf_op jit(solution)/shard_map/ppermute | solution.py:483
  46.0 5.5 %collective-permute-start.13 = (f32[136,256]{1,0:T(8,128)S(1)}, f32[136,256]{1,0:T(8,128)S(1)}, u32[]{:S(2)}, u32[]{:S(2)}) collective-permute-start(f32[136,256]{1,0:T(8,128)S(1)} %get-tuple-element.53.token_ref.own_ref), channel_id=1, source_target_pairs={{0,8},{1,9},{2,10},{3,11},{4,12},{5,13},{6,14},{7,15},{8,0},{9,1},... | collective-permute-start | bytes 417800 | tf_op jit(solution)/shard_map/ppermute | solution.py:483
  47.7 3.8 %collective-permute-start.12 = (f32[128,256]{1,0:T(8,128)S(1)}, f32[128,256]{1,0:T(8,128)S(1)}, u32[]{:S(2)}, u32[]{:S(2)}) collective-permute-start(f32[128,256]{1,0:T(8,128)S(1)} %collective-permute-done.11.r_ref.refs_0_), channel_id=1, source_target_pairs={{0,1},{1,0},{2,3},{3,2},{4,5},{5,4},{6,7},{7,6},{8,9},{9,8},{10,11... | collective-permute-start | bytes 393224 | tf_op jit(solution)/shard_map/ppermute | solution.py:483
  52.2 8.7 %collective-permute-start.14 = (f32[136,256]{1,0:T(8,128)S(1)}, f32[136,256]{1,0:T(8,128)S(1)}, u32[]{:S(2)}, u32[]{:S(2)}) collective-permute-start(f32[136,256]{1,0:T(8,128)S(1)} %level.1.token_ref), channel_id=1, source_target_pairs={{0,16},{1,17},{2,18},{3,19},{4,20},{5,21},{6,22},{7,23},{8,24},{9,... | collective-permute-start | bytes 417800 | tf_op jit(solution)/shard_map/ppermute | solution.py:483

commit v3 on v2

v3 whole, which is shorter than its diff:
```python
import functools

import jax
import jax.numpy as jnp
from jax import lax
from jax.experimental import pallas as pl
from jax.experimental.pallas import tpu as pltpu
from jax.sharding import PartitionSpec as P

f32, bf16 = jnp.float32, jnp.bfloat16
PLANE = 8


def nn(a, b):
    return jnp.dot(a, b, preferred_element_type=f32)


def nt(a, b):
    return lax.dot_general(a, b, (((1,), (1,)), ((), ())), preferred_element_type=f32)


def halves(x):
    high = x.astype(bf16)
    return high, (x - high.astype(f32)).astype(bf16)


def times(late, early):
    (lh, ll), (eh, el) = late, early
    return nn(lh, eh) + (nn(ll, eh) + nn(lh, el))


def advance(late, noise, shift):
    n = noise.shape[1]
    lh, ll = late
    xh, xl = halves(jnp.concatenate([times(late, halves(noise)), shift], axis=0))
    out = nt(xh, lh) + (nt(xl, lh) + nt(xh, ll))
    return out[:n], out[n:]


def wide(col):
    return jnp.concatenate([col, col], axis=1)


def apart(late):
    row = diag_row(late)
    return row, spread(row), jnp.where(eye_mask(late.shape[0]), 0.0, late).astype(bf16)


def conjugate(late, noise):
    row, col, rest = late
    x = wide(col) * noise + nn(rest, noise.astype(bf16))
    return x * row + nt(x.astype(bf16), rest)


def through(late, shift):
    return row_of(jnp.sum(late * shift, axis=1, keepdims=True))


def joined(early, late):
    parts = halves(late[0])
    noise, shift = advance(parts, early[1], early[2])
    return times(parts, halves(early[0])), noise + late[1], shift + late[2]


def eye_mask(n):
    return lax.broadcasted_iota(jnp.int32, (n, n), 0) == lax.broadcasted_iota(jnp.int32, (n, n), 1)


def column(row):
    n = row.shape[1]
    out = []
    for k in range(0, n, 128):
        m = min(128, n - k)
        out.append(jnp.sum(jnp.where(eye_mask(m), row[:, k:k + m], 0.0), axis=1, keepdims=True))
    return out[0] if len(out) == 1 else jnp.concatenate(out, axis=0)


def spread(row):
    n = row.shape[1]
    return jnp.concatenate([jnp.broadcast_to(row[:, k:k + 128], (128, 128)).T for k in range(0, n, 128)], axis=0)


def row_of(col):
    n = col.shape[0]
    out = [jnp.sum(jnp.where(eye_mask(128), col[k:k + 128], 0.0), axis=0, keepdims=True) for k in range(0, n, 128)]
    return jnp.concatenate(out, axis=1)


def diag_row(x):
    n = x.shape[1]
    out = [jnp.sum(jnp.where(eye_mask(128), x[k:k + 128, k:k + 128], 0.0), axis=0, keepdims=True)
           for k in range(0, n, 128)]
    return jnp.concatenate(out, axis=1)


def rows16(row):
    return jnp.broadcast_to(row, (16, row.shape[1]))


def pack(noise, shift):
    n = noise.shape[1]
    h = n // 2
    lower = lax.broadcasted_iota(jnp.int32, (h, h), 0) >= lax.broadcasted_iota(jnp.int32, (h, h), 1)
    a, b, c = noise[:h, :h], noise[:h, h:], noise[h:, h:]
    body = jnp.concatenate([jnp.where(lower, a, c), b], axis=1)
    extra = jnp.concatenate([jnp.zeros((1, h), f32), diag_row(noise)[:, h:]], axis=1)
    return jnp.concatenate([body, shift[0:1], extra, jnp.zeros((6, n), f32)], axis=0)


def unpack(x):
    n = x.shape[1]
    h = n // 2
    i = lax.broadcasted_iota(jnp.int32, (h, h), 0)
    j = lax.broadcasted_iota(jnp.int32, (h, h), 1)
    body, b = x[:h, :h], x[:h, h:]
    turned = body.T
    a = jnp.where(i >= j, body, turned)
    c = jnp.where(i == j, x[h + 1:h + 2, h:], jnp.where(i < j, body, turned))
    noise = jnp.concatenate([jnp.concatenate([a, b], axis=1), jnp.concatenate([b.T, c], axis=1)], axis=0)
    return noise, x[h:h + 1]


def rank_of(axes):
    rank = 0
    for name, size in axes:
        rank = rank * size + lax.axis_index(name)
    return rank


def bit_of(rank, bit):
    return (rank // bit) % 2


def whole(upper, mine_ref, others_ref):
    mine, others = mine_ref[...], others_ref[...]
    return jnp.concatenate([jnp.where(upper, others, mine), jnp.where(upper, mine, others)], axis=0)


def identity(n):
    return jnp.where(eye_mask(n), 1.0, 0.0), jnp.zeros((n, n), f32), jnp.zeros((16, n), f32)


def maps_kernel(subs, axes, mean_hbm, decay_hbm, coup_hbm, omap_hbm, gain_hbm, seen_hbm,
                g_ref, e_ref, dcol_ref, delta_ref, shift_ref, maps_ref, total_ref,
                mean_ref, decay_ref, coup_ref, omap_ref, gain_ref, seen_ref, small_sem, sem, g_s, part_s, eh_s, row_s):
    n = decay_ref.shape[1]
    steps = coup_ref.shape[1]
    small = [pltpu.make_async_copy(x, y, small_sem.at[k]) for k, (x, y) in enumerate(
        [(mean_hbm, mean_ref), (decay_hbm, decay_ref), (seen_hbm, seen_ref)])]

    def chunk(j):
        return [pltpu.make_async_copy(x.at[:, j], y.at[:, j], sem.at[k, j]) for k, (x, y) in enumerate(
            [(coup_hbm, coup_ref), (omap_hbm, omap_ref), (gain_hbm, gain_ref)])]

    for c in small + chunk(0):
        c.start()
    for j in range(1, steps):
        for c in chunk(j):
            c.start()
    for c in small:
        c.wait()
    begins = rank_of(axes) == 0

    def step(j, first):
        for c in chunk(j):
            c.wait()
        all_subs = range(subs)
        rows = [decay_ref[pl.ds(s * steps + j, 1), :] for s in all_subs]
        obs_f = [(omap_ref[s, j].astype(f32) * rows[s] + nn(omap_ref[s, j], coup_ref[s, j])).astype(bf16)
                 for s in all_subs]

        def build(s):
            t = s * steps + j
            gain = gain_ref[s, j]
            e = coup_ref[s, j].astype(f32) - nn(gain.T, obs_f[s])
            e_h = e.astype(bf16)
            e_ref[s, j] = e_h
            eh_s[s] = e_h
            col = spread(rows[s])
            dcol_ref[s, j] = col
            if first:
                start = (s == 0) & begins
                delta = jnp.where(start, 0.0, jnp.ones((1, n), f32))
                b = jnp.where(start, mean_ref[...], 0.0)
                g_new = e * delta
                g_s[s] = g_new
                g_ref[s, j] = g_new
            else:
                delta = row_s[s, 0:1, :]
                b = row_s[s, 1:2, :]
                part_s[s] = jnp.concatenate([col, col], axis=1) * g_s[s] + e * delta
            along = row_of(jnp.sum(e * b, axis=1, keepdims=True))
            shift = jnp.sum(gain.astype(f32) * column(seen_ref[pl.ds(t, 1), :]), axis=0, keepdims=True)
            b_new = rows[s] * b + along + shift
            shift_ref[pl.ds(t, 1), :] = b_new
            delta_ref[pl.ds(t, 1), :] = delta * rows[s]
            row_s[s, 0:1, :] = delta * rows[s]
            row_s[s, 1:2, :] = b_new

        def follow(s):
            if not first:
                g_new = part_s[s] + nn(eh_s[s], g_s[s].astype(bf16))
                g_s[s] = g_new
                g_ref[s, j] = g_new

        build(0)
        build(1)
        follow(0)
        build(2)
        follow(1)
        build(3)
        follow(2)
        follow(3)

    step(0, True)
    lax.fori_loop(1, steps, lambda j, c: (step(j, False), c)[1], 0)

    eye = eye_mask(n)
    maps = [g_ref[s, steps - 1] + jnp.where(eye, delta_ref[(s + 1) * steps - 1:(s + 1) * steps, :], 0.0)
            for s in range(subs)]
    for s in range(subs):
        maps_ref[s] = maps[s]
    parts = [halves(m) for m in maps]
    low, high = times(parts[1], parts[0]), times(parts[3], parts[2])
    maps_ref[subs] = low
    maps_ref[subs + 1] = high
    total_ref[...] = times(halves(high), halves(low))


def noises_kernel(subs, axes, init_ref, decay_ref, e_ref, dcol_ref, omap_ref, gain_ref, nf_ref, var_ref, shift_ref,
                  maps_ref, diag_ref, noises_ref, total_ref, q_s, shaped_s):
    n = nf_ref.shape[0]
    m = omap_ref.shape[2]
    steps = e_ref.shape[1]
    nf = nf_ref[...]
    var_col = column(var_ref[...])

    all_subs = range(subs)

    def shape_step(j, slot):
        obs_g = nn(jnp.concatenate([omap_ref[s, j] for s in all_subs], axis=0), nf).astype(bf16)
        for s in all_subs:
            shaped_s[slot, s] = (nf.astype(f32) - nn(gain_ref[s, j].T, obs_g[s * m:(s + 1) * m])).astype(bf16)

    def noise(s, j, slot):
        shaped, gain = shaped_s[slot, s], gain_ref[s, j]
        return nt(shaped, shaped) + nn(gain.T, (gain.astype(f32) * var_col).astype(bf16))

    def first_half(s, j, q):
        d_col = jnp.concatenate([dcol_ref[s, j], dcol_ref[s, j]], axis=1)
        return d_col * q + nn(e_ref[s, j], q.astype(bf16))

    def second_half(s, j, slot, x):
        return x * decay_ref[pl.ds(s * steps + j, 1), :] + (nt(x.astype(bf16), e_ref[s, j]) + noise(s, j, slot))

    def step(j, carry):
        slot = j % 2
        x = [first_half(s, j, q_s[s]) for s in all_subs]
        shape_step(jnp.minimum(j + 1, steps - 1), 1 - slot)
        for s in all_subs:
            q_new = second_half(s, j, slot, x[s])
            q_s[s] = q_new
            diag_ref[pl.ds(s * steps + j, 1), :] = diag_row(q_new)
        return carry

    shape_step(0, 0)
    shape_step(1, 1)
    for s in all_subs:
        q_s[s] = noise(s, 0, 0)

    @pl.when(rank_of(axes) == 0)
    def _():
        q_s[0] = second_half(0, 0, 0, first_half(0, 0, jnp.where(eye_mask(n), init_ref[...], 0.0)))

    for s in all_subs:
        diag_ref[pl.ds(s * steps, 1), :] = diag_row(q_s[s])
    lax.fori_loop(1, steps, step, 0)

    shift = [shift_ref[(s + 1) * steps - 1:(s + 1) * steps, :] for s in range(subs)]
    pairs = [(conjugate(apart(maps_ref[s + 1]), q_s[s]) + q_s[s + 1], through(maps_ref[s + 1], shift[s]) + shift[s + 1])
             for s in (0, 2)]
    last = maps_ref[subs + 1]
    total_ref[...] = pack(conjugate(apart(last), pairs[0][0]) + pairs[1][0], through(last, pairs[0][1]) + pairs[1][1])
    for s in range(subs):
        noises_ref[s, 0:n, :] = q_s[s]
        noises_ref[s, n:, :] = rows16(shift[s])


def core_kernel(axes, own_map_ref, other_map_ref, own_ref, other_ref, out_ref):
    upper = rank_of(axes) % 2 == 1
    own, other = unpack(own_ref[...]), unpack(other_ref[...])
    late = jnp.where(upper, own_map_ref[...], other_map_ref[...])
    early_noise, early_shift = (jnp.where(upper, a, b) for a, b in zip(other, own))
    late_noise, late_shift = (jnp.where(upper, a, b) for a, b in zip(own, other))
    out_ref[...] = pack(conjugate(apart(late), early_noise) + late_noise, through(late, early_shift) + late_shift)


def fetch(rank, refs, dst, sem):
    place = (rank % PLANE) // (PLANE // len(refs))
    copies = [pltpu.make_async_copy(r, dst.at[place ^ k], sem.at[k]) for k, r in enumerate(refs)]
    for c in copies:
        c.start()
    for c in copies:
        c.wait()


def plane_maps_kernel(axes, *refs):
    ins, refs = refs[:PLANE], refs[PLANE:]
    late_ref, rest_ref, col_ref, row_ref, total_ref, half_ref, picks_ref, map_s, chip_s, sem = refs
    rank = rank_of(axes)
    fetch(rank, ins, map_s, sem)
    place = rank % PLANE
    y = bit_of(rank, 4)

    def keep(k, late):
        late_ref[k] = late
        row_ref[k:k + 1, :], col_ref[k], rest_ref[k] = apart(late)

    chips = [times(halves(map_s[2 * k + 1]), halves(map_s[2 * k])) for k in range(4)]
    for k in range(4):
        chip_s[k] = chips[k]
    pairs = [times(halves(chips[2 * k + 1]), halves(chips[2 * k])) for k in range(2)]
    total_ref[...] = times(halves(pairs[1]), halves(pairs[0]))
    for k, late in enumerate((chips[1], chips[3], pairs[1])):
        keep(k, late)
    h = half_ref.shape[0]
    half_ref[...] = jnp.where(rank % 2 == 1, total_ref[h:], total_ref[:h])
    picks_ref[0] = pairs[0]
    picks_ref[1] = chip_s[2 * y]
    picks_ref[2] = map_s[place - place % 2]


def plane_noises_kernel(axes, *refs):
    ins, (late_ref, rest_ref, col_ref, row_ref, core_ref, _, _, total_ref, picks_ref, in_s, sem) = refs[:4], refs[4:]
    rank = rank_of(axes)
    fetch(rank, ins, in_s, sem)
    n = late_ref.shape[-1]

    def join(k, early, late):
        noise = conjugate((row_ref[k:k + 1, :], col_ref[k], rest_ref[k]), early[0])
        return noise + late[0], through(late_ref[k], early[1]) + late[1]

    def pick(k, element):
        picks_ref[k, 0:n], picks_ref[k, n:] = element[0], rows16(element[1])

    chips = [unpack(in_s[k]) for k in range(4)]
    pairs = [join(k, chips[2 * k], chips[2 * k + 1]) for k in range(2)]
    total_ref[...] = pack(*join(2, pairs[0], pairs[1]))
    pick(0, pairs[0])
    pick(1, unpack(in_s[2 * bit_of(rank, 4)]))
    pick(2, unpack(core_ref[...]))


def level_kernel(axes, bit, own_map_ref, own_ref, r_ref, x_ref, other_ref, inner_ref, token_ref, *outs):
    rank = rank_of(axes)
    upper, high = rank % 2 == 1, bit_of(rank, bit) == 1
    other_map, own_map = whole(upper, r_ref, x_ref), own_map_ref[...]
    other, own = unpack(other_ref[...]), unpack(own_ref[...])
    late = jnp.where(high, own_map, other_map)
    early_noise, early_shift = (jnp.where(high, a, b) for a, b in zip(other, own))
    late_noise, late_shift = (jnp.where(high, a, b) for a, b in zip(own, other))
    outs[0][...] = pack(conjugate(apart(late), early_noise) + late_noise, through(late, early_shift) + late_shift)
    if len(outs) > 1:
        outs[1][...] = times(halves(late), halves(jnp.where(high, other_map, own_map)))
        h = outs[2].shape[0]
        outs[2][...] = jnp.where(upper, outs[1][h:], outs[1][:h])


def inner_kernel(axes, maps_ref, noises_ref, out_ref):
    rank = rank_of(axes)
    n = out_ref.shape[1]
    one = identity(n)
    parts = []
    for k, bit in enumerate((4, 2, 1)):
        element = (maps_ref[k], noises_ref[k, 0:n, :], noises_ref[k, n:, :])
        parts.append(tuple(jnp.where(bit_of(rank, bit) == 1, a, b) for a, b in zip(element, one)))
    em, en, es = joined(parts[0], joined(parts[1], parts[2]))
    out_ref[0:n, :], out_ref[n:2 * n, :], out_ref[2 * n:, :] = em, en, es


def place_kernel(axes, bits, subs_ref, sub_noises_ref, inner_ref, *refs):
    out_ref, rest_ref, col_ref, row_ref = refs[-4:]
    rank = rank_of(axes)
    upper = rank % 2 == 1
    n = out_ref.shape[2]
    before = identity(n)
    for k, bit in enumerate(bits):
        r_ref, x_ref, other_ref = refs[3 * k:3 * k + 3]
        noise, shift = unpack(other_ref[...])
        other = whole(upper, r_ref, x_ref), noise, rows16(shift)
        new = other if k == 0 else joined(other, before)
        before = tuple(jnp.where(bit_of(rank, bit) == 1, a, b) for a, b in zip(new, before))
    inner = inner_ref[0:n, :], inner_ref[n:2 * n, :], inner_ref[2 * n:, :]

    def put(s, element):
        em, en, es = element
        out_ref[s, 0:n, :], out_ref[s, n:2 * n, :], out_ref[s, 2 * n:, :] = em, en, es

    def sub(s, carry):
        before = out_ref[s, 0:n, :], out_ref[s, n:2 * n, :], out_ref[s, 2 * n:, :]
        put(s + 1, joined(before, (subs_ref[s], sub_noises_ref[s, 0:n, :], sub_noises_ref[s, n:, :])))
        return carry

    put(0, joined(before, inner))
    lax.fori_loop(0, out_ref.shape[0] - 1, sub, 0)

    def split(s, carry):
        row_ref[s, 0:1, :], col_ref[s], rest_ref[s] = apart(out_ref[s, 0:n, :])
        return carry

    lax.fori_loop(0, out_ref.shape[0], split, 0)


def turn_kernel(sub, g_ref, delta_ref, token_ref, high_ref, low_ref, diag_ref):
    steps, n = high_ref.shape[:2]
    eye = eye_mask(n)

    def step(j, carry):
        turned = g_ref[sub, j].T
        diag_ref[pl.ds(j, 1), :] = delta_ref[pl.ds(sub * steps + j, 1), :] + diag_row(turned)
        high_ref[j], low_ref[j] = halves(jnp.where(eye, 0.0, turned))
        return carry

    lax.fori_loop(0, steps, step, 0, unroll=2)


def finish_kernel(axes, bit, parts, *refs):
    high, low, diag = refs[:parts], refs[parts:2 * parts], refs[2 * parts:3 * parts]
    var_ref, mean_ref, place_ref, rest_ref, col_ref, arow_ref, r_ref, means_ref, vars_ref, left_s, row_s = refs[3 * parts:]
    n = left_s.shape[-1]
    steps = high[0].shape[0]
    is_high = bit_of(rank_of(axes), bit) == 1
    received, moved = unpack(r_ref[...])
    for s in range(parts):
        noise = conjugate((arow_ref[s, 0:1, :], col_ref[s], rest_ref[s]), received)
        p = jnp.where(is_high, noise, 0.0) + place_ref[s, n:2 * n, :]
        mean = jnp.where(is_high, through(place_ref[s, 0:n, :], moved), 0.0) + place_ref[s, 2 * n:2 * n + 1, :]
        mh, ml = halves(mean)
        left_s[s, 0:n, :] = p.astype(bf16)
        left_s[s, n:, :] = jnp.concatenate([mh, ml, jnp.zeros((14, n), bf16)], axis=0)
        row_s[s, 0:1, :] = mean
        row_s[s, 1:2, :] = diag_row(p)

    def step(j, carry):
        both = [nn(left_s[s], high[s][j]) for s in range(parts)]
        rest = [nn(left_s[s, n:, :], low[s][j]) for s in range(parts)]
        for s in range(parts):
            t = s * steps + j
            d = diag[s][pl.ds(j, 1), :]
            vars_ref[pl.ds(t, 1), :] = (var_ref[pl.ds(t, 1), :] + d * (d * row_s[s, 1:2, :] + 2.0 * diag_row(both[s]))
                                        + jnp.sum(high[s][j].astype(f32) * both[s][:n], axis=0, keepdims=True))
            means_ref[pl.ds(t, 1), :] = (mean_ref[pl.ds(t, 1), :] + d * row_s[s, 0:1, :]
                                         + both[s][n:n + 1] + (both[s][n + 1:n + 2] + rest[s][0:1]))
        return carry

    lax.fori_loop(0, steps, step, 0)


def vmem():
    return pl.BlockSpec(memory_space=pltpu.VMEM)


def anywhere():
    return pl.BlockSpec(memory_space=pl.ANY)


def shape(*dims, dtype=f32):
    return jax.ShapeDtypeStruct(dims, dtype)


def call(kernel, name, outs, args, specs=None, scratch=(), limit=16, flops=10 ** 9):
    return pl.pallas_call(
        kernel,
        in_specs=specs or [vmem()] * len(args),
        out_specs=[vmem()] * len(outs),
        out_shape=outs,
        scratch_shapes=scratch,
        compiler_params=pltpu.CompilerParams(vmem_limit_bytes=limit * 1024 * 1024),
        cost_estimate=pl.CostEstimate(flops=flops, bytes_accessed=0, transcendentals=0),
        name=name,
    )(*args)


def hbm():
    return pl.BlockSpec(memory_space=pltpu.HBM)


def step_maps(axes, subs, init_mean, decay, coupling, obs_map, gain, observed):
    T, n = decay.shape
    m = obs_map.shape[1]
    steps = T // subs
    outs = [shape(subs, steps, n, n), shape(subs, steps, n, n, dtype=bf16), shape(subs, steps, n, 128),
            shape(T, n), shape(T, n), shape(subs + 2, n, n), shape(n, n)]
    args = [init_mean.reshape(1, n), decay, coupling.reshape(subs, steps, n, n), obs_map.reshape(subs, steps, m, n),
            gain.reshape(subs, steps, m, n), observed]
    scratch = [pltpu.VMEM(x.shape, x.dtype) for x in args]
    args = [pltpu.with_memory_space_constraint(x, pltpu.HBM) for x in args]
    scratch += [pltpu.SemaphoreType.DMA((3,)), pltpu.SemaphoreType.DMA((3, steps)), pltpu.VMEM((subs, n, n), f32),
                pltpu.VMEM((subs, n, n), f32), pltpu.VMEM((subs, n, n), bf16), pltpu.VMEM((subs, 8, n), f32)]
    return call(functools.partial(maps_kernel, subs, axes), "step_maps", outs, args, [hbm()] * len(args), scratch,
                limit=26, flops=10 ** 10)


def step_noises(axes, subs, init_var, decay, e, dcol, obs_map, gain, noise_factor, obs_var, shift, maps):
    T, n = decay.shape
    m = obs_map.shape[1]
    steps = T // subs
    args = [init_var.reshape(1, n), decay, e, dcol, obs_map.reshape(subs, steps, m, n),
            gain.reshape(subs, steps, m, n), noise_factor, obs_var.reshape(1, m), shift, maps]
    return call(functools.partial(noises_kernel, subs, axes), "step_noises",
                [shape(T, n), shape(subs, n + 16, n), shape(n // 2 + 8, n)], args,
                scratch=[pltpu.VMEM((subs, n, n), f32), pltpu.VMEM((2, subs, n, n), bf16)])


def turn(sub, g, delta, token):
    _, steps, n, _ = g.shape
    return call(functools.partial(turn_kernel, sub), "turn",
                [shape(steps, n, n, dtype=bf16), shape(steps, n, n, dtype=bf16), shape(steps, n)],
                [g, delta, token], [vmem()] * 2 + [anywhere()], flops=4 * 10 ** 9)


def finish(axes, bit, turned, var, mean, placed, r):
    parts = len(turned)
    T, n = var.shape
    high, low, diag = zip(*turned)
    return call(functools.partial(finish_kernel, axes, bit, parts), "finish", [shape(T, n)] * 2,
                [*high, *low, *diag, var, mean, *placed, r],
                scratch=[pltpu.VMEM((parts, n + 16, n), bf16), pltpu.VMEM((parts, 8, n), f32)])


def per_device(axes, init_mean, init_var, decay, coupling, obs_map, gain, noise_factor, obs_var, observed):
    n = decay.shape[1]
    h = n // 2
    subs = 4
    count = 1
    for _, size in axes:
        count *= size
    names = tuple(name for name, _ in axes)

    def swap(x, bit):
        return lax.ppermute(x, names, [(k, k ^ bit) for k in range(count)])

    bits = []
    bit = PLANE
    while bit < count:
        bits.append(bit)
        bit *= 2

    g, e, dcol, delta, shift, maps, own = step_maps(axes, subs, init_mean, decay, coupling, obs_map, gain, observed)
    far = [swap(own, bit) for bit in (2, 4, 6)]
    other = swap(own, 1)
    diag, noises, packed = step_noises(
        axes, subs, init_var, decay, e, dcol, obs_map, gain, noise_factor, obs_var, shift, maps)
    other_packed = swap(packed, 1)
    (chip,) = call(functools.partial(core_kernel, axes), "core_noises", [shape(h + 8, n)],
                   [own, other, packed, other_packed])
    chips = [chip] + [swap(chip, bit) for bit in (2, 4, 6)]
    *far, _ = lax.optimization_barrier((*far, chip))
    all_maps = [own, other] + [v for r in far for v in (r, swap(r, 1))]
    turned = [turn(0, g, delta, chip)]
    *late, total, half, map_picks = call(
        functools.partial(plane_maps_kernel, axes), "plane_maps",
        [shape(3, n, n), shape(3, n, n, dtype=bf16), shape(3, n, 128), shape(8, n), shape(n, n), shape(h, n), shape(3, n, n)],
        all_maps, [anywhere()] * PLANE,
        [pltpu.VMEM((PLANE, n, n), f32), pltpu.VMEM((4, n, n), f32), pltpu.SemaphoreType.DMA((PLANE,))])
    turned.append(turn(1, g, delta, total))
    packed, noise_picks = call(
        functools.partial(plane_noises_kernel, axes), "plane_noises",
        [shape(h + 8, n), shape(3, n + 16, n)],
        [*chips, *late, other_packed, turned[0][2], turned[1][2]],
        [anywhere()] * 4 + [vmem()] * 5 + [anywhere()] * 2,
        [pltpu.VMEM((4, h + 8, n), f32), pltpu.SemaphoreType.DMA((4,))])
    (inner,) = call(functools.partial(inner_kernel, axes), "inner", [shape(2 * n + 16, n)], [map_picks, noise_picks])
    received = []
    for k, bit in enumerate(bits[:-1]):
        moving = swap(packed, bit)
        r, packed = lax.optimization_barrier((swap(half, bit), packed))
        got = (r, swap(r, 1), moving)
        received += got
        more = k < len(bits) - 2
        if k == 0:
            turned.append(turn(2, g, delta, packed))
        args = [total, packed, *got, inner, turned[2][2]]
        new = call(functools.partial(level_kernel, axes, bit), "level",
                   [shape(h + 8, n)] + ([shape(n, n), shape(h, n)] if more else []), args,
                   [vmem()] * 5 + [anywhere()] * 2)
        if k == 0:
            turned.append(turn(3, g, delta, new[0]))
        packed = new[0]
        if more:
            total, half = new[1:]
    placed = call(functools.partial(place_kernel, axes, bits[:-1]), "place",
                  [shape(subs, 2 * n + 16, n), shape(subs, n, n, dtype=bf16), shape(subs, n, 128), shape(subs, 8, n)],
                    [maps, noises, inner, *received], flops=10 ** 5)
    r = swap(packed, bits[-1])
    return tuple(finish(axes, bits[-1], turned, diag, shift, placed, r))


def solution(mesh):
    axes = tuple((name, mesh.shape[name]) for name in mesh.axis_names)
    time = P(tuple(mesh.axis_names))
    return jax.shard_map(
        functools.partial(per_device, axes),
        mesh=mesh,
        in_specs=(P(), P(), time, time, time, time, P(), P(), time),
        out_specs=(time, time),
        check_vma=False,
    )
```

time: 65.9 us -> 58.4 us (0.89)
  Pallas kernels: 44.9 us -> 36.1 us
  starting transfers between devices: 13.7 us -> 15 us
    pallas_call x12 -> x13, Pallas kernels: 44.9 us -> 36.1 us  [call(): pl.pallas_call(kernel, in_specs=specs or [vmem()] * len(args), out_specs=...]
    ppermute x15, starting transfers between devices: 13.7 us -> 15 us  [swap(): return lax.ppermute(x, names, [(k, k ^ bit) for k in range(count)])]
  transfers between devices with their start and end apart: 15 -> 15, of which waited for: 5 -> 5; matrix products, arithmetic and copies ran while one was open for 0% -> 0% of each run, Pallas kernels for 41% -> 36%
where the time goes in v3:
time: 58.4 us; the launch traced here: 58.2 us
  Pallas kernels  36.1 us (62%)
  starting transfers between devices  15 us (26%)
  waiting for transfers between devices  6.27 us (11%)
  between operations  0.83 us (1%)
    pallas_call x13, Pallas kernels, call(): pl.pallas_call(kernel, in_specs=specs or [vmem()] * len(args), out_specs=...  36.1 us
    ppermute x15, starting transfers between devices, swap(): return lax.ppermute(x, names, [(k, k ^ bit) for k in range(count)])  15 us
    ppermute x15, waiting for transfers between devices, swap(): return lax.ppermute(x, names, [(k, k ^ bit) for k in range(count)])  6.27 us
  transfers between devices with their start and end apart: 15, of which 5 were waited for; matrix products, arithmetic and copies ran while one was open for 0% of the time, Pallas kernels for 36%

profile of v3, /device:TPU:0, one launch (start us, length us, event | category | flops | bytes accessed | tf_op | source)
XLA Modules:
  0.0 58.2 jit_solution(14537653089574802990)
XLA Ops:
  0.6 0.0 copy-start
  0.6 0.0 copy-start.1
  0.7 10.0 %step_maps.1 = (f32[4,8,256,256]{3,2,1,0:T(8,128)S(1)}, bf16[4,8,256,256]{3,2,1,0:T(8,128)(2,1)S(1)}, f32[4,8,256,128]{3,2,1,0:T(8,128)S(1)}, f32[32,256]{1,0:T(...) custom-call(f32[1,256]{1,0:T(1,128)} %bitcast.13, f32[32,256]{1,0:T(8,128)} %decay_ref.1, ...), custom_call_target="tpu_custom_call" | custom-call | flops 10000000000 | tf_op jit(solution)/shard_map/step_maps/pallas_call | solution.py:472
  10.7 0.5 collective-permute-start
  11.2 3.5 %collective-permute-start.4 = (f32[256,256]{1,0:T(8,128)S(1)}, f32[256,256]{1,0:T(8,128)S(1)}, u32[]{:S(2)}, u32[]{:S(2)}) collective-permute-start(f32[256,256]{1,0:T(8,128)S(1)} %get-tuple-element.44.own_map_ref.refs_0_), channel_id=1, source_target_pairs={{0,6},{1,7},{2,4},{3,5},{4,2},{5,3},{6,0},{7,1},{8,14},{9,15},{10,... | collective-permute-start | bytes 786440 | tf_op jit(solution)/shard_map/ppermute | solution.py:541
  14.7 0.5 collective-permute-start.3
  15.2 0.1 collective-permute-start.2
  15.4 0.0 copy-done.3
  15.4 0.0 copy-done.4
  15.4 0.0 copy-done.5
  15.4 9.9 %step_noises.1 = (f32[32,256]{1,0:T(8,128)S(1)}, f32[4,272,256]{2,1,0:T(8,128)S(1)}, f32[136,256]{1,0:T(8,128)S(1)}) custom-call(f32[1,256]{1,0:T(1,128)S(1)} %bitcast.10, f32[32,256]{1,0:T(8,128)S(1)} %copy-done.3, bf16[4,8,256,256]{3,2,1,0:T(8,128)(2,1)S(1)} %get-tuple-element.45.e_ref, f32[4,8,256,128]{3,2,1,0:T(8,128)S(1)} %get-tuple-element.46.dcol_ref, ...), custom_call_target="tpu_custom_call" | custom-call | flops 1000000000 | tf_op jit(solution)/shard_map/step_noises/pallas_call | solution.py:472
  25.3 0.1 collective-permute-start.1
  25.4 1.3 %collective-permute-done.1.other_ref.refs_8_ = f32[136,256]{1,0:T(8,128)S(1)} collective-permute-done((f32[136,256]{1,0:T(8,128)S(1)}, f32[136,256]{1,0:T(8,128)S(1)}, u32[]{:S(2)}, u32[]{:S(2)}) %collective-permute-start.1) | collective-permute-done | bytes 139296 | tf_op jit(solution)/shard_map/ppermute | solution.py:541
  26.7 0.0 collective-permute-done.other_map_ref.refs_1_
  26.7 0.5 core_noises.1.token_ref.refs_0_
  27.2 2.6 %collective-permute-start.11 = (f32[136,256]{1,0:T(8,128)S(1)}, f32[136,256]{1,0:T(8,128)S(1)}, u32[]{:S(2)}, u32[]{:S(2)}) collective-permute-start(f32[136,256]{1,0:T(8,128)S(1)} %core_noises.1.token_ref.refs_0_), channel_id=1, source_target_pairs={{0,6},{1,7},{2,4},{3,5},{4,2},{5,3},{6,0},{7,1},{8,14},{9,15},{10,... | collective-permute-start | bytes 417800 | tf_op jit(solution)/shard_map/ppermute | solution.py:541
  29.8 0.5 collective-permute-start.10
  30.3 0.0 collective-permute-done.4.refs_6_
  30.3 0.0 collective-permute-done.3.refs_4_
  30.3 0.0 collective-permute-done.2.refs_2_
  30.3 0.1 collective-permute-start.5
  30.4 0.5 collective-permute-start.6
  30.9 0.1 collective-permute-start.7
  31.0 0.9 %turn.4 = (bf16[8,256,256]{2,1,0:T(8,128)(2,1)S(1)}, bf16[8,256,256]{2,1,0:T(8,128)(2,1)S(1)}, f32[8,256]{1,0:T(8,128)S(1)}) custom-call(f32[4,8,256,256]{3,2,1,0:T(8,128)S(1)} %get-tuple-element.42.g_ref, f32[32,256]{1,0:T(8,128)S(1)} %get-tuple-element.43.delta_ref, f32[136,256]{1,0:T(8,128)S(1)} %core_noises.1.token_ref.refs_0_), custom_call_target="tpu_custom_call" | custom-call | flops 4000000000 | tf_op jit(solution)/shard_map/turn/pallas_call | solution.py:472
  31.9 0.0 collective-permute-done.5.refs_3_
  31.9 0.5 collective-permute-start.9
  32.4 0.0 collective-permute-done.6.refs_5_
  32.4 0.2 collective-permute-done.7.refs_7_
  32.7 1.6 %plane_maps.1 = (f32[3,256,256]{2,1,0:T(8,128)S(1)}, bf16[3,256,256]{2,1,0:T(8,128)(2,1)S(1)}, f32[3,256,128]{2,1,0:T(8,128)S(1)}, f32[8,256]{1,0:T(8,128)S(1)},...) custom-call(f32[256,256]{1,0:T(8,128)S(1)} %get-tuple-element.44.own_map_ref.refs_0_, ...), custom_call_target="tpu_custom_call" | custom-call | flops 1000000000 | tf_op jit(solution)/shard_map/plane_maps/pallas_call | solution.py:472
  34.3 1.6 %collective-permute-start.8 = (f32[128,256]{1,0:T(8,128)S(1)}, f32[128,256]{1,0:T(8,128)S(1)}, u32[]{:S(2)}, u32[]{:S(2)}) collective-permute-start(f32[128,256]{1,0:T(8,128)S(1)} %get-tuple-element.56), channel_id=1, source_target_pairs={{0,8},{1,9},{2,10},{3,11},{4,12},{5,13},{6,14},{7,15},{8,0},{9,1},... | collective-permute-start | bytes 393224 | tf_op jit(solution)/shard_map/ppermute | solution.py:541
  35.9 0.9 %turn.5 = (bf16[8,256,256]{2,1,0:T(8,128)(2,1)S(1)}, bf16[8,256,256]{2,1,0:T(8,128)(2,1)S(1)}, f32[8,256]{1,0:T(8,128)S(1)}) custom-call(f32[4,8,256,256]{3,2,1,0:T(8,128)S(1)} %get-tuple-element.42.g_ref, f32[32,256]{1,0:T(8,128)S(1)} %get-tuple-element.43.delta_ref, f32[256,256]{1,0:T(8,128)S(1)} %get-tuple-element.54.token_ref.own_map_ref), custom_call_target="tpu_custom_call" | custom-call | flops 4000000000 | tf_op jit(solution)/shard_map/turn/pallas_call | solution.py:472
  36.9 0.0 collective-permute-done.11.refs_3_
  36.9 0.0 collective-permute-done.10.refs_2_
  36.9 1.1 %collective-permute-done.9.refs_1_ = f32[136,256]{1,0:T(8,128)S(1)} collective-permute-done((f32[136,256]{1,0:T(8,128)S(1)}, f32[136,256]{1,0:T(8,128)S(1)}, u32[]{:S(2)}, u32[]{:S(2)}) %collective-permute-start.9) | collective-permute-done | bytes 139296 | tf_op jit(solution)/shard_map/ppermute | solution.py:541
  38.0 1.5 %plane_noises.1 = (f32[136,256]{1,0:T(8,128)S(1)}, f32[3,272,256]{2,1,0:T(8,128)S(1)}) custom-call(f32[136,256]{1,0:T(8,128)S(1)} %core_noises.1.token_ref.refs_0_, f32[136,256]{1,0:T(8,128)S(1)} %collective-permute-done.9.refs_1_, f32[136,256]{1,0:T(8,128)S(1)} %collective-permute-done.10.refs_2_, f32[136,256]{1,0:T(8,128)S(1)} %collective-permute-done.11.refs_3_, ...), custom_call_target="tpu_custom_call" | custom-call | flops 1000000000 | tf_op jit(solution)/shard_map/plane_noises/pallas_call | solution.py:472
  39.5 1.6 %collective-permute-start.13 = (f32[136,256]{1,0:T(8,128)S(1)}, f32[136,256]{1,0:T(8,128)S(1)}, u32[]{:S(2)}, u32[]{:S(2)}) collective-permute-start(f32[136,256]{1,0:T(8,128)S(1)} %get-tuple-element.64.token_ref.own_ref), channel_id=1, source_target_pairs={{0,8},{1,9},{2,10},{3,11},{4,12},{5,13},{6,14},{7,15},{8,0},{9,1},... | collective-permute-start | bytes 417800 | tf_op jit(solution)/shard_map/ppermute | solution.py:541
  41.1 1.1 %inner.1.inner_ref = f32[528,256]{1,0:T(8,128)S(1)} custom-call(f32[3,256,256]{2,1,0:T(8,128)S(1)} %get-tuple-element.67.maps_ref, f32[3,272,256]{2,1,0:T(8,128)S(1)} %get-tuple-element.68.noises_ref), custom_call_target="tpu_custom_call" | custom-call | flops 1000000000 | tf_op jit(solution)/shard_map/inner/pallas_call | solution.py:472
  42.3 0.0 collective-permute-done.8.r_ref.refs_0_
  42.3 0.1 collective-permute-start.12
  42.3 0.9 %turn.6 = (bf16[8,256,256]{2,1,0:T(8,128)(2,1)S(1)}, bf16[8,256,256]{2,1,0:T(8,128)(2,1)S(1)}, f32[8,256]{1,0:T(8,128)S(1)}) custom-call(f32[4,8,256,256]{3,2,1,0:T(8,128)S(1)} %get-tuple-element.42.g_ref, f32[32,256]{1,0:T(8,128)S(1)} %get-tuple-element.43.delta_ref, f32[136,256]{1,0:T(8,128)S(1)} %get-tuple-element.64.token_ref.own_ref), custom_call_target="tpu_custom_call" | custom-call | flops 4000000000 | tf_op jit(solution)/shard_map/turn/pallas_call | solution.py:472
  43.2 1.5 %collective-permute-done.13.other_ref.refs_2_ = f32[136,256]{1,0:T(8,128)S(1)} collective-permute-done((f32[136,256]{1,0:T(8,128)S(1)}, f32[136,256]{1,0:T(8,128)S(1)}, u32[]{:S(2)}, u32[]{:S(2)}) %collective-permute-start.13) | collective-permute-done | bytes 139296 | tf_op jit(solution)/shard_map/ppermute | solution.py:541
  44.8 0.0 collective-permute-done.12.x_ref.refs_1_
  44.8 0.5 level.1.token_ref
  45.3 2.7 %collective-permute-start.14 = (f32[136,256]{1,0:T(8,128)S(1)}, f32[136,256]{1,0:T(8,128)S(1)}, u32[]{:S(2)}, u32[]{:S(2)}) collective-permute-start(f32[136,256]{1,0:T(8,128)S(1)} %level.1.token_ref), channel_id=1, source_target_pairs={{0,16},{1,17},{2,18},{3,19},{4,20},{5,21},{6,22},{7,23},{8,24},{9,... | collective-permute-start | bytes 417800 | tf_op jit(solution)/shard_map/ppermute | solution.py:541
  47.9 0.9 %turn.7 = (bf16[8,256,256]{2,1,0:T(8,128)(2,1)S(1)}, bf16[8,256,256]{2,1,0:T(8,128)(2,1)S(1)}, f32[8,256]{1,0:T(8,128)S(1)}) custom-call(f32[4,8,256,256]{3,2,1,0:T(8,128)S(1)} %get-tuple-element.42.g_ref, f32[32,256]{1,0:T(8,128)S(1)} %get-tuple-element.43.delta_ref, f32[136,256]{1,0:T(8,128)S(1)} %level.1.token_ref), custom_call_target="tpu_custom_call" | custom-call | flops 4000000000 | tf_op jit(solution)/shard_map/turn/pallas_call | solution.py:472
  48.8 3.0 %place.1 = (f32[4,528,256]{2,1,0:T(8,128)S(1)}, bf16[4,256,256]{2,1,0:T(8,128)(2,1)S(1)}, f32[4,256,128]{2,1,0:T(8,128)S(1)}, f32[4,8,256]{2,1,0:T(8,128)S(1)}) custom-call(f32[6,256,256]{2,1,0:T(8,128)S(1)} %get-tuple-element.48.maps_ref.subs_ref, f32[4,272,256]{2,1,0:T(8,128)S(1)} %get-tuple-element.77.sub_noises_ref, f32[528,256]{1,0:T(8,128)S(1)} %inner.1.inner_ref, ...), custom_call_target="tpu_custom_call" | custom-call | flops 100000 | tf_op jit(solution)/shard_map/place/pallas_call | solution.py:472
  51.9 2.0 %collective-permute-done.14.refs_18_ = f32[136,256]{1,0:T(8,128)S(1)} collective-permute-done((f32[136,256]{1,0:T(8,128)S(1)}, f32[136,256]{1,0:T(8,128)S(1)}, u32[]{:S(2)}, u32[]{:S(2)}) %collective-permute-start.14) | collective-permute-done | bytes 139296 | tf_op jit(solution)/shard_map/ppermute | solution.py:541
  53.8 4.4 %finish.1 = (f32[32,256]{1,0:T(8,128)}, f32[32,256]{1,0:T(8,128)}) custom-call(bf16[8,256,256]{2,1,0:T(8,128)(2,1)S(1)} %get-tuple-element.50.refs_0_, bf16[8,256,256]{2,1,0:T(8,128)(2,1)S(1)} %get-tuple-element.55.refs_1_, bf16[8,256,256]{2,1,0:T(8,128)(2,1)S(1)} %get-tuple-element.65.refs_2_, bf16[8,256,256]{2,1,0:T(8,128)(2,1)S(1)} %get-tuple-element.70.refs_3_, ...), custom_call_target="tpu_custom_call" | custom-call | flops 1000000000 | tf_op jit(solution)/shard_map/finish/pallas_call | solution.py:472
  (7 shorter events, 0.0 us)
Async XLA Ops:
  0.6 14.8 %copy-start = (bf16[32,64,256]{2,1,0:T(8,128)(2,1)S(1)}, bf16[32,64,256]{2,1,0:T(8,128)(2,1)}, u32[]{:S(2)}) copy-start(bf16[32,64,256]{2,1,0:T(8,128)(2,1)} %param.13) | copy-start | bytes 3145732
  0.6 14.7 %copy-start.1 = (bf16[32,64,256]{2,1,0:T(8,128)(2,1)S(1)}, bf16[32,64,256]{2,1,0:T(8,128)(2,1)}, u32[]{:S(2)}) copy-start(bf16[32,64,256]{2,1,0:T(8,128)(2,1)} %param.14) | copy-start | bytes 3145732
  0.7 14.7 %copy-start.2 = (bf16[256,256]{1,0:T(8,128)(2,1)S(1)}, bf16[256,256]{1,0:T(8,128)(2,1)}, u32[]{:S(2)}) copy-start(bf16[256,256]{1,0:T(8,128)(2,1)} %nf_ref.1) | copy-start | bytes 393220
  0.7 14.7 %copy-start.3 = (f32[32,256]{1,0:T(8,128)S(1)}, f32[32,256]{1,0:T(8,128)}, u32[]{:S(2)}) copy-start(f32[32,256]{1,0:T(8,128)} %decay_ref.1) | copy-start | bytes 98308
  0.7 14.7 %copy-start.4 = (f32[256]{0:T(256)S(1)}, f32[256]{0:T(256)}, u32[]{:S(2)}) copy-start(f32[256]{0:T(256)} %param.10) | copy-start | bytes 3076
  0.7 14.7 %copy-start.5 = (f32[64]{0:T(128)S(1)}, f32[64]{0:T(128)}, u32[]{:S(2)}) copy-start(f32[64]{0:T(128)} %param.16) | copy-start | bytes 772
  10.7 16.0 %collective-permute-start = (f32[256,256]{1,0:T(8,128)S(1)}, f32[256,256]{1,0:T(8,128)S(1)}, u32[]{:S(2)}, u32[]{:S(2)}) collective-permute-start(f32[256,256]{1,0:T(8,128)S(1)} %get-tuple-element.44.own_map_ref.refs_0_), channel_id=1, source_target_pairs={{0,1},{1,0},{2,3},{3,2},{4,5},{5,4},{6,7},{7,6},{8,9},{9,8},{10,11... | collective-permute-start | bytes 786440 | tf_op jit(solution)/shard_map/ppermute | solution.py:541
  11.2 19.1 %collective-permute-start.4 = (f32[256,256]{1,0:T(8,128)S(1)}, f32[256,256]{1,0:T(8,128)S(1)}, u32[]{:S(2)}, u32[]{:S(2)}) collective-permute-start(f32[256,256]{1,0:T(8,128)S(1)} %get-tuple-element.44.own_map_ref.refs_0_), channel_id=1, source_target_pairs={{0,6},{1,7},{2,4},{3,5},{4,2},{5,3},{6,0},{7,1},{8,14},{9,15},{10,... | collective-permute-start | bytes 786440 | tf_op jit(solution)/shard_map/ppermute | solution.py:541
  14.7 15.6 %collective-permute-start.3 = (f32[256,256]{1,0:T(8,128)S(1)}, f32[256,256]{1,0:T(8,128)S(1)}, u32[]{:S(2)}, u32[]{:S(2)}) collective-permute-start(f32[256,256]{1,0:T(8,128)S(1)} %get-tuple-element.44.own_map_ref.refs_0_), channel_id=1, source_target_pairs={{0,4},{1,5},{2,6},{3,7},{4,0},{5,1},{6,2},{7,3},{8,12},{9,13},{10,... | collective-permute-start | bytes 786440 | tf_op jit(solution)/shard_map/ppermute | solution.py:541
  15.2 15.1 %collective-permute-start.2 = (f32[256,256]{1,0:T(8,128)S(1)}, f32[256,256]{1,0:T(8,128)S(1)}, u32[]{:S(2)}, u32[]{:S(2)}) collective-permute-start(f32[256,256]{1,0:T(8,128)S(1)} %get-tuple-element.44.own_map_ref.refs_0_), channel_id=1, source_target_pairs={{0,2},{1,3},{2,0},{3,1},{4,6},{5,7},{6,4},{7,5},{8,10},{9,11},{10,... | collective-permute-start | bytes 786440 | tf_op jit(solution)/shard_map/ppermute | solution.py:541
  25.3 1.4 %collective-permute-start.1 = (f32[136,256]{1,0:T(8,128)S(1)}, f32[136,256]{1,0:T(8,128)S(1)}, u32[]{:S(2)}, u32[]{:S(2)}) collective-permute-start(f32[136,256]{1,0:T(8,128)S(1)} %get-tuple-element.49.own_ref), channel_id=1, source_target_pairs={{0,1},{1,0},{2,3},{3,2},{4,5},{5,4},{6,7},{7,6},{8,9},{9,8},{10,11... | collective-permute-start | bytes 417800 | tf_op jit(solution)/shard_map/ppermute | solution.py:541
  27.2 9.7 %collective-permute-start.11 = (f32[136,256]{1,0:T(8,128)S(1)}, f32[136,256]{1,0:T(8,128)S(1)}, u32[]{:S(2)}, u32[]{:S(2)}) collective-permute-start(f32[136,256]{1,0:T(8,128)S(1)} %core_noises.1.token_ref.refs_0_), channel_id=1, source_target_pairs={{0,6},{1,7},{2,4},{3,5},{4,2},{5,3},{6,0},{7,1},{8,14},{9,15},{10,... | collective-permute-start | bytes 417800 | tf_op jit(solution)/shard_map/ppermute | solution.py:541
  29.8 7.1 %collective-permute-start.10 = (f32[136,256]{1,0:T(8,128)S(1)}, f32[136,256]{1,0:T(8,128)S(1)}, u32[]{:S(2)}, u32[]{:S(2)}) collective-permute-start(f32[136,256]{1,0:T(8,128)S(1)} %core_noises.1.token_ref.refs_0_), channel_id=1, source_target_pairs={{0,4},{1,5},{2,6},{3,7},{4,0},{5,1},{6,2},{7,3},{8,12},{9,13},{10,... | collective-permute-start | bytes 417800 | tf_op jit(solution)/shard_map/ppermute | solution.py:541
  30.3 1.6 %collective-permute-start.5 = (f32[256,256]{1,0:T(8,128)S(1)}, f32[256,256]{1,0:T(8,128)S(1)}, u32[]{:S(2)}, u32[]{:S(2)}) collective-permute-start(f32[256,256]{1,0:T(8,128)S(1)} %collective-permute-done.2.refs_2_), channel_id=1, source_target_pairs={{0,1},{1,0},{2,3},{3,2},{4,5},{5,4},{6,7},{7,6},{8,9},{9,8},{10,11... | collective-permute-start | bytes 786440 | tf_op jit(solution)/shard_map/ppermute | solution.py:541
  30.4 2.0 %collective-permute-start.6 = (f32[256,256]{1,0:T(8,128)S(1)}, f32[256,256]{1,0:T(8,128)S(1)}, u32[]{:S(2)}, u32[]{:S(2)}) collective-permute-start(f32[256,256]{1,0:T(8,128)S(1)} %collective-permute-done.3.refs_4_), channel_id=1, source_target_pairs={{0,1},{1,0},{2,3},{3,2},{4,5},{5,4},{6,7},{7,6},{8,9},{9,8},{10,11... | collective-permute-start | bytes 786440 | tf_op jit(solution)/shard_map/ppermute | solution.py:541
  30.9 1.8 %collective-permute-start.7 = (f32[256,256]{1,0:T(8,128)S(1)}, f32[256,256]{1,0:T(8,128)S(1)}, u32[]{:S(2)}, u32[]{:S(2)}) collective-permute-start(f32[256,256]{1,0:T(8,128)S(1)} %collective-permute-done.4.refs_6_), channel_id=1, source_target_pairs={{0,1},{1,0},{2,3},{3,2},{4,5},{5,4},{6,7},{7,6},{8,9},{9,8},{10,11... | collective-permute-start | bytes 786440 | tf_op jit(solution)/shard_map/ppermute | solution.py:541
  31.9 6.1 %collective-permute-start.9 = (f32[136,256]{1,0:T(8,128)S(1)}, f32[136,256]{1,0:T(8,128)S(1)}, u32[]{:S(2)}, u32[]{:S(2)}) collective-permute-start(f32[136,256]{1,0:T(8,128)S(1)} %core_noises.1.token_ref.refs_0_), channel_id=1, source_target_pairs={{0,2},{1,3},{2,0},{3,1},{4,6},{5,7},{6,4},{7,5},{8,10},{9,11},{10,... | collective-permute-start | bytes 417800 | tf_op jit(solution)/shard_map/ppermute | solution.py:541
  34.3 8.0 %collective-permute-start.8 = (f32[128,256]{1,0:T(8,128)S(1)}, f32[128,256]{1,0:T(8,128)S(1)}, u32[]{:S(2)}, u32[]{:S(2)}) collective-permute-start(f32[128,256]{1,0:T(8,128)S(1)} %get-tuple-element.56), channel_id=1, source_target_pairs={{0,8},{1,9},{2,10},{3,11},{4,12},{5,13},{6,14},{7,15},{8,0},{9,1},... | collective-permute-start | bytes 393224 | tf_op jit(solution)/shard_map/ppermute | solution.py:541
  39.5 5.3 %collective-permute-start.13 = (f32[136,256]{1,0:T(8,128)S(1)}, f32[136,256]{1,0:T(8,128)S(1)}, u32[]{:S(2)}, u32[]{:S(2)}) collective-permute-start(f32[136,256]{1,0:T(8,128)S(1)} %get-tuple-element.64.token_ref.own_ref), channel_id=1, source_target_pairs={{0,8},{1,9},{2,10},{3,11},{4,12},{5,13},{6,14},{7,15},{8,0},{9,1},... | collective-permute-start | bytes 417800 | tf_op jit(solution)/shard_map/ppermute | solution.py:541
  42.3 2.5 %collective-permute-start.12 = (f32[128,256]{1,0:T(8,128)S(1)}, f32[128,256]{1,0:T(8,128)S(1)}, u32[]{:S(2)}, u32[]{:S(2)}) collective-permute-start(f32[128,256]{1,0:T(8,128)S(1)} %collective-permute-done.8.r_ref.refs_0_), channel_id=1, source_target_pairs={{0,1},{1,0},{2,3},{3,2},{4,5},{5,4},{6,7},{7,6},{8,9},{9,8},{10,11... | collective-permute-start | bytes 393224 | tf_op jit(solution)/shard_map/ppermute | solution.py:541
  45.3 8.6 %collective-permute-start.14 = (f32[136,256]{1,0:T(8,128)S(1)}, f32[136,256]{1,0:T(8,128)S(1)}, u32[]{:S(2)}, u32[]{:S(2)}) collective-permute-start(f32[136,256]{1,0:T(8,128)S(1)} %level.1.token_ref), channel_id=1, source_target_pairs={{0,16},{1,17},{2,18},{3,19},{4,20},{5,21},{6,22},{7,23},{8,24},{9,... | collective-permute-start | bytes 417800 | tf_op jit(solution)/shard_map/ppermute | solution.py:541

commit v4 on v3

v4 whole, which is shorter than its diff:
```python
import functools

import jax
import jax.numpy as jnp
from jax import lax
from jax.experimental import pallas as pl
from jax.experimental.pallas import tpu as pltpu
from jax.sharding import PartitionSpec as P

f32, bf16 = jnp.float32, jnp.bfloat16
PLANE = 8


def nn(a, b):
    return jnp.dot(a, b, preferred_element_type=f32)


def nt(a, b):
    return lax.dot_general(a, b, (((1,), (1,)), ((), ())), preferred_element_type=f32)


def halves(x):
    high = x.astype(bf16)
    return high, (x - high.astype(f32)).astype(bf16)


def times(late, early):
    (lh, ll), (eh, el) = late, early
    return nn(lh, eh) + (nn(ll, eh) + nn(lh, el))


def advance(late, noise, shift):
    n = noise.shape[1]
    lh, ll = late
    xh, xl = halves(jnp.concatenate([times(late, halves(noise)), shift], axis=0))
    out = nt(xh, lh) + (nt(xl, lh) + nt(xh, ll))
    return out[:n], out[n:]


def wide(col):
    return jnp.concatenate([col, col], axis=1)


def apart(late):
    row = diag_row(late)
    return row, spread(row), jnp.where(eye_mask(late.shape[0]), 0.0, late).astype(bf16)


def conjugate(late, noise):
    row, col, rest = late
    x = wide(col) * noise + nn(rest, noise.astype(bf16))
    return x * row + nt(x.astype(bf16), rest)


def through(late, shift):
    return row_of(jnp.sum(late * shift, axis=1, keepdims=True))


def joined(early, late):
    parts = halves(late[0])
    noise, shift = advance(parts, early[1], early[2])
    return times(parts, halves(early[0])), noise + late[1], shift + late[2]


def eye_mask(n):
    return lax.broadcasted_iota(jnp.int32, (n, n), 0) == lax.broadcasted_iota(jnp.int32, (n, n), 1)


def column(row):
    n = row.shape[1]
    out = []
    for k in range(0, n, 128):
        m = min(128, n - k)
        out.append(jnp.sum(jnp.where(eye_mask(m), row[:, k:k + m], 0.0), axis=1, keepdims=True))
    return out[0] if len(out) == 1 else jnp.concatenate(out, axis=0)


def spread(row):
    n = row.shape[1]
    return jnp.concatenate([jnp.broadcast_to(row[:, k:k + 128], (128, 128)).T for k in range(0, n, 128)], axis=0)


def row_of(col):
    n = col.shape[0]
    out = [jnp.sum(jnp.where(eye_mask(128), col[k:k + 128], 0.0), axis=0, keepdims=True) for k in range(0, n, 128)]
    return jnp.concatenate(out, axis=1)


def diag_row(x):
    n = x.shape[1]
    out = [jnp.sum(jnp.where(eye_mask(128), x[k:k + 128, k:k + 128], 0.0), axis=0, keepdims=True)
           for k in range(0, n, 128)]
    return jnp.concatenate(out, axis=1)


def rows16(row):
    return jnp.broadcast_to(row, (16, row.shape[1]))


def pack(noise, shift):
    n = noise.shape[1]
    h = n // 2
    lower = lax.broadcasted_iota(jnp.int32, (h, h), 0) >= lax.broadcasted_iota(jnp.int32, (h, h), 1)
    a, b, c = noise[:h, :h], noise[:h, h:], noise[h:, h:]
    body = jnp.concatenate([jnp.where(lower, a, c), b], axis=1)
    extra = jnp.concatenate([jnp.zeros((1, h), f32), diag_row(noise)[:, h:]], axis=1)
    return jnp.concatenate([body, shift[0:1], extra, jnp.zeros((14, n), f32)], axis=0)


def unpack(x):
    n = x.shape[1]
    h = n // 2
    i = lax.broadcasted_iota(jnp.int32, (h, h), 0)
    j = lax.broadcasted_iota(jnp.int32, (h, h), 1)
    body, b = x[:h, :h], x[:h, h:]
    turned = body.T
    a = jnp.where(i >= j, body, turned)
    c = jnp.where(i == j, x[h + 1:h + 2, h:], jnp.where(i < j, body, turned))
    noise = jnp.concatenate([jnp.concatenate([a, b], axis=1), jnp.concatenate([b.T, c], axis=1)], axis=0)
    return noise, x[h:h + 1]


def rank_of(axes):
    rank = 0
    for name, size in axes:
        rank = rank * size + lax.axis_index(name)
    return rank


def bit_of(rank, bit):
    return (rank // bit) % 2


def put_half(ref, total_ref, upper):
    rows = ref.shape[0]
    ref[...] = jnp.where(upper, total_ref[rows:], total_ref[:rows])


def put_out(ref, total_ref, upper):
    if ref.shape[0] == total_ref.shape[0]:
        ref[...] = total_ref[...]
    else:
        put_half(ref, total_ref, upper)


def whole(upper, mine_ref, others_ref):
    mine, others = mine_ref[...], others_ref[...]
    return jnp.concatenate([jnp.where(upper, others, mine), jnp.where(upper, mine, others)], axis=0)


def identity(n):
    return jnp.where(eye_mask(n), 1.0, 0.0), jnp.zeros((n, n), f32), jnp.zeros((16, n), f32)


def maps_kernel(subs, decay_hbm, coup_hbm, omap_hbm, gain_hbm, seen_hbm,
                g_ref, e_ref, dcol_ref, delta_ref, shift_ref, maps_ref, total_ref,
                decay_ref, coup_ref, omap_ref, gain_ref, seen_ref, small_sem, sem, g_s, part_s, eh_s, row_s):
    n = decay_ref.shape[1]
    steps = coup_ref.shape[1]
    small = [pltpu.make_async_copy(x, y, small_sem.at[k]) for k, (x, y) in enumerate(
        [(decay_hbm, decay_ref), (seen_hbm, seen_ref)])]

    def chunk(j):
        return [pltpu.make_async_copy(x.at[:, j], y.at[:, j], sem.at[k, j]) for k, (x, y) in enumerate(
            [(coup_hbm, coup_ref), (omap_hbm, omap_ref), (gain_hbm, gain_ref)])]

    for c in small + chunk(0):
        c.start()
    for j in range(1, steps):
        for c in chunk(j):
            c.start()
    for c in small:
        c.wait()

    def step(j, first):
        for c in chunk(j):
            c.wait()
        all_subs = range(subs)
        rows = [decay_ref[pl.ds(s * steps + j, 1), :] for s in all_subs]
        obs_f = [(omap_ref[s, j].astype(f32) * rows[s] + nn(omap_ref[s, j], coup_ref[s, j])).astype(bf16)
                 for s in all_subs]

        def build(s):
            t = s * steps + j
            gain = gain_ref[s, j]
            e = coup_ref[s, j].astype(f32) - nn(gain.T, obs_f[s])
            e_h = e.astype(bf16)
            e_ref[s, j] = e_h
            eh_s[s] = e_h
            col = spread(rows[s])
            dcol_ref[s, j] = col
            shift = jnp.sum(gain.astype(f32) * column(seen_ref[pl.ds(t, 1), :]), axis=0, keepdims=True)
            if first:
                g_s[s] = e
                g_ref[s, j] = e
                delta, b_new = rows[s], shift
            else:
                delta = row_s[s, 0:1, :]
                b = row_s[s, 1:2, :]
                part_s[s] = wide(col) * g_s[s] + e * delta
                delta = delta * rows[s]
                b_new = rows[s] * b + row_of(jnp.sum(e * b, axis=1, keepdims=True)) + shift
            shift_ref[pl.ds(t, 1), :] = b_new
            delta_ref[pl.ds(t, 1), :] = delta
            row_s[s, 0:1, :] = delta
            row_s[s, 1:2, :] = b_new

        def follow(s):
            if not first:
                g_new = part_s[s] + nn(eh_s[s], g_s[s].astype(bf16))
                g_s[s] = g_new
                g_ref[s, j] = g_new

        build(0)
        build(1)
        follow(0)
        build(2)
        follow(1)
        build(3)
        follow(2)
        follow(3)

    step(0, True)
    lax.fori_loop(1, steps, lambda j, c: (step(j, False), c)[1], 0)

    eye = eye_mask(n)
    maps = [g_ref[s, steps - 1] + jnp.where(eye, delta_ref[(s + 1) * steps - 1:(s + 1) * steps, :], 0.0)
            for s in range(subs)]
    for s in range(subs):
        maps_ref[s] = maps[s]
    parts = [halves(m) for m in maps]
    low, high = times(parts[1], parts[0]), times(parts[3], parts[2])
    maps_ref[subs] = low
    maps_ref[subs + 1] = high
    total_ref[...] = times(halves(high), halves(low))


def shapes_kernel(omap_ref, gain_ref, nf_ref, _, shaped_ref, seen_s):
    subs, steps, m = omap_ref.shape[:3]
    nf = nf_ref[...]

    def see(j, carry):
        seen_s[j] = nn(jnp.concatenate([omap_ref[s, j] for s in range(subs)], axis=0), nf).astype(bf16)
        return carry

    def shape_step(j, carry):
        shaped = [(nf.astype(f32) - nn(gain_ref[s, j].T, seen_s[j, s * m:(s + 1) * m])).astype(bf16) for s in range(subs)]
        for s in range(subs):
            shaped_ref[s, j] = shaped[s]
        return carry

    lax.fori_loop(0, steps, see, 0, unroll=4)
    lax.fori_loop(0, steps, shape_step, 0, unroll=4)


def noises_kernel(subs, decay_ref, e_ref, dcol_ref, shaped_ref, gain_ref, var_ref, shift_ref,
                  maps_ref, _, diag_ref, noises_ref, total_ref, q_s):
    n = e_ref.shape[-1]
    steps = e_ref.shape[1]
    var_col = column(var_ref[...])
    all_subs = range(subs)

    def noise(s, j):
        shaped, gain = shaped_ref[s, j], gain_ref[s, j]
        return nt(shaped, shaped) + nn(gain.T, (gain.astype(f32) * var_col).astype(bf16))

    def first_half(s, j, q):
        return wide(dcol_ref[s, j]) * q + nn(e_ref[s, j], q.astype(bf16))

    def second_half(s, j, x):
        return x * decay_ref[pl.ds(s * steps + j, 1), :] + (nt(x.astype(bf16), e_ref[s, j]) + noise(s, j))

    def step(j, carry):
        x = [first_half(s, j, q_s[s]) for s in all_subs]
        for s in all_subs:
            q_new = second_half(s, j, x[s])
            q_s[s] = q_new
            diag_ref[pl.ds(s * steps + j, 1), :] = diag_row(q_new)
        return carry

    for s in all_subs:
        q_s[s] = noise(s, 0)

    for s in all_subs:
        diag_ref[pl.ds(s * steps, 1), :] = diag_row(q_s[s])
    lax.fori_loop(1, steps, step, 0)

    shift = [shift_ref[(s + 1) * steps - 1:(s + 1) * steps, :] for s in range(subs)]
    pairs = [(conjugate(apart(maps_ref[s + 1]), q_s[s]) + q_s[s + 1], through(maps_ref[s + 1], shift[s]) + shift[s + 1])
             for s in (0, 2)]
    last = maps_ref[subs + 1]
    total_ref[...] = pack(conjugate(apart(last), pairs[0][0]) + pairs[1][0], through(last, pairs[0][1]) + pairs[1][1])
    for s in range(subs):
        noises_ref[s, 0:n, :] = q_s[s]
        noises_ref[s, n:, :] = rows16(shift[s])


def chip_kernel(axes, own_ref, other_ref, _, out_ref):
    upper = rank_of(axes) % 2 == 1
    own, other = own_ref[...], other_ref[...]
    out_ref[...] = times(halves(jnp.where(upper, own, other)), halves(jnp.where(upper, other, own)))


def core_kernel(axes, own_map_ref, other_map_ref, own_ref, other_ref, out_ref, half_ref):
    upper = rank_of(axes) % 2 == 1
    own, other = unpack(own_ref[...]), unpack(other_ref[...])
    late = jnp.where(upper, own_map_ref[...], other_map_ref[...])
    early_noise, early_shift = (jnp.where(upper, a, b) for a, b in zip(other, own))
    late_noise, late_shift = (jnp.where(upper, a, b) for a, b in zip(own, other))
    out_ref[...] = pack(conjugate(apart(late), early_noise) + late_noise, through(late, early_shift) + late_shift)
    put_half(half_ref, out_ref, upper)


def fetch(rank, refs, dst, sem):
    place = (rank % PLANE) // (PLANE // len(refs))
    copies = [pltpu.make_async_copy(r, dst.at[place ^ k], sem.at[k]) for k, r in enumerate(refs)]
    for c in copies:
        c.start()
    for c in copies:
        c.wait()


def plane_maps_kernel(axes, *refs):
    ins, refs = refs[:4], refs[4:]
    core_ref, var_ref, mean_ref, late_ref, rest_ref, col_ref, row_ref, start_ref, total_ref, half_ref, picks_ref, chip_s, sem = refs
    rank = rank_of(axes)
    fetch(rank, ins, chip_s, sem)

    def keep(k, late):
        late_ref[k] = late
        row_ref[k:k + 1, :], col_ref[k], rest_ref[k] = apart(late)

    chips = [chip_s[k] for k in range(4)]
    pairs = [times(halves(chips[2 * k + 1]), halves(chips[2 * k])) for k in range(2)]
    total = times(halves(pairs[1]), halves(pairs[0]))
    first = rank // PLANE == 0
    n = total.shape[0]
    noise = conjugate(apart(total), jnp.where(eye_mask(n), var_ref[...], 0.0))
    start_ref[0:n, :] = jnp.where(first, noise, 0.0)
    start_ref[n:, :] = rows16(jnp.where(first, through(total, mean_ref[...]), 0.0))
    total_ref[...] = jnp.where(first, 0.0, total)
    for k, late in enumerate((chips[1], chips[3], pairs[1])):
        keep(k, late)
    h = half_ref.shape[0]
    half_ref[...] = jnp.where(rank % 2 == 1, total_ref[h:], total_ref[:h])
    picks_ref[0] = pairs[0]
    picks_ref[1] = chip_s[2 * bit_of(rank, 4)]
    picks_ref[2] = core_ref[...]


def plane_noises_kernel(axes, *refs):
    ins, (late_ref, rest_ref, col_ref, row_ref, start_ref, core_ref, out_ref, picks_ref, in_s, total_s, sem) = refs[:7], refs[7:]
    rank = rank_of(axes)
    place = (rank % PLANE) // 2
    rows = total_s.shape[0] // 2
    copies = [pltpu.make_async_copy(ins[0], in_s.at[place], sem.at[0])]
    for k in range(1, 4):
        for other in range(2):
            part = (rank % 2) ^ other
            copies.append(pltpu.make_async_copy(
                ins[2 * k - 1 + other], in_s.at[place ^ k, pl.ds(pl.multiple_of(part * rows, 8), rows)],
                sem.at[2 * k - 1 + other]))
    for c in copies:
        c.start()
    for c in copies:
        c.wait()
    n = late_ref.shape[-1]

    def join(k, early, late):
        noise = conjugate((row_ref[k:k + 1, :], col_ref[k], rest_ref[k]), early[0])
        return noise + late[0], through(late_ref[k], early[1]) + late[1]

    def pick(k, element):
        picks_ref[k, 0:n], picks_ref[k, n:] = element[0], rows16(element[1])

    chips = [unpack(in_s[k]) for k in range(4)]
    pairs = [join(k, chips[2 * k], chips[2 * k + 1]) for k in range(2)]
    noise, shift = join(2, pairs[0], pairs[1])
    total_s[...] = pack(noise + start_ref[0:n, :], shift + start_ref[n:n + 1, :])
    put_out(out_ref, total_s, rank % 2 == 1)
    pick(0, pairs[0])
    pick(1, unpack(in_s[2 * bit_of(rank, 4)]))
    pick(2, unpack(core_ref[...]))


def level_kernel(axes, bit, own_map_ref, own_ref, r_ref, x_ref, other_ref, _, __, *outs):
    *outs, total_s = outs
    rank = rank_of(axes)
    upper, high = rank % 2 == 1, bit_of(rank, bit) == 1
    other_map, own_map = whole(upper, r_ref, x_ref), own_map_ref[...]
    other, own = unpack(other_ref[...]), unpack(own_ref[...])
    late = jnp.where(high, own_map, other_map)
    early_noise, early_shift = (jnp.where(high, a, b) for a, b in zip(other, own))
    late_noise, late_shift = (jnp.where(high, a, b) for a, b in zip(own, other))
    total_s[...] = pack(conjugate(apart(late), early_noise) + late_noise, through(late, early_shift) + late_shift)
    put_out(outs[0], total_s, upper)
    if len(outs) > 1:
        outs[1][...] = times(halves(late), halves(jnp.where(high, other_map, own_map)))
        put_half(outs[2], outs[1], upper)


def place_kernel(axes, subs_ref, sub_noises_ref, maps_ref, noises_ref, out_ref, rest_ref, col_ref, row_ref):
    rank = rank_of(axes)
    n = out_ref.shape[2]
    one = identity(n)
    parts = []
    for k, bit in enumerate((4, 2, 1)):
        element = (maps_ref[k], noises_ref[k, 0:n], noises_ref[k, n:])
        parts.append(tuple(jnp.where(bit_of(rank, bit) == 1, a, b) for a, b in zip(element, one)))

    def put(s, element):
        em, en, es = element
        out_ref[s, 0:n, :], out_ref[s, n:2 * n, :], out_ref[s, 2 * n:, :] = em, en, es

    def sub(s, carry):
        before = out_ref[s, 0:n, :], out_ref[s, n:2 * n, :], out_ref[s, 2 * n:, :]
        put(s + 1, joined(before, (subs_ref[s], sub_noises_ref[s, 0:n, :], sub_noises_ref[s, n:, :])))
        return carry

    def split(s, carry):
        row_ref[s, 0:1, :], col_ref[s], rest_ref[s] = apart(out_ref[s, 0:n, :])
        return carry

    put(0, joined(parts[0], joined(parts[1], parts[2])))
    lax.fori_loop(0, out_ref.shape[0] - 1, sub, 0)
    lax.fori_loop(0, out_ref.shape[0], split, 0)


def before_kernel(axes, bits, var_ref, mean_ref, *refs):
    map_ref, noise_ref, shift_ref, rest_ref, col_ref, row_ref = refs[-6:]
    rank = rank_of(axes)
    before = identity(map_ref.shape[0])
    for k, bit in enumerate(bits):
        r_ref, x_ref, other_ref = refs[3 * k:3 * k + 3]
        noise, shift = unpack(other_ref[...])
        other = whole(rank % 2 == 1, r_ref, x_ref), noise, rows16(shift)
        new = other if k == 0 else joined(other, before)
        before = tuple(jnp.where(bit_of(rank, bit) == 1, a, b) for a, b in zip(new, before))
    n = map_ref.shape[0]
    start = jnp.zeros((n, n), f32), jnp.where(eye_mask(n), var_ref[...], 0.0), rows16(mean_ref[...])
    before = tuple(jnp.where(rank // PLANE == 0, a, b) for a, b in zip(start, before))
    map_ref[...], noise_ref[...], shift_ref[...] = before
    row_ref[0:1, :], col_ref[...], rest_ref[...] = apart(before[0])


def turn_kernel(sub, g_ref, delta_ref, token_ref, high_ref, low_ref, diag_ref):
    steps, n = high_ref.shape[:2]
    eye = eye_mask(n)

    def step(j, carry):
        turned = g_ref[sub, j].T
        diag_ref[pl.ds(j, 1), :] = delta_ref[pl.ds(sub * steps + j, 1), :] + diag_row(turned)
        high_ref[j], low_ref[j] = halves(jnp.where(eye, 0.0, turned))
        return carry

    lax.fori_loop(0, steps, step, 0, unroll=2)


def finish_kernel(axes, bit, parts, *refs):
    high, low, diag = refs[:parts], refs[parts:2 * parts], refs[2 * parts:3 * parts]
    var_ref, mean_ref, place_ref, rest_ref, col_ref, arow_ref, bmap_ref, bnoise_ref, bshift_ref, brest_ref, bcol_ref, brow_ref, r_ref, x_ref, means_ref, vars_ref, left_s, row_s = refs[3 * parts:]
    n = left_s.shape[-1]
    steps = high[0].shape[0]
    rank = rank_of(axes)
    is_high = bit_of(rank, bit) == 1
    received, moved = unpack(whole(rank % 2 == 1, r_ref, x_ref))
    noise = conjugate((brow_ref[0:1, :], bcol_ref[...], brest_ref[...]), received)
    state = jnp.where(is_high, noise, 0.0) + bnoise_ref[...]
    moved = jnp.where(is_high, through(bmap_ref[...], moved), 0.0) + bshift_ref[0:1, :]
    for s in range(parts):
        p = conjugate((arow_ref[s, 0:1, :], col_ref[s], rest_ref[s]), state) + place_ref[s, n:2 * n, :]
        mean = through(place_ref[s, 0:n, :], moved) + place_ref[s, 2 * n:2 * n + 1, :]
        mh, ml = halves(mean)
        left_s[s, 0:n, :] = p.astype(bf16)
        left_s[s, n:, :] = jnp.concatenate([mh, ml, jnp.zeros((14, n), bf16)], axis=0)
        row_s[s, 0:1, :] = mean
        row_s[s, 1:2, :] = diag_row(p)

    def step(j, carry):
        both = [nn(left_s[s], high[s][j]) for s in range(parts)]
        rest = [nn(left_s[s, n:, :], low[s][j]) for s in range(parts)]
        for s in range(parts):
            t = s * steps + j
            d = diag[s][pl.ds(j, 1), :]
            vars_ref[pl.ds(t, 1), :] = (var_ref[pl.ds(t, 1), :] + d * (d * row_s[s, 1:2, :] + 2.0 * diag_row(both[s]))
                                        + jnp.sum(high[s][j].astype(f32) * both[s][:n], axis=0, keepdims=True))
            means_ref[pl.ds(t, 1), :] = (mean_ref[pl.ds(t, 1), :] + d * row_s[s, 0:1, :]
                                         + both[s][n:n + 1] + (both[s][n + 1:n + 2] + rest[s][0:1]))
        return carry

    lax.fori_loop(0, steps, step, 0)


def vmem():
    return pl.BlockSpec(memory_space=pltpu.VMEM)


def anywhere():
    return pl.BlockSpec(memory_space=pl.ANY)


def shape(*dims, dtype=f32):
    return jax.ShapeDtypeStruct(dims, dtype)


def call(kernel, name, outs, args, specs=None, scratch=(), limit=16, flops=10 ** 5):
    return pl.pallas_call(
        kernel,
        in_specs=specs or [vmem()] * len(args),
        out_specs=[vmem()] * len(outs),
        out_shape=outs,
        scratch_shapes=scratch,
        compiler_params=pltpu.CompilerParams(vmem_limit_bytes=limit * 1024 * 1024),
        cost_estimate=pl.CostEstimate(flops=flops, bytes_accessed=0, transcendentals=0),
        name=name,
    )(*args)


def hbm():
    return pl.BlockSpec(memory_space=pltpu.HBM)


def step_maps(subs, decay, coupling, obs_map, gain, observed):
    T, n = decay.shape
    m = obs_map.shape[1]
    steps = T // subs
    outs = [shape(subs, steps, n, n), shape(subs, steps, n, n, dtype=bf16), shape(subs, steps, n, 128),
            shape(T, n), shape(T, n), shape(subs + 2, n, n), shape(n, n)]
    args = [decay, coupling.reshape(subs, steps, n, n), obs_map.reshape(subs, steps, m, n),
            gain.reshape(subs, steps, m, n), observed]
    scratch = [pltpu.VMEM(x.shape, x.dtype) for x in args]
    args = [pltpu.with_memory_space_constraint(x, pltpu.HBM) for x in args]
    scratch += [pltpu.SemaphoreType.DMA((2,)), pltpu.SemaphoreType.DMA((3, steps)), pltpu.VMEM((subs, n, n), f32),
                pltpu.VMEM((subs, n, n), f32), pltpu.VMEM((subs, n, n), bf16), pltpu.VMEM((subs, 8, n), f32)]
    return call(functools.partial(maps_kernel, subs), "step_maps", outs, args, [hbm()] * len(args), scratch,
                limit=26, flops=10 ** 10)


def step_shapes(subs, obs_map, gain, noise_factor, token):
    T, m, n = obs_map.shape
    steps = T // subs
    return call(shapes_kernel, "step_shapes", [shape(subs, steps, n, n, dtype=bf16)],
                [obs_map.reshape(subs, steps, m, n), gain.reshape(subs, steps, m, n), noise_factor, token],
                [vmem()] * 3 + [anywhere()], [pltpu.VMEM((steps, subs * m, n), bf16)])[0]


def step_noises(subs, decay, e, dcol, shaped, gain, obs_var, shift, maps, token):
    T, n = decay.shape
    m = gain.shape[1]
    args = [decay, e, dcol, shaped, gain.reshape(subs, T // subs, m, n), obs_var.reshape(1, m),
            shift, maps, token]
    return call(functools.partial(noises_kernel, subs), "step_noises",
                [shape(T, n), shape(subs, n + 16, n), shape(n // 2 + 16, n)], args, [vmem()] * 8 + [anywhere()],
                [pltpu.VMEM((subs, n, n), f32)])


def turn(sub, g, delta, token):
    _, steps, n, _ = g.shape
    return call(functools.partial(turn_kernel, sub), "turn",
                [shape(steps, n, n, dtype=bf16), shape(steps, n, n, dtype=bf16), shape(steps, n)],
                [g, delta, token], [vmem()] * 2 + [anywhere()], flops=10 ** 5)


def finish(axes, bit, turned, var, mean, placed, before, r, x):
    parts = len(turned)
    T, n = var.shape
    high, low, diag = zip(*turned)
    return call(functools.partial(finish_kernel, axes, bit, parts), "finish", [shape(T, n)] * 2,
                [*high, *low, *diag, var, mean, *placed, *before, r, x],
                scratch=[pltpu.VMEM((parts, n + 16, n), bf16), pltpu.VMEM((parts, 8, n), f32)])


def per_device(axes, init_mean, init_var, decay, coupling, obs_map, gain, noise_factor, obs_var, observed):
    n = decay.shape[1]
    h = n // 2
    subs = 4
    count = 1
    for _, size in axes:
        count *= size
    names = tuple(name for name, _ in axes)

    def swap(x, bit):
        return lax.ppermute(x, names, [(k, k ^ bit) for k in range(count)])

    bits = []
    bit = PLANE
    while bit < count:
        bits.append(bit)
        bit *= 2

    g, e, dcol, delta, shift, maps, own = step_maps(subs, decay, coupling, obs_map, gain, observed)
    other = swap(own, 1)
    shaped = step_shapes(subs, obs_map, gain, noise_factor, delta)
    (chip_map,) = call(functools.partial(chip_kernel, axes), "chip_maps", [shape(n, n)], [own, other, shaped],
                       [vmem()] * 2 + [anywhere()])
    far = [swap(chip_map, bit) for bit in (2, 4, 6)]
    diag, noises, packed = step_noises(subs, decay, e, dcol, shaped, gain, obs_var, shift, maps, chip_map)
    other_packed = swap(packed, 1)
    chip, chip_half = call(functools.partial(core_kernel, axes), "core_noises", [shape(h + 16, n), shape(h // 2 + 8, n)],
                   [own, other, packed, other_packed])
    chips = [chip] + [v for r in [swap(chip_half, bit) for bit in (2, 4, 6)] for v in (r, swap(r, 1))]
    *far, _ = lax.optimization_barrier((*far, chip))
    *late, total, half, map_picks = call(
        functools.partial(plane_maps_kernel, axes), "plane_maps",
        [shape(3, n, n), shape(3, n, n, dtype=bf16), shape(3, n, 128), shape(8, n), shape(n + 16, n), shape(n, n), shape(h, n), shape(3, n, n)],
        [chip_map, *far, other, init_var.reshape(1, n), init_mean.reshape(1, n)], [anywhere()] * 4 + [vmem()] * 3,
        [pltpu.VMEM((4, n, n), f32), pltpu.SemaphoreType.DMA((4,))])
    size = h + 16 if len(bits) > 1 else h // 2 + 8
    packed, noise_picks = call(
        functools.partial(plane_noises_kernel, axes), "plane_noises",
        [shape(size, n), shape(3, n + 16, n)],
        [*chips, *late, other_packed], [anywhere()] * 7 + [vmem()] * 6,
        [pltpu.VMEM((4, h + 16, n), f32), pltpu.VMEM((h + 16, n), f32), pltpu.SemaphoreType.DMA((7,))])
    placed = call(functools.partial(place_kernel, axes), "place",
                  [shape(subs, 2 * n + 16, n), shape(subs, n, n, dtype=bf16), shape(subs, n, 128), shape(subs, 8, n)],
                  [maps, noises, map_picks, noise_picks])
    turned = [turn(0, g, delta, packed)]
    received = []
    for k, bit in enumerate(bits[:-1]):
        moving = swap(packed, bit)
        r, packed = lax.optimization_barrier((swap(half, bit), packed))
        got = (r, swap(r, 1), moving)
        received += got
        more = k < len(bits) - 2
        size = h + 16 if more else h // 2 + 8
        new = call(functools.partial(level_kernel, axes, bit), "level",
                   [shape(size, n)] + ([shape(n, n), shape(h, n)] if more else []), [total, packed, *got, placed[3], turned[0][2]],
                   [vmem()] * 5 + [anywhere()] * 2, [pltpu.VMEM((h + 16, n), f32)])
        packed = new[0]
        if more:
            total, half = new[1:]
    before = call(functools.partial(before_kernel, axes, bits[:-1]), "before",
                  [shape(n, n), shape(n, n), shape(16, n), shape(n, n, dtype=bf16), shape(n, 128), shape(8, n)],
                  [init_var.reshape(1, n), init_mean.reshape(1, n), *received])
    turned += [turn(k, g, delta, packed) for k in range(1, subs)]
    r, *_ = lax.optimization_barrier((swap(packed, bits[-1]), *before, turned[1][2], turned[2][2]))
    return tuple(finish(axes, bits[-1], turned, diag, shift, placed, before, r, swap(r, 1)))


def solution(mesh):
    axes = tuple((name, mesh.shape[name]) for name in mesh.axis_names)
    time = P(tuple(mesh.axis_names))
    return jax.shard_map(
        functools.partial(per_device, axes),
        mesh=mesh,
        in_specs=(P(), P(), time, time, time, time, P(), P(), time),
        out_specs=(time, time),
        check_vma=False,
    )
```

time: 58.4 us -> 56.3 us (0.964)
  Pallas kernels: 36.1 us -> 34.2 us
    pallas_call x13 -> x15, Pallas kernels: 36.1 us -> 34.2 us  [call(): pl.pallas_call(kernel, in_specs=specs or [vmem()] * len(args), out_specs=...]
    ppermute x15 -> x16, starting transfers between devices: 15 us -> 14.6 us  [swap(): return lax.ppermute(x, names, [(k, k ^ bit) for k in range(count)])]
    ppermute x15 -> x16, waiting for transfers between devices: 6.27 us -> 6.53 us  [swap(): return lax.ppermute(x, names, [(k, k ^ bit) for k in range(count)])]
  transfers between devices with their start and end apart: 15 -> 16, of which waited for: 5 -> 9; matrix products, arithmetic and copies ran while one was open for 0% -> 0% of each run, Pallas kernels for 36% -> 34%
where the time goes in v4:
time: 56.3 us; the launch traced here: 56.2 us
  Pallas kernels  34.2 us (61%)
  starting transfers between devices  14.6 us (26%)
  waiting for transfers between devices  6.53 us (12%)
  between operations  0.81 us (1%)
    pallas_call x15, Pallas kernels, call(): pl.pallas_call(kernel, in_specs=specs or [vmem()] * len(args), out_specs=...  34.2 us
    ppermute x16, starting transfers between devices, swap(): return lax.ppermute(x, names, [(k, k ^ bit) for k in range(count)])  14.6 us
    ppermute x16, waiting for transfers between devices, swap(): return lax.ppermute(x, names, [(k, k ^ bit) for k in range(count)])  6.53 us
  transfers between devices with their start and end apart: 16, of which 9 were waited for; matrix products, arithmetic and copies ran while one was open for 0% of the time, Pallas kernels for 34%

profile of v4, /device:TPU:0, one launch (start us, length us, event | category | flops | bytes accessed | tf_op | source)
XLA Modules:
  0.0 56.2 jit_solution(16754800970475794520)
XLA Ops:
  0.7 9.7 %step_maps.1 = (f32[4,8,256,256]{3,2,1,0:T(8,128)S(1)}, bf16[4,8,256,256]{3,2,1,0:T(8,128)(2,1)S(1)}, f32[4,8,256,128]{3,2,1,0:T(8,128)S(1)}, f32[32,256]{1,0:T(...) custom-call(f32[32,256]{1,0:T(8,128)} %decay_ref.1, ...), custom_call_target="tpu_custom_call" | custom-call | flops 10000000000 | tf_op jit(solution)/shard_map/step_maps/pallas_call | solution.py:507
  10.4 0.5 collective-permute-start
  10.9 0.0 copy-start.6
  10.9 2.1 %step_shapes.1._.shaped_ref = bf16[4,8,256,256]{3,2,1,0:T(8,128)(2,1)S(1)} custom-call(bf16[4,8,64,256]{3,2,1,0:T(8,128)(2,1)S(1)} %bitcast.10, bf16[4,8,64,256]{3,2,1,0:T(8,128)(2,1)S(1)} %bitcast.7, bf16[256,256]{1,0:T(8,128)(2,1)S(1)} %copy-done.2, f32[32,256]{1,0:T(8,128)S(1)} %get-tuple-element.53._.delta_ref), custom_call_target="tpu_custom_call" | custom-call | flops 100000 | tf_op jit(solution)/shard_map/step_shapes/pallas_call | solution.py:507
  13.0 0.0 collective-permute-done.other_ref.other_map_ref.refs_4_
  13.1 0.3 chip_maps.1._.refs_0_
  13.4 3.5 %collective-permute-start.10 = (f32[256,256]{1,0:T(8,128)S(1)}, f32[256,256]{1,0:T(8,128)S(1)}, u32[]{:S(2)}, u32[]{:S(2)}) collective-permute-start(f32[256,256]{1,0:T(8,128)S(1)} %chip_maps.1._.refs_0_), channel_id=1, source_target_pairs={{0,6},{1,7},{2,4},{3,5},{4,2},{5,3},{6,0},{7,1},{8,14},{9,15},{10,... | collective-permute-start | bytes 786440 | tf_op jit(solution)/shard_map/ppermute | solution.py:583
  16.9 0.5 collective-permute-start.9
  17.4 0.1 collective-permute-start.8
  17.6 6.5 %step_noises.1 = (f32[32,256]{1,0:T(8,128)S(1)}, f32[4,272,256]{2,1,0:T(8,128)S(1)}, f32[144,256]{1,0:T(8,128)S(1)}) custom-call(f32[32,256]{1,0:T(8,128)S(1)} %copy-done.3, bf16[4,8,256,256]{3,2,1,0:T(8,128)(2,1)S(1)} %get-tuple-element.55.e_ref, f32[4,8,256,128]{3,2,1,0:T(8,128)S(1)} %get-tuple-element.56.dcol_ref, ...), custom_call_target="tpu_custom_call" | custom-call | flops 100000 | tf_op jit(solution)/shard_map/step_noises/pallas_call | solution.py:507
  24.1 0.1 collective-permute-start.1
  24.2 1.4 %collective-permute-done.1.other_ref.refs_12_ = f32[144,256]{1,0:T(8,128)S(1)} collective-permute-done((f32[144,256]{1,0:T(8,128)S(1)}, f32[144,256]{1,0:T(8,128)S(1)}, u32[]{:S(2)}, u32[]{:S(2)}) %collective-permute-start.1) | collective-permute-done | bytes 147488 | tf_op jit(solution)/shard_map/ppermute | solution.py:583
  25.5 0.5 core_noises.1
  26.0 2.9 %collective-permute-start.6 = (f32[72,256]{1,0:T(8,128)S(1)}, f32[72,256]{1,0:T(8,128)S(1)}, u32[]{:S(2)}, u32[]{:S(2)}) collective-permute-start(f32[72,256]{1,0:T(8,128)S(1)} %get-tuple-element.61), channel_id=1, source_target_pairs={{0,6},{1,7},{2,4},{3,5},{4,2},{5,3},{6,0},{7,1},{8,14},{9,15},{10,... | collective-permute-start | bytes 221192 | tf_op jit(solution)/shard_map/ppermute | solution.py:583
  28.9 0.5 collective-permute-start.4
  29.4 0.0 collective-permute-done.10.refs_3_
  29.4 0.1 collective-permute-start.2
  29.5 0.0 collective-permute-done.9.refs_2_
  29.5 0.2 collective-permute-done.8.refs_1_
  29.8 1.1 %plane_maps.1 = (f32[3,256,256]{2,1,0:T(8,128)S(1)}, bf16[3,256,256]{2,1,0:T(8,128)(2,1)S(1)}, f32[3,256,128]{2,1,0:T(8,128)S(1)}, f32[8,256]{1,0:T(8,128)S(1)},...) custom-call(f32[256,256]{1,0:T(8,128)S(1)} %chip_maps.1._.refs_0_, ...), custom_call_target="tpu_custom_call" | custom-call | flops 100000 | tf_op jit(solution)/shard_map/plane_maps/pallas_call | solution.py:507
  30.9 1.9 %collective-permute-start.11 = (f32[128,256]{1,0:T(8,128)S(1)}, f32[128,256]{1,0:T(8,128)S(1)}, u32[]{:S(2)}, u32[]{:S(2)}) collective-permute-start(f32[128,256]{1,0:T(8,128)S(1)} %get-tuple-element.73), channel_id=1, source_target_pairs={{0,8},{1,9},{2,10},{3,11},{4,12},{5,13},{6,14},{7,15},{8,0},{9,1},... | collective-permute-start | bytes 393224 | tf_op jit(solution)/shard_map/ppermute | solution.py:583
  32.8 0.0 collective-permute-done.6.refs_5_
  32.8 0.0 collective-permute-start.7
  32.8 0.4 collective-permute-done.4.refs_3_
  33.2 0.1 collective-permute-start.5
  33.3 0.4 collective-permute-done.2.refs_1_
  33.7 0.0 collective-permute-start.3
  33.7 0.3 collective-permute-done.7.refs_6_
  34.1 0.5 collective-permute-done.5.refs_4_
  34.5 0.5 collective-permute-done.3.refs_2_
  35.0 1.6 %plane_noises.1 = (f32[144,256]{1,0:T(8,128)S(1)}, f32[3,272,256]{2,1,0:T(8,128)S(1)}) custom-call(f32[144,256]{1,0:T(8,128)S(1)} %get-tuple-element.60.refs_0_, f32[72,256]{1,0:T(8,128)S(1)} %collective-permute-done.2.refs_1_, f32[72,256]{1,0:T(8,128)S(1)} %collective-permute-done.3.refs_2_, f32[72,256]{1,0:T(8,128)S(1)} %collective-permute-done.4.refs_3_, ...), custom_call_target="tpu_custom_call" | custom-call | flops 100000 | tf_op jit(solution)/shard_map/plane_noises/pallas_call | solution.py:507
  36.6 1.6 %collective-permute-start.13 = (f32[144,256]{1,0:T(8,128)S(1)}, f32[144,256]{1,0:T(8,128)S(1)}, u32[]{:S(2)}, u32[]{:S(2)}) collective-permute-start(f32[144,256]{1,0:T(8,128)S(1)} %get-tuple-element.74.token_ref.own_ref), channel_id=1, source_target_pairs={{0,8},{1,9},{2,10},{3,11},{4,12},{5,13},{6,14},{7,15},{8,0},{9,1},... | collective-permute-start | bytes 442376 | tf_op jit(solution)/shard_map/ppermute | solution.py:583
  38.3 0.0 collective-permute-done.11.r_ref.refs_0_
  38.3 0.0 collective-permute-start.12
  38.3 0.9 %turn.4 = (bf16[8,256,256]{2,1,0:T(8,128)(2,1)S(1)}, bf16[8,256,256]{2,1,0:T(8,128)(2,1)S(1)}, f32[8,256]{1,0:T(8,128)S(1)}) custom-call(f32[4,8,256,256]{3,2,1,0:T(8,128)S(1)} %get-tuple-element.52.g_ref, f32[32,256]{1,0:T(8,128)S(1)} %get-tuple-element.53._.delta_ref, f32[144,256]{1,0:T(8,128)S(1)} %get-tuple-element.74.token_ref.own_ref), custom_call_target="tpu_custom_call" | custom-call | flops 100000 | tf_op jit(solution)/shard_map/turn/pallas_call | solution.py:507
  39.2 3.4 %place.1 = (f32[4,528,256]{2,1,0:T(8,128)S(1)}, bf16[4,256,256]{2,1,0:T(8,128)(2,1)S(1)}, f32[4,256,128]{2,1,0:T(8,128)S(1)}, f32[4,8,256]{2,1,0:T(8,128)S(1)}) custom-call(f32[6,256,256]{2,1,0:T(8,128)S(1)} %get-tuple-element.58.maps_ref.subs_ref, f32[4,272,256]{2,1,0:T(8,128)S(1)} %get-tuple-element.76.sub_noises_ref, ...), custom_call_target="tpu_custom_call" | custom-call | flops 100000 | tf_op jit(solution)/shard_map/place/pallas_call | solution.py:507
  42.6 0.0 collective-permute-done.13.other_ref.refs_2_
  42.6 0.0 collective-permute-done.12.x_ref.refs_1_
  42.6 0.5 level.1.token_ref
  43.1 2.7 %collective-permute-start.14 = (f32[72,256]{1,0:T(8,128)S(1)}, f32[72,256]{1,0:T(8,128)S(1)}, u32[]{:S(2)}, u32[]{:S(2)}) collective-permute-start(f32[72,256]{1,0:T(8,128)S(1)} %level.1.token_ref), channel_id=1, source_target_pairs={{0,16},{1,17},{2,18},{3,19},{4,20},{5,21},{6,22},{7,23},{8,24},{9,... | collective-permute-start | bytes 221192 | tf_op jit(solution)/shard_map/ppermute | solution.py:583
  45.8 0.9 %turn.6 = (bf16[8,256,256]{2,1,0:T(8,128)(2,1)S(1)}, bf16[8,256,256]{2,1,0:T(8,128)(2,1)S(1)}, f32[8,256]{1,0:T(8,128)S(1)}) custom-call(f32[4,8,256,256]{3,2,1,0:T(8,128)S(1)} %get-tuple-element.52.g_ref, f32[32,256]{1,0:T(8,128)S(1)} %get-tuple-element.53._.delta_ref, f32[72,256]{1,0:T(8,128)S(1)} %level.1.token_ref), custom_call_target="tpu_custom_call" | custom-call | flops 100000 | tf_op jit(solution)/shard_map/turn/pallas_call | solution.py:507
  46.7 0.9 %turn.5 = (bf16[8,256,256]{2,1,0:T(8,128)(2,1)S(1)}, bf16[8,256,256]{2,1,0:T(8,128)(2,1)S(1)}, f32[8,256]{1,0:T(8,128)S(1)}) custom-call(f32[4,8,256,256]{3,2,1,0:T(8,128)S(1)} %get-tuple-element.52.g_ref, f32[32,256]{1,0:T(8,128)S(1)} %get-tuple-element.53._.delta_ref, f32[72,256]{1,0:T(8,128)S(1)} %level.1.token_ref), custom_call_target="tpu_custom_call" | custom-call | flops 100000 | tf_op jit(solution)/shard_map/turn/pallas_call | solution.py:507
  47.5 0.2 before.1
  47.8 2.5 %collective-permute-done.14.refs_24_ = f32[72,256]{1,0:T(8,128)S(1)} collective-permute-done((f32[72,256]{1,0:T(8,128)S(1)}, f32[72,256]{1,0:T(8,128)S(1)}, u32[]{:S(2)}, u32[]{:S(2)}) %collective-permute-start.14) | collective-permute-done | bytes 73760 | tf_op jit(solution)/shard_map/ppermute | solution.py:583
  50.2 0.1 collective-permute-start.15
  50.3 0.9 %turn.7 = (bf16[8,256,256]{2,1,0:T(8,128)(2,1)S(1)}, bf16[8,256,256]{2,1,0:T(8,128)(2,1)S(1)}, f32[8,256]{1,0:T(8,128)S(1)}) custom-call(f32[4,8,256,256]{3,2,1,0:T(8,128)S(1)} %get-tuple-element.52.g_ref, f32[32,256]{1,0:T(8,128)S(1)} %get-tuple-element.53._.delta_ref, f32[72,256]{1,0:T(8,128)S(1)} %level.1.token_ref), custom_call_target="tpu_custom_call" | custom-call | flops 100000 | tf_op jit(solution)/shard_map/turn/pallas_call | solution.py:507
  51.2 0.3 collective-permute-done.15.refs_25_
  51.5 4.7 %finish.1 = (f32[32,256]{1,0:T(8,128)}, f32[32,256]{1,0:T(8,128)}) custom-call(bf16[8,256,256]{2,1,0:T(8,128)(2,1)S(1)} %get-tuple-element.71.refs_0_, bf16[8,256,256]{2,1,0:T(8,128)(2,1)S(1)} %get-tuple-element.81.refs_1_, bf16[8,256,256]{2,1,0:T(8,128)(2,1)S(1)} %get-tuple-element.82.refs_2_, bf16[8,256,256]{2,1,0:T(8,128)(2,1)S(1)} %get-tuple-element.83.refs_3_, ...), custom_call_target="tpu_custom_call" | custom-call | flops 100000 | tf_op jit(solution)/shard_map/finish/pallas_call | solution.py:507
  (13 shorter events, 0.0 us)
Async XLA Ops:
  0.6 10.3 %copy-start = (bf16[32,64,256]{2,1,0:T(8,128)(2,1)S(1)}, bf16[32,64,256]{2,1,0:T(8,128)(2,1)}, u32[]{:S(2)}) copy-start(bf16[32,64,256]{2,1,0:T(8,128)(2,1)} %param.14) | copy-start | bytes 3145732
  0.6 10.3 %copy-start.1 = (bf16[32,64,256]{2,1,0:T(8,128)(2,1)S(1)}, bf16[32,64,256]{2,1,0:T(8,128)(2,1)}, u32[]{:S(2)}) copy-start(bf16[32,64,256]{2,1,0:T(8,128)(2,1)} %param.13) | copy-start | bytes 3145732
  0.7 10.3 %copy-start.2 = (bf16[256,256]{1,0:T(8,128)(2,1)S(1)}, bf16[256,256]{1,0:T(8,128)(2,1)}, u32[]{:S(2)}) copy-start(bf16[256,256]{1,0:T(8,128)(2,1)} %nf_ref.1) | copy-start | bytes 393220
  10.4 2.7 %collective-permute-start = (f32[256,256]{1,0:T(8,128)S(1)}, f32[256,256]{1,0:T(8,128)S(1)}, u32[]{:S(2)}, u32[]{:S(2)}) collective-permute-start(f32[256,256]{1,0:T(8,128)S(1)} %get-tuple-element.54.own_ref.own_map_ref), channel_id=1, source_target_pairs={{0,1},{1,0},{2,3},{3,2},{4,5},{5,4},{6,7},{7,6},{8,9},{9,8},{10,11... | collective-permute-start | bytes 786440 | tf_op jit(solution)/shard_map/ppermute | solution.py:583
  10.9 6.7 %copy-start.3 = (f32[32,256]{1,0:T(8,128)S(1)}, f32[32,256]{1,0:T(8,128)}, u32[]{:S(2)}) copy-start(f32[32,256]{1,0:T(8,128)} %decay_ref.1) | copy-start | bytes 98308
  10.9 6.7 %copy-start.6 = (f32[64]{0:T(128)S(1)}, f32[64]{0:T(128)}, u32[]{:S(2)}) copy-start(f32[64]{0:T(128)} %param.16) | copy-start | bytes 772
  13.4 16.0 %collective-permute-start.10 = (f32[256,256]{1,0:T(8,128)S(1)}, f32[256,256]{1,0:T(8,128)S(1)}, u32[]{:S(2)}, u32[]{:S(2)}) collective-permute-start(f32[256,256]{1,0:T(8,128)S(1)} %chip_maps.1._.refs_0_), channel_id=1, source_target_pairs={{0,6},{1,7},{2,4},{3,5},{4,2},{5,3},{6,0},{7,1},{8,14},{9,15},{10,... | collective-permute-start | bytes 786440 | tf_op jit(solution)/shard_map/ppermute | solution.py:583
  16.9 12.6 %collective-permute-start.9 = (f32[256,256]{1,0:T(8,128)S(1)}, f32[256,256]{1,0:T(8,128)S(1)}, u32[]{:S(2)}, u32[]{:S(2)}) collective-permute-start(f32[256,256]{1,0:T(8,128)S(1)} %chip_maps.1._.refs_0_), channel_id=1, source_target_pairs={{0,4},{1,5},{2,6},{3,7},{4,0},{5,1},{6,2},{7,3},{8,12},{9,13},{10,... | collective-permute-start | bytes 786440 | tf_op jit(solution)/shard_map/ppermute | solution.py:583
  17.4 12.4 %collective-permute-start.8 = (f32[256,256]{1,0:T(8,128)S(1)}, f32[256,256]{1,0:T(8,128)S(1)}, u32[]{:S(2)}, u32[]{:S(2)}) collective-permute-start(f32[256,256]{1,0:T(8,128)S(1)} %chip_maps.1._.refs_0_), channel_id=1, source_target_pairs={{0,2},{1,3},{2,0},{3,1},{4,6},{5,7},{6,4},{7,5},{8,10},{9,11},{10,... | collective-permute-start | bytes 786440 | tf_op jit(solution)/shard_map/ppermute | solution.py:583
  17.6 12.2 %copy-start.4 = (f32[256]{0:T(256)S(1)}, f32[256]{0:T(256)}, u32[]{:S(2)}) copy-start(f32[256]{0:T(256)} %param.10) | copy-start | bytes 3076
  17.6 12.2 %copy-start.5 = (f32[256]{0:T(256)S(1)}, f32[256]{0:T(256)}, u32[]{:S(2)}) copy-start(f32[256]{0:T(256)} %param.9) | copy-start | bytes 3076
  24.1 1.4 %collective-permute-start.1 = (f32[144,256]{1,0:T(8,128)S(1)}, f32[144,256]{1,0:T(8,128)S(1)}, u32[]{:S(2)}, u32[]{:S(2)}) collective-permute-start(f32[144,256]{1,0:T(8,128)S(1)} %get-tuple-element.59.own_ref), channel_id=1, source_target_pairs={{0,1},{1,0},{2,3},{3,2},{4,5},{5,4},{6,7},{7,6},{8,9},{9,8},{10,11... | collective-permute-start | bytes 442376 | tf_op jit(solution)/shard_map/ppermute | solution.py:583
  26.0 6.8 %collective-permute-start.6 = (f32[72,256]{1,0:T(8,128)S(1)}, f32[72,256]{1,0:T(8,128)S(1)}, u32[]{:S(2)}, u32[]{:S(2)}) collective-permute-start(f32[72,256]{1,0:T(8,128)S(1)} %get-tuple-element.61), channel_id=1, source_target_pairs={{0,6},{1,7},{2,4},{3,5},{4,2},{5,3},{6,0},{7,1},{8,14},{9,15},{10,... | collective-permute-start | bytes 221192 | tf_op jit(solution)/shard_map/ppermute | solution.py:583
  28.9 4.4 %collective-permute-start.4 = (f32[72,256]{1,0:T(8,128)S(1)}, f32[72,256]{1,0:T(8,128)S(1)}, u32[]{:S(2)}, u32[]{:S(2)}) collective-permute-start(f32[72,256]{1,0:T(8,128)S(1)} %get-tuple-element.61), channel_id=1, source_target_pairs={{0,4},{1,5},{2,6},{3,7},{4,0},{5,1},{6,2},{7,3},{8,12},{9,13},{10,... | collective-permute-start | bytes 221192 | tf_op jit(solution)/shard_map/ppermute | solution.py:583
  29.4 4.4 %collective-permute-start.2 = (f32[72,256]{1,0:T(8,128)S(1)}, f32[72,256]{1,0:T(8,128)S(1)}, u32[]{:S(2)}, u32[]{:S(2)}) collective-permute-start(f32[72,256]{1,0:T(8,128)S(1)} %get-tuple-element.61), channel_id=1, source_target_pairs={{0,2},{1,3},{2,0},{3,1},{4,6},{5,7},{6,4},{7,5},{8,10},{9,11},{10,... | collective-permute-start | bytes 221192 | tf_op jit(solution)/shard_map/ppermute | solution.py:583
  30.9 7.3 %collective-permute-start.11 = (f32[128,256]{1,0:T(8,128)S(1)}, f32[128,256]{1,0:T(8,128)S(1)}, u32[]{:S(2)}, u32[]{:S(2)}) collective-permute-start(f32[128,256]{1,0:T(8,128)S(1)} %get-tuple-element.73), channel_id=1, source_target_pairs={{0,8},{1,9},{2,10},{3,11},{4,12},{5,13},{6,14},{7,15},{8,0},{9,1},... | collective-permute-start | bytes 393224 | tf_op jit(solution)/shard_map/ppermute | solution.py:583
  32.8 1.3 %collective-permute-start.7 = (f32[72,256]{1,0:T(8,128)S(1)}, f32[72,256]{1,0:T(8,128)S(1)}, u32[]{:S(2)}, u32[]{:S(2)}) collective-permute-start(f32[72,256]{1,0:T(8,128)S(1)} %collective-permute-done.6.refs_5_), channel_id=1, source_target_pairs={{0,1},{1,0},{2,3},{3,2},{4,5},{5,4},{6,7},{7,6},{8,9},{9,8},{10,11... | collective-permute-start | bytes 221192 | tf_op jit(solution)/shard_map/ppermute | solution.py:583
  33.2 1.3 %collective-permute-start.5 = (f32[72,256]{1,0:T(8,128)S(1)}, f32[72,256]{1,0:T(8,128)S(1)}, u32[]{:S(2)}, u32[]{:S(2)}) collective-permute-start(f32[72,256]{1,0:T(8,128)S(1)} %collective-permute-done.4.refs_3_), channel_id=1, source_target_pairs={{0,1},{1,0},{2,3},{3,2},{4,5},{5,4},{6,7},{7,6},{8,9},{9,8},{10,11... | collective-permute-start | bytes 221192 | tf_op jit(solution)/shard_map/ppermute | solution.py:583
  33.7 1.3 %collective-permute-start.3 = (f32[72,256]{1,0:T(8,128)S(1)}, f32[72,256]{1,0:T(8,128)S(1)}, u32[]{:S(2)}, u32[]{:S(2)}) collective-permute-start(f32[72,256]{1,0:T(8,128)S(1)} %collective-permute-done.2.refs_1_), channel_id=1, source_target_pairs={{0,1},{1,0},{2,3},{3,2},{4,5},{5,4},{6,7},{7,6},{8,9},{9,8},{10,11... | collective-permute-start | bytes 221192 | tf_op jit(solution)/shard_map/ppermute | solution.py:583
  36.6 6.0 %collective-permute-start.13 = (f32[144,256]{1,0:T(8,128)S(1)}, f32[144,256]{1,0:T(8,128)S(1)}, u32[]{:S(2)}, u32[]{:S(2)}) collective-permute-start(f32[144,256]{1,0:T(8,128)S(1)} %get-tuple-element.74.token_ref.own_ref), channel_id=1, source_target_pairs={{0,8},{1,9},{2,10},{3,11},{4,12},{5,13},{6,14},{7,15},{8,0},{9,1},... | collective-permute-start | bytes 442376 | tf_op jit(solution)/shard_map/ppermute | solution.py:583
  38.3 4.4 %collective-permute-start.12 = (f32[128,256]{1,0:T(8,128)S(1)}, f32[128,256]{1,0:T(8,128)S(1)}, u32[]{:S(2)}, u32[]{:S(2)}) collective-permute-start(f32[128,256]{1,0:T(8,128)S(1)} %collective-permute-done.11.r_ref.refs_0_), channel_id=1, source_target_pairs={{0,1},{1,0},{2,3},{3,2},{4,5},{5,4},{6,7},{7,6},{8,9},{9,8},{10,11... | collective-permute-start | bytes 393224 | tf_op jit(solution)/shard_map/ppermute | solution.py:583
  43.1 7.1 %collective-permute-start.14 = (f32[72,256]{1,0:T(8,128)S(1)}, f32[72,256]{1,0:T(8,128)S(1)}, u32[]{:S(2)}, u32[]{:S(2)}) collective-permute-start(f32[72,256]{1,0:T(8,128)S(1)} %level.1.token_ref), channel_id=1, source_target_pairs={{0,16},{1,17},{2,18},{3,19},{4,20},{5,21},{6,22},{7,23},{8,24},{9,... | collective-permute-start | bytes 221192 | tf_op jit(solution)/shard_map/ppermute | solution.py:583
  50.2 1.3 %collective-permute-start.15 = (f32[72,256]{1,0:T(8,128)S(1)}, f32[72,256]{1,0:T(8,128)S(1)}, u32[]{:S(2)}, u32[]{:S(2)}) collective-permute-start(f32[72,256]{1,0:T(8,128)S(1)} %collective-permute-done.14.refs_24_), channel_id=1, source_target_pairs={{0,1},{1,0},{2,3},{3,2},{4,5},{5,4},{6,7},{7,6},{8,9},{9,8},{10,11... | collective-permute-start | bytes 221192 | tf_op jit(solution)/shard_map/ppermute | solution.py:583

commit v5 on v4

--- a/solution.py
+++ b/solution.py
@@ -383,7 +383,7 @@
     pick(2, unpack(core_ref[...]))
 
 
-def level_kernel(axes, bit, own_map_ref, own_ref, r_ref, x_ref, other_ref, _, __, *outs):
+def level_kernel(axes, bit, own_map_ref, own_ref, r_ref, x_ref, other_ref, _, *outs):
     *outs, total_s = outs
     rank = rank_of(axes)
     upper, high = rank % 2 == 1, bit_of(rank, bit) == 1
@@ -488,7 +488,7 @@
                                          + both[s][n:n + 1] + (both[s][n + 1:n + 2] + rest[s][0:1]))
         return carry
 
-    lax.fori_loop(0, steps, step, 0)
+    lax.fori_loop(0, steps, step, 0, unroll=4)
 
 
 def vmem():
@@ -614,7 +614,6 @@
     placed = call(functools.partial(place_kernel, axes), "place",
                   [shape(subs, 2 * n + 16, n), shape(subs, n, n, dtype=bf16), shape(subs, n, 128), shape(subs, 8, n)],
                   [maps, noises, map_picks, noise_picks])
-    turned = [turn(0, g, delta, packed)]
     received = []
     for k, bit in enumerate(bits[:-1]):
         moving = swap(packed, bit)
@@ -624,16 +623,16 @@
         more = k < len(bits) - 2
         size = h + 16 if more else h // 2 + 8
         new = call(functools.partial(level_kernel, axes, bit), "level",
-                   [shape(size, n)] + ([shape(n, n), shape(h, n)] if more else []), [total, packed, *got, placed[3], turned[0][2]],
-                   [vmem()] * 5 + [anywhere()] * 2, [pltpu.VMEM((h + 16, n), f32)])
+                   [shape(size, n)] + ([shape(n, n), shape(h, n)] if more else []), [total, packed, *got, placed[3]],
+                   [vmem()] * 5 + [anywhere()], [pltpu.VMEM((h + 16, n), f32)])
         packed = new[0]
         if more:
             total, half = new[1:]
     before = call(functools.partial(before_kernel, axes, bits[:-1]), "before",
                   [shape(n, n), shape(n, n), shape(16, n), shape(n, n, dtype=bf16), shape(n, 128), shape(8, n)],
                   [init_var.reshape(1, n), init_mean.reshape(1, n), *received])
-    turned += [turn(k, g, delta, packed) for k in range(1, subs)]
-    r, *_ = lax.optimization_barrier((swap(packed, bits[-1]), *before, turned[1][2], turned[2][2]))
+    turned = [turn(k, g, delta, packed) for k in range(subs)]
+    r, *_ = lax.optimization_barrier((swap(packed, bits[-1]), *before, *(x[2] for x in turned[:3])))
     return tuple(finish(axes, bits[-1], turned, diag, shift, placed, before, r, swap(r, 1)))
 
 

time: 56.3 us -> 54.2 us (0.963)
  waiting for transfers between devices: 6.53 us -> 5 us
  Pallas kernels: 34.2 us -> 33.6 us
    ppermute x16, waiting for transfers between devices: 6.53 us -> 5 us  [swap(): return lax.ppermute(x, names, [(k, k ^ bit) for k in range(count)])]
    pallas_call x15, Pallas kernels: 34.2 us -> 33.6 us  [call(): pl.pallas_call(kernel, in_specs=specs or [vmem()] * len(args), out_specs=...]
  transfers between devices with their start and end apart: 16 -> 16, of which waited for: 9 -> 10; matrix products, arithmetic and copies ran while one was open for 0% -> 0% of each run, Pallas kernels for 34% -> 35%
where the time goes in v5:
time: 54.2 us; the launch traced here: 54.1 us
  Pallas kernels  33.6 us (62%)
  starting transfers between devices  14.6 us (27%)
  waiting for transfers between devices  5 us (9%)
  between operations  0.81 us (1%)
    pallas_call x15, Pallas kernels, call(): pl.pallas_call(kernel, in_specs=specs or [vmem()] * len(args), out_specs=...  33.6 us
    ppermute x16, starting transfers between devices, swap(): return lax.ppermute(x, names, [(k, k ^ bit) for k in range(count)])  14.6 us
    ppermute x16, waiting for transfers between devices, swap(): return lax.ppermute(x, names, [(k, k ^ bit) for k in range(count)])  5 us
  transfers between devices with their start and end apart: 16, of which 10 were waited for; matrix products, arithmetic and copies ran while one was open for 0% of the time, Pallas kernels for 35%

profile of v5, /device:TPU:0, one launch (start us, length us, event | category | flops | bytes accessed | tf_op | source)
XLA Modules:
  0.0 54.1 jit_solution(15820619530680332184)
XLA Ops:
  0.7 9.7 %step_maps.1 = (f32[4,8,256,256]{3,2,1,0:T(8,128)S(1)}, bf16[4,8,256,256]{3,2,1,0:T(8,128)(2,1)S(1)}, f32[4,8,256,128]{3,2,1,0:T(8,128)S(1)}, f32[32,256]{1,0:T(...) custom-call(f32[32,256]{1,0:T(8,128)} %decay_ref.1, ...), custom_call_target="tpu_custom_call" | custom-call | flops 10000000000 | tf_op jit(solution)/shard_map/step_maps/pallas_call | solution.py:507
  10.4 0.5 collective-permute-start
  10.9 0.0 copy-start.6
  10.9 2.1 %step_shapes.1._.shaped_ref = bf16[4,8,256,256]{3,2,1,0:T(8,128)(2,1)S(1)} custom-call(bf16[4,8,64,256]{3,2,1,0:T(8,128)(2,1)S(1)} %bitcast.10, bf16[4,8,64,256]{3,2,1,0:T(8,128)(2,1)S(1)} %bitcast.7, bf16[256,256]{1,0:T(8,128)(2,1)S(1)} %copy-done.2, f32[32,256]{1,0:T(8,128)S(1)} %get-tuple-element.53._.delta_ref), custom_call_target="tpu_custom_call" | custom-call | flops 100000 | tf_op jit(solution)/shard_map/step_shapes/pallas_call | solution.py:507
  13.0 0.0 collective-permute-done.other_ref.other_map_ref.refs_4_
  13.1 0.3 chip_maps.1._.refs_0_
  13.4 3.5 %collective-permute-start.3 = (f32[256,256]{1,0:T(8,128)S(1)}, f32[256,256]{1,0:T(8,128)S(1)}, u32[]{:S(2)}, u32[]{:S(2)}) collective-permute-start(f32[256,256]{1,0:T(8,128)S(1)} %chip_maps.1._.refs_0_), channel_id=1, source_target_pairs={{0,6},{1,7},{2,4},{3,5},{4,2},{5,3},{6,0},{7,1},{8,14},{9,15},{10,... | collective-permute-start | bytes 786440 | tf_op jit(solution)/shard_map/ppermute | solution.py:583
  16.9 0.5 collective-permute-start.2
  17.4 0.1 collective-permute-start.1
  17.6 6.5 %step_noises.1 = (f32[32,256]{1,0:T(8,128)S(1)}, f32[4,272,256]{2,1,0:T(8,128)S(1)}, f32[144,256]{1,0:T(8,128)S(1)}) custom-call(f32[32,256]{1,0:T(8,128)S(1)} %copy-done.3, bf16[4,8,256,256]{3,2,1,0:T(8,128)(2,1)S(1)} %get-tuple-element.55.e_ref, f32[4,8,256,128]{3,2,1,0:T(8,128)S(1)} %get-tuple-element.56.dcol_ref, ...), custom_call_target="tpu_custom_call" | custom-call | flops 100000 | tf_op jit(solution)/shard_map/step_noises/pallas_call | solution.py:507
  24.1 0.1 collective-permute-start.4
  24.2 1.4 %collective-permute-done.4.other_ref.refs_12_ = f32[144,256]{1,0:T(8,128)S(1)} collective-permute-done((f32[144,256]{1,0:T(8,128)S(1)}, f32[144,256]{1,0:T(8,128)S(1)}, u32[]{:S(2)}, u32[]{:S(2)}) %collective-permute-start.4) | collective-permute-done | bytes 147488 | tf_op jit(solution)/shard_map/ppermute | solution.py:583
  25.5 0.5 core_noises.1
  26.0 2.9 %collective-permute-start.10 = (f32[72,256]{1,0:T(8,128)S(1)}, f32[72,256]{1,0:T(8,128)S(1)}, u32[]{:S(2)}, u32[]{:S(2)}) collective-permute-start(f32[72,256]{1,0:T(8,128)S(1)} %get-tuple-element.66), channel_id=1, source_target_pairs={{0,6},{1,7},{2,4},{3,5},{4,2},{5,3},{6,0},{7,1},{8,14},{9,15},{10,... | collective-permute-start | bytes 221192 | tf_op jit(solution)/shard_map/ppermute | solution.py:583
  28.9 0.5 collective-permute-start.8
  29.4 0.0 collective-permute-done.3.refs_3_
  29.4 0.1 collective-permute-start.6
  29.6 0.0 collective-permute-done.2.refs_2_
  29.6 0.2 collective-permute-done.1.refs_1_
  29.8 1.1 %plane_maps.1 = (f32[3,256,256]{2,1,0:T(8,128)S(1)}, bf16[3,256,256]{2,1,0:T(8,128)(2,1)S(1)}, f32[3,256,128]{2,1,0:T(8,128)S(1)}, f32[8,256]{1,0:T(8,128)S(1)},...) custom-call(f32[256,256]{1,0:T(8,128)S(1)} %chip_maps.1._.refs_0_, ...), custom_call_target="tpu_custom_call" | custom-call | flops 100000 | tf_op jit(solution)/shard_map/plane_maps/pallas_call | solution.py:507
  30.9 1.9 %collective-permute-start.5 = (f32[128,256]{1,0:T(8,128)S(1)}, f32[128,256]{1,0:T(8,128)S(1)}, u32[]{:S(2)}, u32[]{:S(2)}) collective-permute-start(f32[128,256]{1,0:T(8,128)S(1)} %get-tuple-element.65), channel_id=1, source_target_pairs={{0,8},{1,9},{2,10},{3,11},{4,12},{5,13},{6,14},{7,15},{8,0},{9,1},... | collective-permute-start | bytes 393224 | tf_op jit(solution)/shard_map/ppermute | solution.py:583
  32.8 0.0 collective-permute-done.10.refs_5_
  32.8 0.0 collective-permute-start.11
  32.8 0.4 collective-permute-done.8.refs_3_
  33.2 0.1 collective-permute-start.9
  33.3 0.4 collective-permute-done.6.refs_1_
  33.8 0.0 collective-permute-start.7
  33.8 0.3 collective-permute-done.11.refs_6_
  34.1 0.4 collective-permute-done.9.refs_4_
  34.5 0.5 collective-permute-done.7.refs_2_
  35.0 1.6 %plane_noises.1 = (f32[144,256]{1,0:T(8,128)S(1)}, f32[3,272,256]{2,1,0:T(8,128)S(1)}) custom-call(f32[144,256]{1,0:T(8,128)S(1)} %get-tuple-element.60.refs_0_, f32[72,256]{1,0:T(8,128)S(1)} %collective-permute-done.6.refs_1_, f32[72,256]{1,0:T(8,128)S(1)} %collective-permute-done.7.refs_2_, f32[72,256]{1,0:T(8,128)S(1)} %collective-permute-done.8.refs_3_, ...), custom_call_target="tpu_custom_call" | custom-call | flops 100000 | tf_op jit(solution)/shard_map/plane_noises/pallas_call | solution.py:507
  36.6 1.6 %collective-permute-start.13 = (f32[144,256]{1,0:T(8,128)S(1)}, f32[144,256]{1,0:T(8,128)S(1)}, u32[]{:S(2)}, u32[]{:S(2)}) collective-permute-start(f32[144,256]{1,0:T(8,128)S(1)} %get-tuple-element.73.own_ref), channel_id=1, source_target_pairs={{0,8},{1,9},{2,10},{3,11},{4,12},{5,13},{6,14},{7,15},{8,0},{9,1},... | collective-permute-start | bytes 442376 | tf_op jit(solution)/shard_map/ppermute | solution.py:583
  38.3 0.0 collective-permute-done.5.r_ref.refs_0_
  38.3 0.0 collective-permute-start.12
  38.3 3.5 %place.1 = (f32[4,528,256]{2,1,0:T(8,128)S(1)}, bf16[4,256,256]{2,1,0:T(8,128)(2,1)S(1)}, f32[4,256,128]{2,1,0:T(8,128)S(1)}, f32[4,8,256]{2,1,0:T(8,128)S(1)}) custom-call(f32[6,256,256]{2,1,0:T(8,128)S(1)} %get-tuple-element.58.maps_ref.subs_ref, f32[4,272,256]{2,1,0:T(8,128)S(1)} %get-tuple-element.75.sub_noises_ref, ...), custom_call_target="tpu_custom_call" | custom-call | flops 100000 | tf_op jit(solution)/shard_map/place/pallas_call | solution.py:507
  41.7 0.9 %collective-permute-done.13.other_ref.refs_2_ = f32[144,256]{1,0:T(8,128)S(1)} collective-permute-done((f32[144,256]{1,0:T(8,128)S(1)}, f32[144,256]{1,0:T(8,128)S(1)}, u32[]{:S(2)}, u32[]{:S(2)}) %collective-permute-start.13) | collective-permute-done | bytes 147488 | tf_op jit(solution)/shard_map/ppermute | solution.py:583
  42.6 0.0 collective-permute-done.12.x_ref.refs_1_
  42.6 0.5 level.1.token_ref
  43.1 2.7 %collective-permute-start.14 = (f32[72,256]{1,0:T(8,128)S(1)}, f32[72,256]{1,0:T(8,128)S(1)}, u32[]{:S(2)}, u32[]{:S(2)}) collective-permute-start(f32[72,256]{1,0:T(8,128)S(1)} %level.1.token_ref), channel_id=1, source_target_pairs={{0,16},{1,17},{2,18},{3,19},{4,20},{5,21},{6,22},{7,23},{8,24},{9,... | collective-permute-start | bytes 221192 | tf_op jit(solution)/shard_map/ppermute | solution.py:583
  45.7 0.9 %turn.6 = (bf16[8,256,256]{2,1,0:T(8,128)(2,1)S(1)}, bf16[8,256,256]{2,1,0:T(8,128)(2,1)S(1)}, f32[8,256]{1,0:T(8,128)S(1)}) custom-call(f32[4,8,256,256]{3,2,1,0:T(8,128)S(1)} %get-tuple-element.52.g_ref, f32[32,256]{1,0:T(8,128)S(1)} %get-tuple-element.53._.delta_ref, f32[72,256]{1,0:T(8,128)S(1)} %level.1.token_ref), custom_call_target="tpu_custom_call" | custom-call | flops 100000 | tf_op jit(solution)/shard_map/turn/pallas_call | solution.py:507
  46.6 0.9 %turn.5 = (bf16[8,256,256]{2,1,0:T(8,128)(2,1)S(1)}, bf16[8,256,256]{2,1,0:T(8,128)(2,1)S(1)}, f32[8,256]{1,0:T(8,128)S(1)}) custom-call(f32[4,8,256,256]{3,2,1,0:T(8,128)S(1)} %get-tuple-element.52.g_ref, f32[32,256]{1,0:T(8,128)S(1)} %get-tuple-element.53._.delta_ref, f32[72,256]{1,0:T(8,128)S(1)} %level.1.token_ref), custom_call_target="tpu_custom_call" | custom-call | flops 100000 | tf_op jit(solution)/shard_map/turn/pallas_call | solution.py:507
  47.5 0.9 %turn.4 = (bf16[8,256,256]{2,1,0:T(8,128)(2,1)S(1)}, bf16[8,256,256]{2,1,0:T(8,128)(2,1)S(1)}, f32[8,256]{1,0:T(8,128)S(1)}) custom-call(f32[4,8,256,256]{3,2,1,0:T(8,128)S(1)} %get-tuple-element.52.g_ref, f32[32,256]{1,0:T(8,128)S(1)} %get-tuple-element.53._.delta_ref, f32[72,256]{1,0:T(8,128)S(1)} %level.1.token_ref), custom_call_target="tpu_custom_call" | custom-call | flops 100000 | tf_op jit(solution)/shard_map/turn/pallas_call | solution.py:507
  48.4 0.2 before.1
  48.6 0.1 collective-permute-done.14.refs_24_
  48.7 0.0 collective-permute-start.15
  48.7 0.9 %turn.7 = (bf16[8,256,256]{2,1,0:T(8,128)(2,1)S(1)}, bf16[8,256,256]{2,1,0:T(8,128)(2,1)S(1)}, f32[8,256]{1,0:T(8,128)S(1)}) custom-call(f32[4,8,256,256]{3,2,1,0:T(8,128)S(1)} %get-tuple-element.52.g_ref, f32[32,256]{1,0:T(8,128)S(1)} %get-tuple-element.53._.delta_ref, f32[72,256]{1,0:T(8,128)S(1)} %level.1.token_ref), custom_call_target="tpu_custom_call" | custom-call | flops 100000 | tf_op jit(solution)/shard_map/turn/pallas_call | solution.py:507
  49.6 0.4 collective-permute-done.15.refs_25_
  50.0 4.1 %finish.1 = (f32[32,256]{1,0:T(8,128)}, f32[32,256]{1,0:T(8,128)}) custom-call(bf16[8,256,256]{2,1,0:T(8,128)(2,1)S(1)} %get-tuple-element.79.refs_0_, bf16[8,256,256]{2,1,0:T(8,128)(2,1)S(1)} %get-tuple-element.80.refs_1_, bf16[8,256,256]{2,1,0:T(8,128)(2,1)S(1)} %get-tuple-element.81.refs_2_, bf16[8,256,256]{2,1,0:T(8,128)(2,1)S(1)} %get-tuple-element.82.refs_3_, ...), custom_call_target="tpu_custom_call" | custom-call | flops 100000 | tf_op jit(solution)/shard_map/finish/pallas_call | solution.py:507
  (13 shorter events, 0.0 us)
Async XLA Ops:
  0.6 10.3 %copy-start = (bf16[32,64,256]{2,1,0:T(8,128)(2,1)S(1)}, bf16[32,64,256]{2,1,0:T(8,128)(2,1)}, u32[]{:S(2)}) copy-start(bf16[32,64,256]{2,1,0:T(8,128)(2,1)} %param.14) | copy-start | bytes 3145732
  0.6 10.3 %copy-start.1 = (bf16[32,64,256]{2,1,0:T(8,128)(2,1)S(1)}, bf16[32,64,256]{2,1,0:T(8,128)(2,1)}, u32[]{:S(2)}) copy-start(bf16[32,64,256]{2,1,0:T(8,128)(2,1)} %param.13) | copy-start | bytes 3145732
  0.7 10.3 %copy-start.2 = (bf16[256,256]{1,0:T(8,128)(2,1)S(1)}, bf16[256,256]{1,0:T(8,128)(2,1)}, u32[]{:S(2)}) copy-start(bf16[256,256]{1,0:T(8,128)(2,1)} %nf_ref.1) | copy-start | bytes 393220
  10.4 2.7 %collective-permute-start = (f32[256,256]{1,0:T(8,128)S(1)}, f32[256,256]{1,0:T(8,128)S(1)}, u32[]{:S(2)}, u32[]{:S(2)}) collective-permute-start(f32[256,256]{1,0:T(8,128)S(1)} %get-tuple-element.54.own_ref.own_map_ref), channel_id=1, source_target_pairs={{0,1},{1,0},{2,3},{3,2},{4,5},{5,4},{6,7},{7,6},{8,9},{9,8},{10,11... | collective-permute-start | bytes 786440 | tf_op jit(solution)/shard_map/ppermute | solution.py:583
  10.9 6.7 %copy-start.3 = (f32[32,256]{1,0:T(8,128)S(1)}, f32[32,256]{1,0:T(8,128)}, u32[]{:S(2)}) copy-start(f32[32,256]{1,0:T(8,128)} %decay_ref.1) | copy-start | bytes 98308
  10.9 6.7 %copy-start.6 = (f32[64]{0:T(128)S(1)}, f32[64]{0:T(128)}, u32[]{:S(2)}) copy-start(f32[64]{0:T(128)} %param.16) | copy-start | bytes 772
  13.4 16.0 %collective-permute-start.3 = (f32[256,256]{1,0:T(8,128)S(1)}, f32[256,256]{1,0:T(8,128)S(1)}, u32[]{:S(2)}, u32[]{:S(2)}) collective-permute-start(f32[256,256]{1,0:T(8,128)S(1)} %chip_maps.1._.refs_0_), channel_id=1, source_target_pairs={{0,6},{1,7},{2,4},{3,5},{4,2},{5,3},{6,0},{7,1},{8,14},{9,15},{10,... | collective-permute-start | bytes 786440 | tf_op jit(solution)/shard_map/ppermute | solution.py:583
  16.9 12.6 %collective-permute-start.2 = (f32[256,256]{1,0:T(8,128)S(1)}, f32[256,256]{1,0:T(8,128)S(1)}, u32[]{:S(2)}, u32[]{:S(2)}) collective-permute-start(f32[256,256]{1,0:T(8,128)S(1)} %chip_maps.1._.refs_0_), channel_id=1, source_target_pairs={{0,4},{1,5},{2,6},{3,7},{4,0},{5,1},{6,2},{7,3},{8,12},{9,13},{10,... | collective-permute-start | bytes 786440 | tf_op jit(solution)/shard_map/ppermute | solution.py:583
  17.4 12.4 %collective-permute-start.1 = (f32[256,256]{1,0:T(8,128)S(1)}, f32[256,256]{1,0:T(8,128)S(1)}, u32[]{:S(2)}, u32[]{:S(2)}) collective-permute-start(f32[256,256]{1,0:T(8,128)S(1)} %chip_maps.1._.refs_0_), channel_id=1, source_target_pairs={{0,2},{1,3},{2,0},{3,1},{4,6},{5,7},{6,4},{7,5},{8,10},{9,11},{10,... | collective-permute-start | bytes 786440 | tf_op jit(solution)/shard_map/ppermute | solution.py:583
  17.6 12.2 %copy-start.4 = (f32[256]{0:T(256)S(1)}, f32[256]{0:T(256)}, u32[]{:S(2)}) copy-start(f32[256]{0:T(256)} %param.10) | copy-start | bytes 3076
  17.6 12.2 %copy-start.5 = (f32[256]{0:T(256)S(1)}, f32[256]{0:T(256)}, u32[]{:S(2)}) copy-start(f32[256]{0:T(256)} %param.9) | copy-start | bytes 3076
  24.1 1.4 %collective-permute-start.4 = (f32[144,256]{1,0:T(8,128)S(1)}, f32[144,256]{1,0:T(8,128)S(1)}, u32[]{:S(2)}, u32[]{:S(2)}) collective-permute-start(f32[144,256]{1,0:T(8,128)S(1)} %get-tuple-element.59.own_ref), channel_id=1, source_target_pairs={{0,1},{1,0},{2,3},{3,2},{4,5},{5,4},{6,7},{7,6},{8,9},{9,8},{10,11... | collective-permute-start | bytes 442376 | tf_op jit(solution)/shard_map/ppermute | solution.py:583
  26.0 6.8 %collective-permute-start.10 = (f32[72,256]{1,0:T(8,128)S(1)}, f32[72,256]{1,0:T(8,128)S(1)}, u32[]{:S(2)}, u32[]{:S(2)}) collective-permute-start(f32[72,256]{1,0:T(8,128)S(1)} %get-tuple-element.66), channel_id=1, source_target_pairs={{0,6},{1,7},{2,4},{3,5},{4,2},{5,3},{6,0},{7,1},{8,14},{9,15},{10,... | collective-permute-start | bytes 221192 | tf_op jit(solution)/shard_map/ppermute | solution.py:583
  28.9 4.4 %collective-permute-start.8 = (f32[72,256]{1,0:T(8,128)S(1)}, f32[72,256]{1,0:T(8,128)S(1)}, u32[]{:S(2)}, u32[]{:S(2)}) collective-permute-start(f32[72,256]{1,0:T(8,128)S(1)} %get-tuple-element.66), channel_id=1, source_target_pairs={{0,4},{1,5},{2,6},{3,7},{4,0},{5,1},{6,2},{7,3},{8,12},{9,13},{10,... | collective-permute-start | bytes 221192 | tf_op jit(solution)/shard_map/ppermute | solution.py:583
  29.4 4.4 %collective-permute-start.6 = (f32[72,256]{1,0:T(8,128)S(1)}, f32[72,256]{1,0:T(8,128)S(1)}, u32[]{:S(2)}, u32[]{:S(2)}) collective-permute-start(f32[72,256]{1,0:T(8,128)S(1)} %get-tuple-element.66), channel_id=1, source_target_pairs={{0,2},{1,3},{2,0},{3,1},{4,6},{5,7},{6,4},{7,5},{8,10},{9,11},{10,... | collective-permute-start | bytes 221192 | tf_op jit(solution)/shard_map/ppermute | solution.py:583
  30.9 7.3 %collective-permute-start.5 = (f32[128,256]{1,0:T(8,128)S(1)}, f32[128,256]{1,0:T(8,128)S(1)}, u32[]{:S(2)}, u32[]{:S(2)}) collective-permute-start(f32[128,256]{1,0:T(8,128)S(1)} %get-tuple-element.65), channel_id=1, source_target_pairs={{0,8},{1,9},{2,10},{3,11},{4,12},{5,13},{6,14},{7,15},{8,0},{9,1},... | collective-permute-start | bytes 393224 | tf_op jit(solution)/shard_map/ppermute | solution.py:583
  32.8 1.3 %collective-permute-start.11 = (f32[72,256]{1,0:T(8,128)S(1)}, f32[72,256]{1,0:T(8,128)S(1)}, u32[]{:S(2)}, u32[]{:S(2)}) collective-permute-start(f32[72,256]{1,0:T(8,128)S(1)} %collective-permute-done.10.refs_5_), channel_id=1, source_target_pairs={{0,1},{1,0},{2,3},{3,2},{4,5},{5,4},{6,7},{7,6},{8,9},{9,8},{10,11... | collective-permute-start | bytes 221192 | tf_op jit(solution)/shard_map/ppermute | solution.py:583
  33.2 1.3 %collective-permute-start.9 = (f32[72,256]{1,0:T(8,128)S(1)}, f32[72,256]{1,0:T(8,128)S(1)}, u32[]{:S(2)}, u32[]{:S(2)}) collective-permute-start(f32[72,256]{1,0:T(8,128)S(1)} %collective-permute-done.8.refs_3_), channel_id=1, source_target_pairs={{0,1},{1,0},{2,3},{3,2},{4,5},{5,4},{6,7},{7,6},{8,9},{9,8},{10,11... | collective-permute-start | bytes 221192 | tf_op jit(solution)/shard_map/ppermute | solution.py:583
  33.8 1.3 %collective-permute-start.7 = (f32[72,256]{1,0:T(8,128)S(1)}, f32[72,256]{1,0:T(8,128)S(1)}, u32[]{:S(2)}, u32[]{:S(2)}) collective-permute-start(f32[72,256]{1,0:T(8,128)S(1)} %collective-permute-done.6.refs_1_), channel_id=1, source_target_pairs={{0,1},{1,0},{2,3},{3,2},{4,5},{5,4},{6,7},{7,6},{8,9},{9,8},{10,11... | collective-permute-start | bytes 221192 | tf_op jit(solution)/shard_map/ppermute | solution.py:583
  36.6 6.0 %collective-permute-start.13 = (f32[144,256]{1,0:T(8,128)S(1)}, f32[144,256]{1,0:T(8,128)S(1)}, u32[]{:S(2)}, u32[]{:S(2)}) collective-permute-start(f32[144,256]{1,0:T(8,128)S(1)} %get-tuple-element.73.own_ref), channel_id=1, source_target_pairs={{0,8},{1,9},{2,10},{3,11},{4,12},{5,13},{6,14},{7,15},{8,0},{9,1},... | collective-permute-start | bytes 442376 | tf_op jit(solution)/shard_map/ppermute | solution.py:583
  38.3 4.3 %collective-permute-start.12 = (f32[128,256]{1,0:T(8,128)S(1)}, f32[128,256]{1,0:T(8,128)S(1)}, u32[]{:S(2)}, u32[]{:S(2)}) collective-permute-start(f32[128,256]{1,0:T(8,128)S(1)} %collective-permute-done.5.r_ref.refs_0_), channel_id=1, source_target_pairs={{0,1},{1,0},{2,3},{3,2},{4,5},{5,4},{6,7},{7,6},{8,9},{9,8},{10,11... | collective-permute-start | bytes 393224 | tf_op jit(solution)/shard_map/ppermute | solution.py:583
  43.1 5.6 %collective-permute-start.14 = (f32[72,256]{1,0:T(8,128)S(1)}, f32[72,256]{1,0:T(8,128)S(1)}, u32[]{:S(2)}, u32[]{:S(2)}) collective-permute-start(f32[72,256]{1,0:T(8,128)S(1)} %level.1.token_ref), channel_id=1, source_target_pairs={{0,16},{1,17},{2,18},{3,19},{4,20},{5,21},{6,22},{7,23},{8,24},{9,... | collective-permute-start | bytes 221192 | tf_op jit(solution)/shard_map/ppermute | solution.py:583
  48.7 1.3 %collective-permute-start.15 = (f32[72,256]{1,0:T(8,128)S(1)}, f32[72,256]{1,0:T(8,128)S(1)}, u32[]{:S(2)}, u32[]{:S(2)}) collective-permute-start(f32[72,256]{1,0:T(8,128)S(1)} %collective-permute-done.14.refs_24_), channel_id=1, source_target_pairs={{0,1},{1,0},{2,3},{3,2},{4,5},{5,4},{6,7},{7,6},{8,9},{9,8},{10,11... | collective-permute-start | bytes 221192 | tf_op jit(solution)/shard_map/ppermute | solution.py:583

commit v6 on v5

--- a/solution.py
+++ b/solution.py
@@ -443,52 +443,44 @@
     row_ref[0:1, :], col_ref[...], rest_ref[...] = apart(before[0])
 
 
-def turn_kernel(sub, g_ref, delta_ref, token_ref, high_ref, low_ref, diag_ref):
-    steps, n = high_ref.shape[:2]
-    eye = eye_mask(n)
-
-    def step(j, carry):
-        turned = g_ref[sub, j].T
-        diag_ref[pl.ds(j, 1), :] = delta_ref[pl.ds(sub * steps + j, 1), :] + diag_row(turned)
-        high_ref[j], low_ref[j] = halves(jnp.where(eye, 0.0, turned))
-        return carry
-
-    lax.fori_loop(0, steps, step, 0, unroll=2)
-
-
-def finish_kernel(axes, bit, parts, *refs):
-    high, low, diag = refs[:parts], refs[parts:2 * parts], refs[2 * parts:3 * parts]
-    var_ref, mean_ref, place_ref, rest_ref, col_ref, arow_ref, bmap_ref, bnoise_ref, bshift_ref, brest_ref, bcol_ref, brow_ref, r_ref, x_ref, means_ref, vars_ref, left_s, row_s = refs[3 * parts:]
-    n = left_s.shape[-1]
-    steps = high[0].shape[0]
+def finish_kernel(axes, bit, per, g_ref, delta_ref, var_ref, mean_ref, place_ref, rest_ref, col_ref, arow_ref,
+                  bmap_ref, bnoise_ref, bshift_ref, brest_ref, bcol_ref, brow_ref, r_ref, x_ref, means_ref, vars_ref,
+                  p_s, row_s, state_s):
+    parts, steps, n, _ = g_ref.shape
     rank = rank_of(axes)
     is_high = bit_of(rank, bit) == 1
-    received, moved = unpack(whole(rank % 2 == 1, r_ref, x_ref))
-    noise = conjugate((brow_ref[0:1, :], bcol_ref[...], brest_ref[...]), received)
-    state = jnp.where(is_high, noise, 0.0) + bnoise_ref[...]
-    moved = jnp.where(is_high, through(bmap_ref[...], moved), 0.0) + bshift_ref[0:1, :]
+    state_s[0:n, :] = bnoise_ref[...]
+    state_s[n:, :] = bshift_ref[0:8, :]
+
+    @pl.when(is_high)
+    def _():
+        received, moved = unpack(whole(rank % 2 == 1, r_ref, x_ref))
+        state_s[0:n, :] += conjugate((brow_ref[0:1, :], bcol_ref[...], brest_ref[...]), received)
+        state_s[n:, :] += through(bmap_ref[...], moved)
+
+    state, moved = state_s[0:n, :], state_s[n:n + 1, :]
     for s in range(parts):
         p = conjugate((arow_ref[s, 0:1, :], col_ref[s], rest_ref[s]), state) + place_ref[s, n:2 * n, :]
         mean = through(place_ref[s, 0:n, :], moved) + place_ref[s, 2 * n:2 * n + 1, :]
-        mh, ml = halves(mean)
-        left_s[s, 0:n, :] = p.astype(bf16)
-        left_s[s, n:, :] = jnp.concatenate([mh, ml, jnp.zeros((14, n), bf16)], axis=0)
+        p_s[s] = p.astype(bf16)
         row_s[s, 0:1, :] = mean
         row_s[s, 1:2, :] = diag_row(p)
 
-    def step(j, carry):
-        both = [nn(left_s[s], high[s][j]) for s in range(parts)]
-        rest = [nn(left_s[s, n:, :], low[s][j]) for s in range(parts)]
-        for s in range(parts):
-            t = s * steps + j
-            d = diag[s][pl.ds(j, 1), :]
-            vars_ref[pl.ds(t, 1), :] = (var_ref[pl.ds(t, 1), :] + d * (d * row_s[s, 1:2, :] + 2.0 * diag_row(both[s]))
-                                        + jnp.sum(high[s][j].astype(f32) * both[s][:n], axis=0, keepdims=True))
-            means_ref[pl.ds(t, 1), :] = (mean_ref[pl.ds(t, 1), :] + d * row_s[s, 0:1, :]
-                                         + both[s][n:n + 1] + (both[s][n + 1:n + 2] + rest[s][0:1]))
+    def step(k, carry):
+        s, j = k // (steps // per), (k % (steps // per)) * per
+        g = g_ref[s, pl.ds(j, per)]
+        both = nn(g.reshape(per * n, n).astype(bf16), p_s[s])
+        mean, spread_of = row_s[s, 0:1, :], row_s[s, 1:2, :]
+        for i in range(per):
+            t = s * steps + j + i
+            d = delta_ref[pl.ds(t, 1), :]
+            w = both[i * n:(i + 1) * n]
+            vars_ref[pl.ds(t, 1), :] = (var_ref[pl.ds(t, 1), :] + d * (d * spread_of + 2.0 * diag_row(w))
+                                        + row_of(jnp.sum(g[i] * w, axis=1, keepdims=True)))
+            means_ref[pl.ds(t, 1), :] = mean_ref[pl.ds(t, 1), :] + d * mean + through(g[i], mean)
         return carry
 
-    lax.fori_loop(0, steps, step, 0, unroll=4)
+    lax.fori_loop(0, parts * steps // per, step, 0)
 
 
 def vmem():
@@ -554,20 +546,12 @@
                 [pltpu.VMEM((subs, n, n), f32)])
 
 
-def turn(sub, g, delta, token):
-    _, steps, n, _ = g.shape
-    return call(functools.partial(turn_kernel, sub), "turn",
-                [shape(steps, n, n, dtype=bf16), shape(steps, n, n, dtype=bf16), shape(steps, n)],
-                [g, delta, token], [vmem()] * 2 + [anywhere()], flops=10 ** 5)
-
-
-def finish(axes, bit, turned, var, mean, placed, before, r, x):
-    parts = len(turned)
+def finish(axes, bit, g, delta, var, mean, placed, before, r, x, per=8):
+    parts = g.shape[0]
     T, n = var.shape
-    high, low, diag = zip(*turned)
-    return call(functools.partial(finish_kernel, axes, bit, parts), "finish", [shape(T, n)] * 2,
-                [*high, *low, *diag, var, mean, *placed, *before, r, x],
-                scratch=[pltpu.VMEM((parts, n + 16, n), bf16), pltpu.VMEM((parts, 8, n), f32)])
+    return call(functools.partial(finish_kernel, axes, bit, per), "finish", [shape(T, n)] * 2,
+                [g, delta, var, mean, *placed, *before, r, x],
+                scratch=[pltpu.VMEM((parts, n, n), bf16), pltpu.VMEM((parts, 8, n), f32), pltpu.VMEM((n + 8, n), f32)])
 
 
 def per_device(axes, init_mean, init_var, decay, coupling, obs_map, gain, noise_factor, obs_var, observed):
@@ -631,9 +615,8 @@
     before = call(functools.partial(before_kernel, axes, bits[:-1]), "before",
                   [shape(n, n), shape(n, n), shape(16, n), shape(n, n, dtype=bf16), shape(n, 128), shape(8, n)],
                   [init_var.reshape(1, n), init_mean.reshape(1, n), *received])
-    turned = [turn(k, g, delta, packed) for k in range(subs)]
-    r, *_ = lax.optimization_barrier((swap(packed, bits[-1]), *before, *(x[2] for x in turned[:3])))
-    return tuple(finish(axes, bits[-1], turned, diag, shift, placed, before, r, swap(r, 1)))
+    r, *_ = lax.optimization_barrier((swap(packed, bits[-1]), *before))
+    return tuple(finish(axes, bits[-1], g, delta, diag, shift, placed, before, r, swap(r, 1)))
 
 
 def solution(mesh):

time: 54.2 us -> 54.2 us (level)
  Pallas kernels: 33.6 us -> 30 us
  waiting for transfers between devices: 5 us -> 8.6 us
    ppermute x16, waiting for transfers between devices: 5 us -> 8.6 us  [swap(): return lax.ppermute(x, names, [(k, k ^ bit) for k in range(count)])]
    pallas_call x15 -> x11, Pallas kernels: 33.6 us -> 30 us  [call(): pl.pallas_call(kernel, in_specs=specs or [vmem()] * len(args), out_specs=...]
  transfers between devices with their start and end apart: 16 -> 16, of which waited for: 10 -> 10; matrix products, arithmetic and copies ran while one was open for 0% -> 0% of each run, Pallas kernels for 35% -> 29%
where the time goes in v6:
time: 54.2 us; the launch traced here: 54 us
  Pallas kernels  30 us (55%)
  starting transfers between devices  14.6 us (27%)
  waiting for transfers between devices  8.6 us (16%)
  between operations  0.77 us (1%)
    pallas_call x11, Pallas kernels, call(): pl.pallas_call(kernel, in_specs=specs or [vmem()] * len(args), out_specs=...  30 us
    ppermute x16, starting transfers between devices, swap(): return lax.ppermute(x, names, [(k, k ^ bit) for k in range(count)])  14.6 us
    ppermute x16, waiting for transfers between devices, swap(): return lax.ppermute(x, names, [(k, k ^ bit) for k in range(count)])  8.6 us
  transfers between devices with their start and end apart: 16, of which 10 were waited for; matrix products, arithmetic and copies ran while one was open for 0% of the time, Pallas kernels for 29%

profile of v6, /device:TPU:0, one launch (start us, length us, event | category | flops | bytes accessed | tf_op | source)
XLA Modules:
  0.0 54.0 jit_solution(14110274371282313963)
XLA Ops:
  0.6 0.0 copy-start
  0.6 0.0 copy-start.1
  0.7 0.0 copy-start.2
  0.7 9.7 %step_maps.1 = (f32[4,8,256,256]{3,2,1,0:T(8,128)S(1)}, bf16[4,8,256,256]{3,2,1,0:T(8,128)(2,1)S(1)}, f32[4,8,256,128]{3,2,1,0:T(8,128)S(1)}, f32[32,256]{1,0:T(...) custom-call(f32[32,256]{1,0:T(8,128)} %decay_ref.1, ...), custom_call_target="tpu_custom_call" | custom-call | flops 10000000000 | tf_op jit(solution)/shard_map/step_maps/pallas_call | solution.py:499
  10.4 0.5 collective-permute-start
  10.9 0.0 copy-start.6
  10.9 2.1 %step_shapes.1._.shaped_ref = bf16[4,8,256,256]{3,2,1,0:T(8,128)(2,1)S(1)} custom-call(bf16[4,8,64,256]{3,2,1,0:T(8,128)(2,1)S(1)} %bitcast.10, bf16[4,8,64,256]{3,2,1,0:T(8,128)(2,1)S(1)} %bitcast.7, bf16[256,256]{1,0:T(8,128)(2,1)S(1)} %copy-done.2, f32[32,256]{1,0:T(8,128)S(1)} %get-tuple-element.41._.delta_ref), custom_call_target="tpu_custom_call" | custom-call | flops 100000 | tf_op jit(solution)/shard_map/step_shapes/pallas_call | solution.py:499
  13.0 0.0 collective-permute-done.other_ref.other_map_ref.refs_4_
  13.1 0.3 chip_maps.1._.refs_0_
  13.4 3.5 %collective-permute-start.3 = (f32[256,256]{1,0:T(8,128)S(1)}, f32[256,256]{1,0:T(8,128)S(1)}, u32[]{:S(2)}, u32[]{:S(2)}) collective-permute-start(f32[256,256]{1,0:T(8,128)S(1)} %chip_maps.1._.refs_0_), channel_id=1, source_target_pairs={{0,6},{1,7},{2,4},{3,5},{4,2},{5,3},{6,0},{7,1},{8,14},{9,15},{10,... | collective-permute-start | bytes 786440 | tf_op jit(solution)/shard_map/ppermute | solution.py:567
  16.9 0.5 collective-permute-start.2
  17.4 0.1 collective-permute-start.1
  17.6 0.0 copy-done.6
  17.6 6.5 %step_noises.1 = (f32[32,256]{1,0:T(8,128)S(1)}, f32[4,272,256]{2,1,0:T(8,128)S(1)}, f32[144,256]{1,0:T(8,128)S(1)}) custom-call(f32[32,256]{1,0:T(8,128)S(1)} %copy-done.3, bf16[4,8,256,256]{3,2,1,0:T(8,128)(2,1)S(1)} %get-tuple-element.42.e_ref, f32[4,8,256,128]{3,2,1,0:T(8,128)S(1)} %get-tuple-element.43.dcol_ref, ...), custom_call_target="tpu_custom_call" | custom-call | flops 100000 | tf_op jit(solution)/shard_map/step_noises/pallas_call | solution.py:499
  24.1 0.1 collective-permute-start.4
  24.2 1.4 %collective-permute-done.4.other_ref.refs_12_ = f32[144,256]{1,0:T(8,128)S(1)} collective-permute-done((f32[144,256]{1,0:T(8,128)S(1)}, f32[144,256]{1,0:T(8,128)S(1)}, u32[]{:S(2)}, u32[]{:S(2)}) %collective-permute-start.4) | collective-permute-done | bytes 147488 | tf_op jit(solution)/shard_map/ppermute | solution.py:567
  25.5 0.5 core_noises.1
  26.0 2.9 %collective-permute-start.9 = (f32[72,256]{1,0:T(8,128)S(1)}, f32[72,256]{1,0:T(8,128)S(1)}, u32[]{:S(2)}, u32[]{:S(2)}) collective-permute-start(f32[72,256]{1,0:T(8,128)S(1)} %get-tuple-element.55), channel_id=1, source_target_pairs={{0,6},{1,7},{2,4},{3,5},{4,2},{5,3},{6,0},{7,1},{8,14},{9,15},{10,... | collective-permute-start | bytes 221192 | tf_op jit(solution)/shard_map/ppermute | solution.py:567
  28.9 0.5 collective-permute-start.7
  29.4 0.0 collective-permute-done.3.refs_3_
  29.4 0.1 collective-permute-start.5
  29.6 0.0 collective-permute-done.2.refs_2_
  29.6 0.2 collective-permute-done.1.refs_1_
  29.8 1.1 %plane_maps.1 = (f32[3,256,256]{2,1,0:T(8,128)S(1)}, bf16[3,256,256]{2,1,0:T(8,128)(2,1)S(1)}, f32[3,256,128]{2,1,0:T(8,128)S(1)}, f32[8,256]{1,0:T(8,128)S(1)},...) custom-call(f32[256,256]{1,0:T(8,128)S(1)} %chip_maps.1._.refs_0_, ...), custom_call_target="tpu_custom_call" | custom-call | flops 100000 | tf_op jit(solution)/shard_map/plane_maps/pallas_call | solution.py:499
  30.9 1.9 %collective-permute-start.11 = (f32[128,256]{1,0:T(8,128)S(1)}, f32[128,256]{1,0:T(8,128)S(1)}, u32[]{:S(2)}, u32[]{:S(2)}) collective-permute-start(f32[128,256]{1,0:T(8,128)S(1)} %get-tuple-element.66), channel_id=1, source_target_pairs={{0,8},{1,9},{2,10},{3,11},{4,12},{5,13},{6,14},{7,15},{8,0},{9,1},... | collective-permute-start | bytes 393224 | tf_op jit(solution)/shard_map/ppermute | solution.py:567
  32.8 0.0 collective-permute-done.9.refs_5_
  32.8 0.0 collective-permute-start.10
  32.8 0.4 collective-permute-done.7.refs_3_
  33.2 0.1 collective-permute-start.8
  33.3 0.4 collective-permute-done.5.refs_1_
  33.8 0.0 collective-permute-start.6
  33.8 0.3 collective-permute-done.10.refs_6_
  34.1 0.4 collective-permute-done.8.refs_4_
  34.5 0.5 collective-permute-done.6.refs_2_
  35.0 1.6 %plane_noises.1 = (f32[144,256]{1,0:T(8,128)S(1)}, f32[3,272,256]{2,1,0:T(8,128)S(1)}) custom-call(f32[144,256]{1,0:T(8,128)S(1)} %get-tuple-element.50.refs_0_, f32[72,256]{1,0:T(8,128)S(1)} %collective-permute-done.5.refs_1_, f32[72,256]{1,0:T(8,128)S(1)} %collective-permute-done.6.refs_2_, f32[72,256]{1,0:T(8,128)S(1)} %collective-permute-done.7.refs_3_, ...), custom_call_target="tpu_custom_call" | custom-call | flops 100000 | tf_op jit(solution)/shard_map/plane_noises/pallas_call | solution.py:499
  36.6 1.6 %collective-permute-start.13 = (f32[144,256]{1,0:T(8,128)S(1)}, f32[144,256]{1,0:T(8,128)S(1)}, u32[]{:S(2)}, u32[]{:S(2)}) collective-permute-start(f32[144,256]{1,0:T(8,128)S(1)} %get-tuple-element.76.own_ref), channel_id=1, source_target_pairs={{0,8},{1,9},{2,10},{3,11},{4,12},{5,13},{6,14},{7,15},{8,0},{9,1},... | collective-permute-start | bytes 442376 | tf_op jit(solution)/shard_map/ppermute | solution.py:567
  38.2 0.0 collective-permute-done.11.refs_0_.r_ref
  38.2 0.0 collective-permute-start.12
  38.3 3.4 %place.1 = (f32[4,528,256]{2,1,0:T(8,128)S(1)}, bf16[4,256,256]{2,1,0:T(8,128)(2,1)S(1)}, f32[4,256,128]{2,1,0:T(8,128)S(1)}, f32[4,8,256]{2,1,0:T(8,128)S(1)}) custom-call(f32[6,256,256]{2,1,0:T(8,128)S(1)} %get-tuple-element.45.maps_ref.subs_ref, f32[4,272,256]{2,1,0:T(8,128)S(1)} %get-tuple-element.48.sub_noises_ref, ...), custom_call_target="tpu_custom_call" | custom-call | flops 100000 | tf_op jit(solution)/shard_map/place/pallas_call | solution.py:499
  41.7 0.9 %collective-permute-done.13.refs_2_.other_ref = f32[144,256]{1,0:T(8,128)S(1)} collective-permute-done((f32[144,256]{1,0:T(8,128)S(1)}, f32[144,256]{1,0:T(8,128)S(1)}, u32[]{:S(2)}, u32[]{:S(2)}) %collective-permute-start.13) | collective-permute-done | bytes 147488 | tf_op jit(solution)/shard_map/ppermute | solution.py:567
  42.6 0.0 collective-permute-done.12.refs_1_.x_ref
  42.6 0.5 level.1
  43.1 2.7 %collective-permute-start.14 = (f32[72,256]{1,0:T(8,128)S(1)}, f32[72,256]{1,0:T(8,128)S(1)}, u32[]{:S(2)}, u32[]{:S(2)}) collective-permute-start(f32[72,256]{1,0:T(8,128)S(1)} %level.1), channel_id=1, source_target_pairs={{0,16},{1,17},{2,18},{3,19},{4,20},{5,21},{6,22},{7,23},{8,24},{9,... | collective-permute-start | bytes 221192 | tf_op jit(solution)/shard_map/ppermute | solution.py:567
  45.7 0.2 before.1
  45.9 2.7 %collective-permute-done.14.r_ref = f32[72,256]{1,0:T(8,128)S(1)} collective-permute-done((f32[72,256]{1,0:T(8,128)S(1)}, f32[72,256]{1,0:T(8,128)S(1)}, u32[]{:S(2)}, u32[]{:S(2)}) %collective-permute-start.14) | collective-permute-done | bytes 73760 | tf_op jit(solution)/shard_map/ppermute | solution.py:567
  48.6 0.0 collective-permute-start.15
  48.6 1.3 %collective-permute-done.15.x_ref = f32[72,256]{1,0:T(8,128)S(1)} collective-permute-done((f32[72,256]{1,0:T(8,128)S(1)}, f32[72,256]{1,0:T(8,128)S(1)}, u32[]{:S(2)}, u32[]{:S(2)}) %collective-permute-start.15) | collective-permute-done | bytes 73760 | tf_op jit(solution)/shard_map/ppermute | solution.py:567
  49.9 4.1 %finish.1 = (f32[32,256]{1,0:T(8,128)}, f32[32,256]{1,0:T(8,128)}) custom-call(f32[4,8,256,256]{3,2,1,0:T(8,128)S(1)} %get-tuple-element.40.g_ref, f32[32,256]{1,0:T(8,128)S(1)} %get-tuple-element.41._.delta_ref, f32[32,256]{1,0:T(8,128)S(1)} %get-tuple-element.47.var_ref, f32[32,256]{1,0:T(8,128)S(1)} %get-tuple-element.44.shift_ref.mean_ref, ...), custom_call_target="tpu_custom_call" | custom-call | flops 100000 | tf_op jit(solution)/shard_map/finish/pallas_call | solution.py:499
  (9 shorter events, 0.0 us)
Async XLA Ops:
  0.6 10.3 %copy-start = (bf16[32,64,256]{2,1,0:T(8,128)(2,1)S(1)}, bf16[32,64,256]{2,1,0:T(8,128)(2,1)}, u32[]{:S(2)}) copy-start(bf16[32,64,256]{2,1,0:T(8,128)(2,1)} %param.14) | copy-start | bytes 3145732
  0.6 10.3 %copy-start.1 = (bf16[32,64,256]{2,1,0:T(8,128)(2,1)S(1)}, bf16[32,64,256]{2,1,0:T(8,128)(2,1)}, u32[]{:S(2)}) copy-start(bf16[32,64,256]{2,1,0:T(8,128)(2,1)} %param.13) | copy-start | bytes 3145732
  0.7 10.3 %copy-start.2 = (bf16[256,256]{1,0:T(8,128)(2,1)S(1)}, bf16[256,256]{1,0:T(8,128)(2,1)}, u32[]{:S(2)}) copy-start(bf16[256,256]{1,0:T(8,128)(2,1)} %nf_ref.1) | copy-start | bytes 393220
  10.4 2.7 %collective-permute-start = (f32[256,256]{1,0:T(8,128)S(1)}, f32[256,256]{1,0:T(8,128)S(1)}, u32[]{:S(2)}, u32[]{:S(2)}) collective-permute-start(f32[256,256]{1,0:T(8,128)S(1)} %get-tuple-element.46.own_ref.own_map_ref), channel_id=1, source_target_pairs={{0,1},{1,0},{2,3},{3,2},{4,5},{5,4},{6,7},{7,6},{8,9},{9,8},{10,11... | collective-permute-start | bytes 786440 | tf_op jit(solution)/shard_map/ppermute | solution.py:567
  10.9 6.7 %copy-start.3 = (f32[32,256]{1,0:T(8,128)S(1)}, f32[32,256]{1,0:T(8,128)}, u32[]{:S(2)}) copy-start(f32[32,256]{1,0:T(8,128)} %decay_ref.1) | copy-start | bytes 98308
  10.9 6.7 %copy-start.6 = (f32[64]{0:T(128)S(1)}, f32[64]{0:T(128)}, u32[]{:S(2)}) copy-start(f32[64]{0:T(128)} %param.16) | copy-start | bytes 772
  13.4 16.0 %collective-permute-start.3 = (f32[256,256]{1,0:T(8,128)S(1)}, f32[256,256]{1,0:T(8,128)S(1)}, u32[]{:S(2)}, u32[]{:S(2)}) collective-permute-start(f32[256,256]{1,0:T(8,128)S(1)} %chip_maps.1._.refs_0_), channel_id=1, source_target_pairs={{0,6},{1,7},{2,4},{3,5},{4,2},{5,3},{6,0},{7,1},{8,14},{9,15},{10,... | collective-permute-start | bytes 786440 | tf_op jit(solution)/shard_map/ppermute | solution.py:567
  16.9 12.6 %collective-permute-start.2 = (f32[256,256]{1,0:T(8,128)S(1)}, f32[256,256]{1,0:T(8,128)S(1)}, u32[]{:S(2)}, u32[]{:S(2)}) collective-permute-start(f32[256,256]{1,0:T(8,128)S(1)} %chip_maps.1._.refs_0_), channel_id=1, source_target_pairs={{0,4},{1,5},{2,6},{3,7},{4,0},{5,1},{6,2},{7,3},{8,12},{9,13},{10,... | collective-permute-start | bytes 786440 | tf_op jit(solution)/shard_map/ppermute | solution.py:567
  17.4 12.4 %collective-permute-start.1 = (f32[256,256]{1,0:T(8,128)S(1)}, f32[256,256]{1,0:T(8,128)S(1)}, u32[]{:S(2)}, u32[]{:S(2)}) collective-permute-start(f32[256,256]{1,0:T(8,128)S(1)} %chip_maps.1._.refs_0_), channel_id=1, source_target_pairs={{0,2},{1,3},{2,0},{3,1},{4,6},{5,7},{6,4},{7,5},{8,10},{9,11},{10,... | collective-permute-start | bytes 786440 | tf_op jit(solution)/shard_map/ppermute | solution.py:567
  17.6 12.2 %copy-start.4 = (f32[256]{0:T(256)S(1)}, f32[256]{0:T(256)}, u32[]{:S(2)}) copy-start(f32[256]{0:T(256)} %param.10) | copy-start | bytes 3076
  17.6 12.2 %copy-start.5 = (f32[256]{0:T(256)S(1)}, f32[256]{0:T(256)}, u32[]{:S(2)}) copy-start(f32[256]{0:T(256)} %param.9) | copy-start | bytes 3076
  24.1 1.4 %collective-permute-start.4 = (f32[144,256]{1,0:T(8,128)S(1)}, f32[144,256]{1,0:T(8,128)S(1)}, u32[]{:S(2)}, u32[]{:S(2)}) collective-permute-start(f32[144,256]{1,0:T(8,128)S(1)} %get-tuple-element.49.own_ref), channel_id=1, source_target_pairs={{0,1},{1,0},{2,3},{3,2},{4,5},{5,4},{6,7},{7,6},{8,9},{9,8},{10,11... | collective-permute-start | bytes 442376 | tf_op jit(solution)/shard_map/ppermute | solution.py:567
  26.0 6.8 %collective-permute-start.9 = (f32[72,256]{1,0:T(8,128)S(1)}, f32[72,256]{1,0:T(8,128)S(1)}, u32[]{:S(2)}, u32[]{:S(2)}) collective-permute-start(f32[72,256]{1,0:T(8,128)S(1)} %get-tuple-element.55), channel_id=1, source_target_pairs={{0,6},{1,7},{2,4},{3,5},{4,2},{5,3},{6,0},{7,1},{8,14},{9,15},{10,... | collective-permute-start | bytes 221192 | tf_op jit(solution)/shard_map/ppermute | solution.py:567
  28.9 4.4 %collective-permute-start.7 = (f32[72,256]{1,0:T(8,128)S(1)}, f32[72,256]{1,0:T(8,128)S(1)}, u32[]{:S(2)}, u32[]{:S(2)}) collective-permute-start(f32[72,256]{1,0:T(8,128)S(1)} %get-tuple-element.55), channel_id=1, source_target_pairs={{0,4},{1,5},{2,6},{3,7},{4,0},{5,1},{6,2},{7,3},{8,12},{9,13},{10,... | collective-permute-start | bytes 221192 | tf_op jit(solution)/shard_map/ppermute | solution.py:567
  29.4 4.4 %collective-permute-start.5 = (f32[72,256]{1,0:T(8,128)S(1)}, f32[72,256]{1,0:T(8,128)S(1)}, u32[]{:S(2)}, u32[]{:S(2)}) collective-permute-start(f32[72,256]{1,0:T(8,128)S(1)} %get-tuple-element.55), channel_id=1, source_target_pairs={{0,2},{1,3},{2,0},{3,1},{4,6},{5,7},{6,4},{7,5},{8,10},{9,11},{10,... | collective-permute-start | bytes 221192 | tf_op jit(solution)/shard_map/ppermute | solution.py:567
  30.9 7.3 %collective-permute-start.11 = (f32[128,256]{1,0:T(8,128)S(1)}, f32[128,256]{1,0:T(8,128)S(1)}, u32[]{:S(2)}, u32[]{:S(2)}) collective-permute-start(f32[128,256]{1,0:T(8,128)S(1)} %get-tuple-element.66), channel_id=1, source_target_pairs={{0,8},{1,9},{2,10},{3,11},{4,12},{5,13},{6,14},{7,15},{8,0},{9,1},... | collective-permute-start | bytes 393224 | tf_op jit(solution)/shard_map/ppermute | solution.py:567
  32.8 1.3 %collective-permute-start.10 = (f32[72,256]{1,0:T(8,128)S(1)}, f32[72,256]{1,0:T(8,128)S(1)}, u32[]{:S(2)}, u32[]{:S(2)}) collective-permute-start(f32[72,256]{1,0:T(8,128)S(1)} %collective-permute-done.9.refs_5_), channel_id=1, source_target_pairs={{0,1},{1,0},{2,3},{3,2},{4,5},{5,4},{6,7},{7,6},{8,9},{9,8},{10,11... | collective-permute-start | bytes 221192 | tf_op jit(solution)/shard_map/ppermute | solution.py:567
  33.2 1.3 %collective-permute-start.8 = (f32[72,256]{1,0:T(8,128)S(1)}, f32[72,256]{1,0:T(8,128)S(1)}, u32[]{:S(2)}, u32[]{:S(2)}) collective-permute-start(f32[72,256]{1,0:T(8,128)S(1)} %collective-permute-done.7.refs_3_), channel_id=1, source_target_pairs={{0,1},{1,0},{2,3},{3,2},{4,5},{5,4},{6,7},{7,6},{8,9},{9,8},{10,11... | collective-permute-start | bytes 221192 | tf_op jit(solution)/shard_map/ppermute | solution.py:567
  33.8 1.3 %collective-permute-start.6 = (f32[72,256]{1,0:T(8,128)S(1)}, f32[72,256]{1,0:T(8,128)S(1)}, u32[]{:S(2)}, u32[]{:S(2)}) collective-permute-start(f32[72,256]{1,0:T(8,128)S(1)} %collective-permute-done.5.refs_1_), channel_id=1, source_target_pairs={{0,1},{1,0},{2,3},{3,2},{4,5},{5,4},{6,7},{7,6},{8,9},{9,8},{10,11... | collective-permute-start | bytes 221192 | tf_op jit(solution)/shard_map/ppermute | solution.py:567
  36.6 6.0 %collective-permute-start.13 = (f32[144,256]{1,0:T(8,128)S(1)}, f32[144,256]{1,0:T(8,128)S(1)}, u32[]{:S(2)}, u32[]{:S(2)}) collective-permute-start(f32[144,256]{1,0:T(8,128)S(1)} %get-tuple-element.76.own_ref), channel_id=1, source_target_pairs={{0,8},{1,9},{2,10},{3,11},{4,12},{5,13},{6,14},{7,15},{8,0},{9,1},... | collective-permute-start | bytes 442376 | tf_op jit(solution)/shard_map/ppermute | solution.py:567
  38.2 4.3 %collective-permute-start.12 = (f32[128,256]{1,0:T(8,128)S(1)}, f32[128,256]{1,0:T(8,128)S(1)}, u32[]{:S(2)}, u32[]{:S(2)}) collective-permute-start(f32[128,256]{1,0:T(8,128)S(1)} %collective-permute-done.11.refs_0_.r_ref), channel_id=1, source_target_pairs={{0,1},{1,0},{2,3},{3,2},{4,5},{5,4},{6,7},{7,6},{8,9},{9,8},{10,11... | collective-permute-start | bytes 393224 | tf_op jit(solution)/shard_map/ppermute | solution.py:567
  43.1 5.6 %collective-permute-start.14 = (f32[72,256]{1,0:T(8,128)S(1)}, f32[72,256]{1,0:T(8,128)S(1)}, u32[]{:S(2)}, u32[]{:S(2)}) collective-permute-start(f32[72,256]{1,0:T(8,128)S(1)} %level.1), channel_id=1, source_target_pairs={{0,16},{1,17},{2,18},{3,19},{4,20},{5,21},{6,22},{7,23},{8,24},{9,... | collective-permute-start | bytes 221192 | tf_op jit(solution)/shard_map/ppermute | solution.py:567
  48.6 1.3 %collective-permute-start.15 = (f32[72,256]{1,0:T(8,128)S(1)}, f32[72,256]{1,0:T(8,128)S(1)}, u32[]{:S(2)}, u32[]{:S(2)}) collective-permute-start(f32[72,256]{1,0:T(8,128)S(1)} %collective-permute-done.14.r_ref), channel_id=1, source_target_pairs={{0,1},{1,0},{2,3},{3,2},{4,5},{5,4},{6,7},{7,6},{8,9},{9,8},{10,11... | collective-permute-start | bytes 221192 | tf_op jit(solution)/shard_map/ppermute | solution.py:567

commit v7 on v6

--- a/solution.py
+++ b/solution.py
@@ -471,13 +471,20 @@
         g = g_ref[s, pl.ds(j, per)]
         both = nn(g.reshape(per * n, n).astype(bf16), p_s[s])
         mean, spread_of = row_s[s, 0:1, :], row_s[s, 1:2, :]
+        t = pl.multiple_of(s * steps + j, per)
+        d = delta_ref[pl.ds(t, per), :]
+        lane = lax.broadcasted_iota(jnp.int32, (n, 128), 1)
+        sums = jnp.zeros((n, 128), f32)
+        diags = []
         for i in range(per):
-            t = s * steps + j + i
-            d = delta_ref[pl.ds(t, 1), :]
             w = both[i * n:(i + 1) * n]
-            vars_ref[pl.ds(t, 1), :] = (var_ref[pl.ds(t, 1), :] + d * (d * spread_of + 2.0 * diag_row(w))
-                                        + row_of(jnp.sum(g[i] * w, axis=1, keepdims=True)))
-            means_ref[pl.ds(t, 1), :] = mean_ref[pl.ds(t, 1), :] + d * mean + through(g[i], mean)
+            diags.append(diag_row(w))
+            sums = jnp.where(lane == i, jnp.sum(g[i] * w, axis=1, keepdims=True), sums)
+            sums = jnp.where(lane == per + i, jnp.sum(g[i] * mean, axis=1, keepdims=True), sums)
+        turned = jnp.concatenate([sums[k:k + 128].T for k in range(0, n, 128)], axis=1)
+        vars_ref[pl.ds(t, per), :] = (var_ref[pl.ds(t, per), :] + turned[0:per]
+                                      + d * (d * spread_of + 2.0 * jnp.concatenate(diags, axis=0)))
+        means_ref[pl.ds(t, per), :] = mean_ref[pl.ds(t, per), :] + d * mean + turned[per:2 * per]
         return carry
 
     lax.fori_loop(0, parts * steps // per, step, 0)

time: 54.2 us -> 54.1 us (level)
  no operation moved by 1% of the time
where the time goes in v7:
time: 54.1 us; the launch traced here: 54 us
  Pallas kernels  30 us (55%)
  starting transfers between devices  14.6 us (27%)
  waiting for transfers between devices  8.6 us (16%)
  between operations  0.77 us (1%)
    pallas_call x11, Pallas kernels, call(): pl.pallas_call(kernel, in_specs=specs or [vmem()] * len(args), out_specs=...  30 us
    ppermute x16, starting transfers between devices, swap(): return lax.ppermute(x, names, [(k, k ^ bit) for k in range(count)])  14.6 us
    ppermute x16, waiting for transfers between devices, swap(): return lax.ppermute(x, names, [(k, k ^ bit) for k in range(count)])  8.6 us
  transfers between devices with their start and end apart: 16, of which 10 were waited for; matrix products, arithmetic and copies ran while one was open for 0% of the time, Pallas kernels for 29%

profile of v7, /device:TPU:0, one launch (start us, length us, event | category | flops | bytes accessed | tf_op | source)
XLA Modules:
  0.0 54.0 jit_solution(6945314669661939306)
XLA Ops:
  0.6 0.0 copy-start
  0.6 0.0 copy-start.1
  0.7 9.7 %step_maps.1 = (f32[4,8,256,256]{3,2,1,0:T(8,128)S(1)}, bf16[4,8,256,256]{3,2,1,0:T(8,128)(2,1)S(1)}, f32[4,8,256,128]{3,2,1,0:T(8,128)S(1)}, f32[32,256]{1,0:T(...) custom-call(f32[32,256]{1,0:T(8,128)} %decay_ref.1, ...), custom_call_target="tpu_custom_call" | custom-call | flops 10000000000 | tf_op jit(solution)/shard_map/step_maps/pallas_call | solution.py:506
  10.4 0.5 collective-permute-start
  10.9 0.0 copy-start.6
  10.9 2.1 %step_shapes.1._.shaped_ref = bf16[4,8,256,256]{3,2,1,0:T(8,128)(2,1)S(1)} custom-call(bf16[4,8,64,256]{3,2,1,0:T(8,128)(2,1)S(1)} %bitcast.10, bf16[4,8,64,256]{3,2,1,0:T(8,128)(2,1)S(1)} %bitcast.7, bf16[256,256]{1,0:T(8,128)(2,1)S(1)} %copy-done.2, f32[32,256]{1,0:T(8,128)S(1)} %get-tuple-element.41._.delta_ref), custom_call_target="tpu_custom_call" | custom-call | flops 100000 | tf_op jit(solution)/shard_map/step_shapes/pallas_call | solution.py:506
  13.0 0.0 collective-permute-done.other_ref.other_map_ref.refs_4_
  13.1 0.3 chip_maps.1._.refs_0_
  13.4 3.5 %collective-permute-start.3 = (f32[256,256]{1,0:T(8,128)S(1)}, f32[256,256]{1,0:T(8,128)S(1)}, u32[]{:S(2)}, u32[]{:S(2)}) collective-permute-start(f32[256,256]{1,0:T(8,128)S(1)} %chip_maps.1._.refs_0_), channel_id=1, source_target_pairs={{0,6},{1,7},{2,4},{3,5},{4,2},{5,3},{6,0},{7,1},{8,14},{9,15},{10,... | collective-permute-start | bytes 786440 | tf_op jit(solution)/shard_map/ppermute | solution.py:574
  16.9 0.5 collective-permute-start.2
  17.4 0.1 collective-permute-start.1
  17.6 0.0 copy-done.3
  17.6 6.5 %step_noises.1 = (f32[32,256]{1,0:T(8,128)S(1)}, f32[4,272,256]{2,1,0:T(8,128)S(1)}, f32[144,256]{1,0:T(8,128)S(1)}) custom-call(f32[32,256]{1,0:T(8,128)S(1)} %copy-done.3, bf16[4,8,256,256]{3,2,1,0:T(8,128)(2,1)S(1)} %get-tuple-element.42.e_ref, f32[4,8,256,128]{3,2,1,0:T(8,128)S(1)} %get-tuple-element.43.dcol_ref, ...), custom_call_target="tpu_custom_call" | custom-call | flops 100000 | tf_op jit(solution)/shard_map/step_noises/pallas_call | solution.py:506
  24.1 0.1 collective-permute-start.4
  24.2 1.4 %collective-permute-done.4.other_ref.refs_12_ = f32[144,256]{1,0:T(8,128)S(1)} collective-permute-done((f32[144,256]{1,0:T(8,128)S(1)}, f32[144,256]{1,0:T(8,128)S(1)}, u32[]{:S(2)}, u32[]{:S(2)}) %collective-permute-start.4) | collective-permute-done | bytes 147488 | tf_op jit(solution)/shard_map/ppermute | solution.py:574
  25.5 0.5 core_noises.1
  26.0 2.9 %collective-permute-start.9 = (f32[72,256]{1,0:T(8,128)S(1)}, f32[72,256]{1,0:T(8,128)S(1)}, u32[]{:S(2)}, u32[]{:S(2)}) collective-permute-start(f32[72,256]{1,0:T(8,128)S(1)} %get-tuple-element.55), channel_id=1, source_target_pairs={{0,6},{1,7},{2,4},{3,5},{4,2},{5,3},{6,0},{7,1},{8,14},{9,15},{10,... | collective-permute-start | bytes 221192 | tf_op jit(solution)/shard_map/ppermute | solution.py:574
  28.9 0.5 collective-permute-start.7
  29.4 0.0 collective-permute-done.3.refs_3_
  29.4 0.1 collective-permute-start.5
  29.6 0.0 collective-permute-done.2.refs_2_
  29.6 0.2 collective-permute-done.1.refs_1_
  29.8 0.0 copy-done.4
  29.8 1.1 %plane_maps.1 = (f32[3,256,256]{2,1,0:T(8,128)S(1)}, bf16[3,256,256]{2,1,0:T(8,128)(2,1)S(1)}, f32[3,256,128]{2,1,0:T(8,128)S(1)}, f32[8,256]{1,0:T(8,128)S(1)},...) custom-call(f32[256,256]{1,0:T(8,128)S(1)} %chip_maps.1._.refs_0_, ...), custom_call_target="tpu_custom_call" | custom-call | flops 100000 | tf_op jit(solution)/shard_map/plane_maps/pallas_call | solution.py:506
  30.9 1.9 %collective-permute-start.11 = (f32[128,256]{1,0:T(8,128)S(1)}, f32[128,256]{1,0:T(8,128)S(1)}, u32[]{:S(2)}, u32[]{:S(2)}) collective-permute-start(f32[128,256]{1,0:T(8,128)S(1)} %get-tuple-element.66), channel_id=1, source_target_pairs={{0,8},{1,9},{2,10},{3,11},{4,12},{5,13},{6,14},{7,15},{8,0},{9,1},... | collective-permute-start | bytes 393224 | tf_op jit(solution)/shard_map/ppermute | solution.py:574
  32.8 0.0 collective-permute-done.9.refs_5_
  32.8 0.0 collective-permute-start.10
  32.8 0.4 collective-permute-done.7.refs_3_
  33.2 0.1 collective-permute-start.8
  33.3 0.4 collective-permute-done.5.refs_1_
  33.8 0.0 collective-permute-start.6
  33.8 0.3 collective-permute-done.10.refs_6_
  34.1 0.4 collective-permute-done.8.refs_4_
  34.5 0.5 collective-permute-done.6.refs_2_
  35.0 1.6 %plane_noises.1 = (f32[144,256]{1,0:T(8,128)S(1)}, f32[3,272,256]{2,1,0:T(8,128)S(1)}) custom-call(f32[144,256]{1,0:T(8,128)S(1)} %get-tuple-element.50.refs_0_, f32[72,256]{1,0:T(8,128)S(1)} %collective-permute-done.5.refs_1_, f32[72,256]{1,0:T(8,128)S(1)} %collective-permute-done.6.refs_2_, f32[72,256]{1,0:T(8,128)S(1)} %collective-permute-done.7.refs_3_, ...), custom_call_target="tpu_custom_call" | custom-call | flops 100000 | tf_op jit(solution)/shard_map/plane_noises/pallas_call | solution.py:506
  36.6 1.6 %collective-permute-start.13 = (f32[144,256]{1,0:T(8,128)S(1)}, f32[144,256]{1,0:T(8,128)S(1)}, u32[]{:S(2)}, u32[]{:S(2)}) collective-permute-start(f32[144,256]{1,0:T(8,128)S(1)} %get-tuple-element.76.own_ref), channel_id=1, source_target_pairs={{0,8},{1,9},{2,10},{3,11},{4,12},{5,13},{6,14},{7,15},{8,0},{9,1},... | collective-permute-start | bytes 442376 | tf_op jit(solution)/shard_map/ppermute | solution.py:574
  38.2 0.0 collective-permute-done.11.refs_0_.r_ref
  38.2 0.0 collective-permute-start.12
  38.3 3.4 %place.1 = (f32[4,528,256]{2,1,0:T(8,128)S(1)}, bf16[4,256,256]{2,1,0:T(8,128)(2,1)S(1)}, f32[4,256,128]{2,1,0:T(8,128)S(1)}, f32[4,8,256]{2,1,0:T(8,128)S(1)}) custom-call(f32[6,256,256]{2,1,0:T(8,128)S(1)} %get-tuple-element.45.maps_ref.subs_ref, f32[4,272,256]{2,1,0:T(8,128)S(1)} %get-tuple-element.48.sub_noises_ref, ...), custom_call_target="tpu_custom_call" | custom-call | flops 100000 | tf_op jit(solution)/shard_map/place/pallas_call | solution.py:506
  41.7 0.9 %collective-permute-done.13.refs_2_.other_ref = f32[144,256]{1,0:T(8,128)S(1)} collective-permute-done((f32[144,256]{1,0:T(8,128)S(1)}, f32[144,256]{1,0:T(8,128)S(1)}, u32[]{:S(2)}, u32[]{:S(2)}) %collective-permute-start.13) | collective-permute-done | bytes 147488 | tf_op jit(solution)/shard_map/ppermute | solution.py:574
  42.6 0.0 collective-permute-done.12.refs_1_.x_ref
  42.6 0.5 level.1
  43.1 2.7 %collective-permute-start.14 = (f32[72,256]{1,0:T(8,128)S(1)}, f32[72,256]{1,0:T(8,128)S(1)}, u32[]{:S(2)}, u32[]{:S(2)}) collective-permute-start(f32[72,256]{1,0:T(8,128)S(1)} %level.1), channel_id=1, source_target_pairs={{0,16},{1,17},{2,18},{3,19},{4,20},{5,21},{6,22},{7,23},{8,24},{9,... | collective-permute-start | bytes 221192 | tf_op jit(solution)/shard_map/ppermute | solution.py:574
  45.7 0.2 before.1
  45.9 2.7 %collective-permute-done.14.r_ref = f32[72,256]{1,0:T(8,128)S(1)} collective-permute-done((f32[72,256]{1,0:T(8,128)S(1)}, f32[72,256]{1,0:T(8,128)S(1)}, u32[]{:S(2)}, u32[]{:S(2)}) %collective-permute-start.14) | collective-permute-done | bytes 73760 | tf_op jit(solution)/shard_map/ppermute | solution.py:574
  48.6 0.0 collective-permute-start.15
  48.6 1.3 %collective-permute-done.15.x_ref = f32[72,256]{1,0:T(8,128)S(1)} collective-permute-done((f32[72,256]{1,0:T(8,128)S(1)}, f32[72,256]{1,0:T(8,128)S(1)}, u32[]{:S(2)}, u32[]{:S(2)}) %collective-permute-start.15) | collective-permute-done | bytes 73760 | tf_op jit(solution)/shard_map/ppermute | solution.py:574
  49.9 4.1 %finish.1 = (f32[32,256]{1,0:T(8,128)}, f32[32,256]{1,0:T(8,128)}) custom-call(f32[4,8,256,256]{3,2,1,0:T(8,128)S(1)} %get-tuple-element.40.g_ref, f32[32,256]{1,0:T(8,128)S(1)} %get-tuple-element.41._.delta_ref, f32[32,256]{1,0:T(8,128)S(1)} %get-tuple-element.47.var_ref, f32[32,256]{1,0:T(8,128)S(1)} %get-tuple-element.44.shift_ref.mean_ref, ...), custom_call_target="tpu_custom_call" | custom-call | flops 100000 | tf_op jit(solution)/shard_map/finish/pallas_call | solution.py:506
  (9 shorter events, 0.0 us)
Async XLA Ops:
  0.6 10.3 %copy-start = (bf16[32,64,256]{2,1,0:T(8,128)(2,1)S(1)}, bf16[32,64,256]{2,1,0:T(8,128)(2,1)}, u32[]{:S(2)}) copy-start(bf16[32,64,256]{2,1,0:T(8,128)(2,1)} %param.14) | copy-start | bytes 3145732
  0.6 10.3 %copy-start.1 = (bf16[32,64,256]{2,1,0:T(8,128)(2,1)S(1)}, bf16[32,64,256]{2,1,0:T(8,128)(2,1)}, u32[]{:S(2)}) copy-start(bf16[32,64,256]{2,1,0:T(8,128)(2,1)} %param.13) | copy-start | bytes 3145732
  0.7 10.3 %copy-start.2 = (bf16[256,256]{1,0:T(8,128)(2,1)S(1)}, bf16[256,256]{1,0:T(8,128)(2,1)}, u32[]{:S(2)}) copy-start(bf16[256,256]{1,0:T(8,128)(2,1)} %nf_ref.1) | copy-start | bytes 393220
  10.4 2.7 %collective-permute-start = (f32[256,256]{1,0:T(8,128)S(1)}, f32[256,256]{1,0:T(8,128)S(1)}, u32[]{:S(2)}, u32[]{:S(2)}) collective-permute-start(f32[256,256]{1,0:T(8,128)S(1)} %get-tuple-element.46.own_ref.own_map_ref), channel_id=1, source_target_pairs={{0,1},{1,0},{2,3},{3,2},{4,5},{5,4},{6,7},{7,6},{8,9},{9,8},{10,11... | collective-permute-start | bytes 786440 | tf_op jit(solution)/shard_map/ppermute | solution.py:574
  10.9 6.7 %copy-start.3 = (f32[32,256]{1,0:T(8,128)S(1)}, f32[32,256]{1,0:T(8,128)}, u32[]{:S(2)}) copy-start(f32[32,256]{1,0:T(8,128)} %decay_ref.1) | copy-start | bytes 98308
  10.9 6.7 %copy-start.6 = (f32[64]{0:T(128)S(1)}, f32[64]{0:T(128)}, u32[]{:S(2)}) copy-start(f32[64]{0:T(128)} %param.16) | copy-start | bytes 772
  13.4 16.0 %collective-permute-start.3 = (f32[256,256]{1,0:T(8,128)S(1)}, f32[256,256]{1,0:T(8,128)S(1)}, u32[]{:S(2)}, u32[]{:S(2)}) collective-permute-start(f32[256,256]{1,0:T(8,128)S(1)} %chip_maps.1._.refs_0_), channel_id=1, source_target_pairs={{0,6},{1,7},{2,4},{3,5},{4,2},{5,3},{6,0},{7,1},{8,14},{9,15},{10,... | collective-permute-start | bytes 786440 | tf_op jit(solution)/shard_map/ppermute | solution.py:574
  16.9 12.6 %collective-permute-start.2 = (f32[256,256]{1,0:T(8,128)S(1)}, f32[256,256]{1,0:T(8,128)S(1)}, u32[]{:S(2)}, u32[]{:S(2)}) collective-permute-start(f32[256,256]{1,0:T(8,128)S(1)} %chip_maps.1._.refs_0_), channel_id=1, source_target_pairs={{0,4},{1,5},{2,6},{3,7},{4,0},{5,1},{6,2},{7,3},{8,12},{9,13},{10,... | collective-permute-start | bytes 786440 | tf_op jit(solution)/shard_map/ppermute | solution.py:574
  17.4 12.4 %collective-permute-start.1 = (f32[256,256]{1,0:T(8,128)S(1)}, f32[256,256]{1,0:T(8,128)S(1)}, u32[]{:S(2)}, u32[]{:S(2)}) collective-permute-start(f32[256,256]{1,0:T(8,128)S(1)} %chip_maps.1._.refs_0_), channel_id=1, source_target_pairs={{0,2},{1,3},{2,0},{3,1},{4,6},{5,7},{6,4},{7,5},{8,10},{9,11},{10,... | collective-permute-start | bytes 786440 | tf_op jit(solution)/shard_map/ppermute | solution.py:574
  17.6 12.2 %copy-start.4 = (f32[256]{0:T(256)S(1)}, f32[256]{0:T(256)}, u32[]{:S(2)}) copy-start(f32[256]{0:T(256)} %param.10) | copy-start | bytes 3076
  17.6 12.2 %copy-start.5 = (f32[256]{0:T(256)S(1)}, f32[256]{0:T(256)}, u32[]{:S(2)}) copy-start(f32[256]{0:T(256)} %param.9) | copy-start | bytes 3076
  24.1 1.4 %collective-permute-start.4 = (f32[144,256]{1,0:T(8,128)S(1)}, f32[144,256]{1,0:T(8,128)S(1)}, u32[]{:S(2)}, u32[]{:S(2)}) collective-permute-start(f32[144,256]{1,0:T(8,128)S(1)} %get-tuple-element.49.own_ref), channel_id=1, source_target_pairs={{0,1},{1,0},{2,3},{3,2},{4,5},{5,4},{6,7},{7,6},{8,9},{9,8},{10,11... | collective-permute-start | bytes 442376 | tf_op jit(solution)/shard_map/ppermute | solution.py:574
  26.0 6.8 %collective-permute-start.9 = (f32[72,256]{1,0:T(8,128)S(1)}, f32[72,256]{1,0:T(8,128)S(1)}, u32[]{:S(2)}, u32[]{:S(2)}) collective-permute-start(f32[72,256]{1,0:T(8,128)S(1)} %get-tuple-element.55), channel_id=1, source_target_pairs={{0,6},{1,7},{2,4},{3,5},{4,2},{5,3},{6,0},{7,1},{8,14},{9,15},{10,... | collective-permute-start | bytes 221192 | tf_op jit(solution)/shard_map/ppermute | solution.py:574
  28.9 4.4 %collective-permute-start.7 = (f32[72,256]{1,0:T(8,128)S(1)}, f32[72,256]{1,0:T(8,128)S(1)}, u32[]{:S(2)}, u32[]{:S(2)}) collective-permute-start(f32[72,256]{1,0:T(8,128)S(1)} %get-tuple-element.55), channel_id=1, source_target_pairs={{0,4},{1,5},{2,6},{3,7},{4,0},{5,1},{6,2},{7,3},{8,12},{9,13},{10,... | collective-permute-start | bytes 221192 | tf_op jit(solution)/shard_map/ppermute | solution.py:574
  29.4 4.4 %collective-permute-start.5 = (f32[72,256]{1,0:T(8,128)S(1)}, f32[72,256]{1,0:T(8,128)S(1)}, u32[]{:S(2)}, u32[]{:S(2)}) collective-permute-start(f32[72,256]{1,0:T(8,128)S(1)} %get-tuple-element.55), channel_id=1, source_target_pairs={{0,2},{1,3},{2,0},{3,1},{4,6},{5,7},{6,4},{7,5},{8,10},{9,11},{10,... | collective-permute-start | bytes 221192 | tf_op jit(solution)/shard_map/ppermute | solution.py:574
  30.9 7.3 %collective-permute-start.11 = (f32[128,256]{1,0:T(8,128)S(1)}, f32[128,256]{1,0:T(8,128)S(1)}, u32[]{:S(2)}, u32[]{:S(2)}) collective-permute-start(f32[128,256]{1,0:T(8,128)S(1)} %get-tuple-element.66), channel_id=1, source_target_pairs={{0,8},{1,9},{2,10},{3,11},{4,12},{5,13},{6,14},{7,15},{8,0},{9,1},... | collective-permute-start | bytes 393224 | tf_op jit(solution)/shard_map/ppermute | solution.py:574
  32.8 1.3 %collective-permute-start.10 = (f32[72,256]{1,0:T(8,128)S(1)}, f32[72,256]{1,0:T(8,128)S(1)}, u32[]{:S(2)}, u32[]{:S(2)}) collective-permute-start(f32[72,256]{1,0:T(8,128)S(1)} %collective-permute-done.9.refs_5_), channel_id=1, source_target_pairs={{0,1},{1,0},{2,3},{3,2},{4,5},{5,4},{6,7},{7,6},{8,9},{9,8},{10,11... | collective-permute-start | bytes 221192 | tf_op jit(solution)/shard_map/ppermute | solution.py:574
  33.2 1.3 %collective-permute-start.8 = (f32[72,256]{1,0:T(8,128)S(1)}, f32[72,256]{1,0:T(8,128)S(1)}, u32[]{:S(2)}, u32[]{:S(2)}) collective-permute-start(f32[72,256]{1,0:T(8,128)S(1)} %collective-permute-done.7.refs_3_), channel_id=1, source_target_pairs={{0,1},{1,0},{2,3},{3,2},{4,5},{5,4},{6,7},{7,6},{8,9},{9,8},{10,11... | collective-permute-start | bytes 221192 | tf_op jit(solution)/shard_map/ppermute | solution.py:574
  33.8 1.3 %collective-permute-start.6 = (f32[72,256]{1,0:T(8,128)S(1)}, f32[72,256]{1,0:T(8,128)S(1)}, u32[]{:S(2)}, u32[]{:S(2)}) collective-permute-start(f32[72,256]{1,0:T(8,128)S(1)} %collective-permute-done.5.refs_1_), channel_id=1, source_target_pairs={{0,1},{1,0},{2,3},{3,2},{4,5},{5,4},{6,7},{7,6},{8,9},{9,8},{10,11... | collective-permute-start | bytes 221192 | tf_op jit(solution)/shard_map/ppermute | solution.py:574
  36.6 6.0 %collective-permute-start.13 = (f32[144,256]{1,0:T(8,128)S(1)}, f32[144,256]{1,0:T(8,128)S(1)}, u32[]{:S(2)}, u32[]{:S(2)}) collective-permute-start(f32[144,256]{1,0:T(8,128)S(1)} %get-tuple-element.76.own_ref), channel_id=1, source_target_pairs={{0,8},{1,9},{2,10},{3,11},{4,12},{5,13},{6,14},{7,15},{8,0},{9,1},... | collective-permute-start | bytes 442376 | tf_op jit(solution)/shard_map/ppermute | solution.py:574
  38.2 4.3 %collective-permute-start.12 = (f32[128,256]{1,0:T(8,128)S(1)}, f32[128,256]{1,0:T(8,128)S(1)}, u32[]{:S(2)}, u32[]{:S(2)}) collective-permute-start(f32[128,256]{1,0:T(8,128)S(1)} %collective-permute-done.11.refs_0_.r_ref), channel_id=1, source_target_pairs={{0,1},{1,0},{2,3},{3,2},{4,5},{5,4},{6,7},{7,6},{8,9},{9,8},{10,11... | collective-permute-start | bytes 393224 | tf_op jit(solution)/shard_map/ppermute | solution.py:574
  43.1 5.6 %collective-permute-start.14 = (f32[72,256]{1,0:T(8,128)S(1)}, f32[72,256]{1,0:T(8,128)S(1)}, u32[]{:S(2)}, u32[]{:S(2)}) collective-permute-start(f32[72,256]{1,0:T(8,128)S(1)} %level.1), channel_id=1, source_target_pairs={{0,16},{1,17},{2,18},{3,19},{4,20},{5,21},{6,22},{7,23},{8,24},{9,... | collective-permute-start | bytes 221192 | tf_op jit(solution)/shard_map/ppermute | solution.py:574
  48.6 1.3 %collective-permute-start.15 = (f32[72,256]{1,0:T(8,128)S(1)}, f32[72,256]{1,0:T(8,128)S(1)}, u32[]{:S(2)}, u32[]{:S(2)}) collective-permute-start(f32[72,256]{1,0:T(8,128)S(1)} %collective-permute-done.14.r_ref), channel_id=1, source_target_pairs={{0,1},{1,0},{2,3},{3,2},{4,5},{5,4},{6,7},{7,6},{8,9},{9,8},{10,11... | collective-permute-start | bytes 221192 | tf_op jit(solution)/shard_map/ppermute | solution.py:574

commit v8 on v7

--- a/solution.py
+++ b/solution.py
@@ -249,8 +249,8 @@
             shaped_ref[s, j] = shaped[s]
         return carry
 
-    lax.fori_loop(0, steps, see, 0, unroll=4)
-    lax.fori_loop(0, steps, shape_step, 0, unroll=4)
+    lax.fori_loop(0, steps, see, 0, unroll=8)
+    lax.fori_loop(0, steps, shape_step, 0, unroll=8)
 
 
 def noises_kernel(subs, decay_ref, e_ref, dcol_ref, shaped_ref, gain_ref, var_ref, shift_ref,

time: 54.1 us -> 53.5 us (0.989)
  Pallas kernels: 30 us -> 29.4 us
    pallas_call x11, Pallas kernels: 30 us -> 29.4 us  [call(): pl.pallas_call(kernel, in_specs=specs or [vmem()] * len(args), out_specs=...]
  transfers between devices with their start and end apart: 16 -> 16, of which waited for: 10 -> 10; matrix products, arithmetic and copies ran while one was open for 0% -> 0% of each run, Pallas kernels for 29% -> 28%
where the time goes in v8:
time: 53.5 us; the launch traced here: 53.4 us
  Pallas kernels  29.4 us (55%)
  starting transfers between devices  14.6 us (27%)
  waiting for transfers between devices  8.6 us (16%)
  between operations  0.77 us (1%)
    pallas_call x11, Pallas kernels, call(): pl.pallas_call(kernel, in_specs=specs or [vmem()] * len(args), out_specs=...  29.4 us
    ppermute x16, starting transfers between devices, swap(): return lax.ppermute(x, names, [(k, k ^ bit) for k in range(count)])  14.6 us
    ppermute x16, waiting for transfers between devices, swap(): return lax.ppermute(x, names, [(k, k ^ bit) for k in range(count)])  8.6 us
  transfers between devices with their start and end apart: 16, of which 10 were waited for; matrix products, arithmetic and copies ran while one was open for 0% of the time, Pallas kernels for 28%

profile of v8, /device:TPU:0, one launch (start us, length us, event | category | flops | bytes accessed | tf_op | source)
XLA Modules:
  0.0 53.4 jit_solution(12990025634864054513)
XLA Ops:
  0.6 0.0 copy-start
  0.6 0.0 copy-start.1
  0.7 9.7 %step_maps.1 = (f32[4,8,256,256]{3,2,1,0:T(8,128)S(1)}, bf16[4,8,256,256]{3,2,1,0:T(8,128)(2,1)S(1)}, f32[4,8,256,128]{3,2,1,0:T(8,128)S(1)}, f32[32,256]{1,0:T(...) custom-call(f32[32,256]{1,0:T(8,128)} %decay_ref.1, ...), custom_call_target="tpu_custom_call" | custom-call | flops 10000000000 | tf_op jit(solution)/shard_map/step_maps/pallas_call | solution.py:506
  10.4 0.5 collective-permute-start
  10.9 0.0 copy-start.6
  10.9 1.5 %step_shapes.1._.shaped_ref = bf16[4,8,256,256]{3,2,1,0:T(8,128)(2,1)S(1)} custom-call(bf16[4,8,64,256]{3,2,1,0:T(8,128)(2,1)S(1)} %bitcast.10, bf16[4,8,64,256]{3,2,1,0:T(8,128)(2,1)S(1)} %bitcast.7, bf16[256,256]{1,0:T(8,128)(2,1)S(1)} %copy-done.2, f32[32,256]{1,0:T(8,128)S(1)} %get-tuple-element.41._.delta_ref), custom_call_target="tpu_custom_call" | custom-call | flops 100000 | tf_op jit(solution)/shard_map/step_shapes/pallas_call | solution.py:506
  12.5 0.0 collective-permute-done.other_ref.other_map_ref.refs_4_
  12.5 0.3 chip_maps.1._.refs_0_
  12.8 3.5 %collective-permute-start.3 = (f32[256,256]{1,0:T(8,128)S(1)}, f32[256,256]{1,0:T(8,128)S(1)}, u32[]{:S(2)}, u32[]{:S(2)}) collective-permute-start(f32[256,256]{1,0:T(8,128)S(1)} %chip_maps.1._.refs_0_), channel_id=1, source_target_pairs={{0,6},{1,7},{2,4},{3,5},{4,2},{5,3},{6,0},{7,1},{8,14},{9,15},{10,... | collective-permute-start | bytes 786440 | tf_op jit(solution)/shard_map/ppermute | solution.py:574
  16.3 0.5 collective-permute-start.2
  16.8 0.1 collective-permute-start.1
  17.0 0.0 copy-done.6
  17.0 6.5 %step_noises.1 = (f32[32,256]{1,0:T(8,128)S(1)}, f32[4,272,256]{2,1,0:T(8,128)S(1)}, f32[144,256]{1,0:T(8,128)S(1)}) custom-call(f32[32,256]{1,0:T(8,128)S(1)} %copy-done.3, bf16[4,8,256,256]{3,2,1,0:T(8,128)(2,1)S(1)} %get-tuple-element.42.e_ref, f32[4,8,256,128]{3,2,1,0:T(8,128)S(1)} %get-tuple-element.43.dcol_ref, ...), custom_call_target="tpu_custom_call" | custom-call | flops 100000 | tf_op jit(solution)/shard_map/step_noises/pallas_call | solution.py:506
  23.5 0.1 collective-permute-start.4
  23.6 1.4 %collective-permute-done.4.other_ref.refs_12_ = f32[144,256]{1,0:T(8,128)S(1)} collective-permute-done((f32[144,256]{1,0:T(8,128)S(1)}, f32[144,256]{1,0:T(8,128)S(1)}, u32[]{:S(2)}, u32[]{:S(2)}) %collective-permute-start.4) | collective-permute-done | bytes 147488 | tf_op jit(solution)/shard_map/ppermute | solution.py:574
  25.0 0.5 core_noises.1
  25.4 2.9 %collective-permute-start.9 = (f32[72,256]{1,0:T(8,128)S(1)}, f32[72,256]{1,0:T(8,128)S(1)}, u32[]{:S(2)}, u32[]{:S(2)}) collective-permute-start(f32[72,256]{1,0:T(8,128)S(1)} %get-tuple-element.55), channel_id=1, source_target_pairs={{0,6},{1,7},{2,4},{3,5},{4,2},{5,3},{6,0},{7,1},{8,14},{9,15},{10,... | collective-permute-start | bytes 221192 | tf_op jit(solution)/shard_map/ppermute | solution.py:574
  28.3 0.5 collective-permute-start.7
  28.8 0.0 collective-permute-done.3.refs_3_
  28.8 0.1 collective-permute-start.5
  29.0 0.0 collective-permute-done.2.refs_2_
  29.0 0.2 collective-permute-done.1.refs_1_
  29.2 0.0 copy-done.5
  29.2 1.1 %plane_maps.1 = (f32[3,256,256]{2,1,0:T(8,128)S(1)}, bf16[3,256,256]{2,1,0:T(8,128)(2,1)S(1)}, f32[3,256,128]{2,1,0:T(8,128)S(1)}, f32[8,256]{1,0:T(8,128)S(1)},...) custom-call(f32[256,256]{1,0:T(8,128)S(1)} %chip_maps.1._.refs_0_, ...), custom_call_target="tpu_custom_call" | custom-call | flops 100000 | tf_op jit(solution)/shard_map/plane_maps/pallas_call | solution.py:506
  30.3 1.9 %collective-permute-start.11 = (f32[128,256]{1,0:T(8,128)S(1)}, f32[128,256]{1,0:T(8,128)S(1)}, u32[]{:S(2)}, u32[]{:S(2)}) collective-permute-start(f32[128,256]{1,0:T(8,128)S(1)} %get-tuple-element.66), channel_id=1, source_target_pairs={{0,8},{1,9},{2,10},{3,11},{4,12},{5,13},{6,14},{7,15},{8,0},{9,1},... | collective-permute-start | bytes 393224 | tf_op jit(solution)/shard_map/ppermute | solution.py:574
  32.2 0.0 collective-permute-done.9.refs_5_
  32.2 0.0 collective-permute-start.10
  32.2 0.4 collective-permute-done.7.refs_3_
  32.7 0.1 collective-permute-start.8
  32.7 0.4 collective-permute-done.5.refs_1_
  33.2 0.0 collective-permute-start.6
  33.2 0.3 collective-permute-done.10.refs_6_
  33.5 0.4 collective-permute-done.8.refs_4_
  33.9 0.5 collective-permute-done.6.refs_2_
  34.5 1.6 %plane_noises.1 = (f32[144,256]{1,0:T(8,128)S(1)}, f32[3,272,256]{2,1,0:T(8,128)S(1)}) custom-call(f32[144,256]{1,0:T(8,128)S(1)} %get-tuple-element.50.refs_0_, f32[72,256]{1,0:T(8,128)S(1)} %collective-permute-done.5.refs_1_, f32[72,256]{1,0:T(8,128)S(1)} %collective-permute-done.6.refs_2_, f32[72,256]{1,0:T(8,128)S(1)} %collective-permute-done.7.refs_3_, ...), custom_call_target="tpu_custom_call" | custom-call | flops 100000 | tf_op jit(solution)/shard_map/plane_noises/pallas_call | solution.py:506
  36.0 1.6 %collective-permute-start.13 = (f32[144,256]{1,0:T(8,128)S(1)}, f32[144,256]{1,0:T(8,128)S(1)}, u32[]{:S(2)}, u32[]{:S(2)}) collective-permute-start(f32[144,256]{1,0:T(8,128)S(1)} %get-tuple-element.76.own_ref), channel_id=1, source_target_pairs={{0,8},{1,9},{2,10},{3,11},{4,12},{5,13},{6,14},{7,15},{8,0},{9,1},... | collective-permute-start | bytes 442376 | tf_op jit(solution)/shard_map/ppermute | solution.py:574
  37.7 0.0 collective-permute-done.11.refs_0_.r_ref
  37.7 0.0 collective-permute-start.12
  37.7 3.4 %place.1 = (f32[4,528,256]{2,1,0:T(8,128)S(1)}, bf16[4,256,256]{2,1,0:T(8,128)(2,1)S(1)}, f32[4,256,128]{2,1,0:T(8,128)S(1)}, f32[4,8,256]{2,1,0:T(8,128)S(1)}) custom-call(f32[6,256,256]{2,1,0:T(8,128)S(1)} %get-tuple-element.45.maps_ref.subs_ref, f32[4,272,256]{2,1,0:T(8,128)S(1)} %get-tuple-element.48.sub_noises_ref, ...), custom_call_target="tpu_custom_call" | custom-call | flops 100000 | tf_op jit(solution)/shard_map/place/pallas_call | solution.py:506
  41.1 0.9 %collective-permute-done.13.refs_2_.other_ref = f32[144,256]{1,0:T(8,128)S(1)} collective-permute-done((f32[144,256]{1,0:T(8,128)S(1)}, f32[144,256]{1,0:T(8,128)S(1)}, u32[]{:S(2)}, u32[]{:S(2)}) %collective-permute-start.13) | collective-permute-done | bytes 147488 | tf_op jit(solution)/shard_map/ppermute | solution.py:574
  42.0 0.0 collective-permute-done.12.refs_1_.x_ref
  42.0 0.5 level.1
  42.5 2.7 %collective-permute-start.14 = (f32[72,256]{1,0:T(8,128)S(1)}, f32[72,256]{1,0:T(8,128)S(1)}, u32[]{:S(2)}, u32[]{:S(2)}) collective-permute-start(f32[72,256]{1,0:T(8,128)S(1)} %level.1), channel_id=1, source_target_pairs={{0,16},{1,17},{2,18},{3,19},{4,20},{5,21},{6,22},{7,23},{8,24},{9,... | collective-permute-start | bytes 221192 | tf_op jit(solution)/shard_map/ppermute | solution.py:574
  45.1 0.2 before.1
  45.3 2.7 %collective-permute-done.14.r_ref = f32[72,256]{1,0:T(8,128)S(1)} collective-permute-done((f32[72,256]{1,0:T(8,128)S(1)}, f32[72,256]{1,0:T(8,128)S(1)}, u32[]{:S(2)}, u32[]{:S(2)}) %collective-permute-start.14) | collective-permute-done | bytes 73760 | tf_op jit(solution)/shard_map/ppermute | solution.py:574
  48.1 0.0 collective-permute-start.15
  48.1 1.3 %collective-permute-done.15.x_ref = f32[72,256]{1,0:T(8,128)S(1)} collective-permute-done((f32[72,256]{1,0:T(8,128)S(1)}, f32[72,256]{1,0:T(8,128)S(1)}, u32[]{:S(2)}, u32[]{:S(2)}) %collective-permute-start.15) | collective-permute-done | bytes 73760 | tf_op jit(solution)/shard_map/ppermute | solution.py:574
  49.3 4.1 %finish.1 = (f32[32,256]{1,0:T(8,128)}, f32[32,256]{1,0:T(8,128)}) custom-call(f32[4,8,256,256]{3,2,1,0:T(8,128)S(1)} %get-tuple-element.40.g_ref, f32[32,256]{1,0:T(8,128)S(1)} %get-tuple-element.41._.delta_ref, f32[32,256]{1,0:T(8,128)S(1)} %get-tuple-element.47.var_ref, f32[32,256]{1,0:T(8,128)S(1)} %get-tuple-element.44.shift_ref.mean_ref, ...), custom_call_target="tpu_custom_call" | custom-call | flops 100000 | tf_op jit(solution)/shard_map/finish/pallas_call | solution.py:506
  (9 shorter events, 0.0 us)
Async XLA Ops:
  0.6 10.3 %copy-start = (bf16[32,64,256]{2,1,0:T(8,128)(2,1)S(1)}, bf16[32,64,256]{2,1,0:T(8,128)(2,1)}, u32[]{:S(2)}) copy-start(bf16[32,64,256]{2,1,0:T(8,128)(2,1)} %param.14) | copy-start | bytes 3145732
  0.6 10.3 %copy-start.1 = (bf16[32,64,256]{2,1,0:T(8,128)(2,1)S(1)}, bf16[32,64,256]{2,1,0:T(8,128)(2,1)}, u32[]{:S(2)}) copy-start(bf16[32,64,256]{2,1,0:T(8,128)(2,1)} %param.13) | copy-start | bytes 3145732
  0.7 10.3 %copy-start.2 = (bf16[256,256]{1,0:T(8,128)(2,1)S(1)}, bf16[256,256]{1,0:T(8,128)(2,1)}, u32[]{:S(2)}) copy-start(bf16[256,256]{1,0:T(8,128)(2,1)} %nf_ref.1) | copy-start | bytes 393220
  10.4 2.1 %collective-permute-start = (f32[256,256]{1,0:T(8,128)S(1)}, f32[256,256]{1,0:T(8,128)S(1)}, u32[]{:S(2)}, u32[]{:S(2)}) collective-permute-start(f32[256,256]{1,0:T(8,128)S(1)} %get-tuple-element.46.own_ref.own_map_ref), channel_id=1, source_target_pairs={{0,1},{1,0},{2,3},{3,2},{4,5},{5,4},{6,7},{7,6},{8,9},{9,8},{10,11... | collective-permute-start | bytes 786440 | tf_op jit(solution)/shard_map/ppermute | solution.py:574
  10.9 6.1 %copy-start.3 = (f32[32,256]{1,0:T(8,128)S(1)}, f32[32,256]{1,0:T(8,128)}, u32[]{:S(2)}) copy-start(f32[32,256]{1,0:T(8,128)} %decay_ref.1) | copy-start | bytes 98308
  10.9 6.1 %copy-start.6 = (f32[64]{0:T(128)S(1)}, f32[64]{0:T(128)}, u32[]{:S(2)}) copy-start(f32[64]{0:T(128)} %param.16) | copy-start | bytes 772
  12.8 16.0 %collective-permute-start.3 = (f32[256,256]{1,0:T(8,128)S(1)}, f32[256,256]{1,0:T(8,128)S(1)}, u32[]{:S(2)}, u32[]{:S(2)}) collective-permute-start(f32[256,256]{1,0:T(8,128)S(1)} %chip_maps.1._.refs_0_), channel_id=1, source_target_pairs={{0,6},{1,7},{2,4},{3,5},{4,2},{5,3},{6,0},{7,1},{8,14},{9,15},{10,... | collective-permute-start | bytes 786440 | tf_op jit(solution)/shard_map/ppermute | solution.py:574
  16.3 12.6 %collective-permute-start.2 = (f32[256,256]{1,0:T(8,128)S(1)}, f32[256,256]{1,0:T(8,128)S(1)}, u32[]{:S(2)}, u32[]{:S(2)}) collective-permute-start(f32[256,256]{1,0:T(8,128)S(1)} %chip_maps.1._.refs_0_), channel_id=1, source_target_pairs={{0,4},{1,5},{2,6},{3,7},{4,0},{5,1},{6,2},{7,3},{8,12},{9,13},{10,... | collective-permute-start | bytes 786440 | tf_op jit(solution)/shard_map/ppermute | solution.py:574
  16.8 12.3 %collective-permute-start.1 = (f32[256,256]{1,0:T(8,128)S(1)}, f32[256,256]{1,0:T(8,128)S(1)}, u32[]{:S(2)}, u32[]{:S(2)}) collective-permute-start(f32[256,256]{1,0:T(8,128)S(1)} %chip_maps.1._.refs_0_), channel_id=1, source_target_pairs={{0,2},{1,3},{2,0},{3,1},{4,6},{5,7},{6,4},{7,5},{8,10},{9,11},{10,... | collective-permute-start | bytes 786440 | tf_op jit(solution)/shard_map/ppermute | solution.py:574
  17.0 12.2 %copy-start.4 = (f32[256]{0:T(256)S(1)}, f32[256]{0:T(256)}, u32[]{:S(2)}) copy-start(f32[256]{0:T(256)} %param.10) | copy-start | bytes 3076
  17.0 12.2 %copy-start.5 = (f32[256]{0:T(256)S(1)}, f32[256]{0:T(256)}, u32[]{:S(2)}) copy-start(f32[256]{0:T(256)} %param.9) | copy-start | bytes 3076
  23.5 1.4 %collective-permute-start.4 = (f32[144,256]{1,0:T(8,128)S(1)}, f32[144,256]{1,0:T(8,128)S(1)}, u32[]{:S(2)}, u32[]{:S(2)}) collective-permute-start(f32[144,256]{1,0:T(8,128)S(1)} %get-tuple-element.49.own_ref), channel_id=1, source_target_pairs={{0,1},{1,0},{2,3},{3,2},{4,5},{5,4},{6,7},{7,6},{8,9},{9,8},{10,11... | collective-permute-start | bytes 442376 | tf_op jit(solution)/shard_map/ppermute | solution.py:574
  25.4 6.8 %collective-permute-start.9 = (f32[72,256]{1,0:T(8,128)S(1)}, f32[72,256]{1,0:T(8,128)S(1)}, u32[]{:S(2)}, u32[]{:S(2)}) collective-permute-start(f32[72,256]{1,0:T(8,128)S(1)} %get-tuple-element.55), channel_id=1, source_target_pairs={{0,6},{1,7},{2,4},{3,5},{4,2},{5,3},{6,0},{7,1},{8,14},{9,15},{10,... | collective-permute-start | bytes 221192 | tf_op jit(solution)/shard_map/ppermute | solution.py:574
  28.3 4.4 %collective-permute-start.7 = (f32[72,256]{1,0:T(8,128)S(1)}, f32[72,256]{1,0:T(8,128)S(1)}, u32[]{:S(2)}, u32[]{:S(2)}) collective-permute-start(f32[72,256]{1,0:T(8,128)S(1)} %get-tuple-element.55), channel_id=1, source_target_pairs={{0,4},{1,5},{2,6},{3,7},{4,0},{5,1},{6,2},{7,3},{8,12},{9,13},{10,... | collective-permute-start | bytes 221192 | tf_op jit(solution)/shard_map/ppermute | solution.py:574
  28.8 4.4 %collective-permute-start.5 = (f32[72,256]{1,0:T(8,128)S(1)}, f32[72,256]{1,0:T(8,128)S(1)}, u32[]{:S(2)}, u32[]{:S(2)}) collective-permute-start(f32[72,256]{1,0:T(8,128)S(1)} %get-tuple-element.55), channel_id=1, source_target_pairs={{0,2},{1,3},{2,0},{3,1},{4,6},{5,7},{6,4},{7,5},{8,10},{9,11},{10,... | collective-permute-start | bytes 221192 | tf_op jit(solution)/shard_map/ppermute | solution.py:574
  30.3 7.3 %collective-permute-start.11 = (f32[128,256]{1,0:T(8,128)S(1)}, f32[128,256]{1,0:T(8,128)S(1)}, u32[]{:S(2)}, u32[]{:S(2)}) collective-permute-start(f32[128,256]{1,0:T(8,128)S(1)} %get-tuple-element.66), channel_id=1, source_target_pairs={{0,8},{1,9},{2,10},{3,11},{4,12},{5,13},{6,14},{7,15},{8,0},{9,1},... | collective-permute-start | bytes 393224 | tf_op jit(solution)/shard_map/ppermute | solution.py:574
  32.2 1.3 %collective-permute-start.10 = (f32[72,256]{1,0:T(8,128)S(1)}, f32[72,256]{1,0:T(8,128)S(1)}, u32[]{:S(2)}, u32[]{:S(2)}) collective-permute-start(f32[72,256]{1,0:T(8,128)S(1)} %collective-permute-done.9.refs_5_), channel_id=1, source_target_pairs={{0,1},{1,0},{2,3},{3,2},{4,5},{5,4},{6,7},{7,6},{8,9},{9,8},{10,11... | collective-permute-start | bytes 221192 | tf_op jit(solution)/shard_map/ppermute | solution.py:574
  32.7 1.3 %collective-permute-start.8 = (f32[72,256]{1,0:T(8,128)S(1)}, f32[72,256]{1,0:T(8,128)S(1)}, u32[]{:S(2)}, u32[]{:S(2)}) collective-permute-start(f32[72,256]{1,0:T(8,128)S(1)} %collective-permute-done.7.refs_3_), channel_id=1, source_target_pairs={{0,1},{1,0},{2,3},{3,2},{4,5},{5,4},{6,7},{7,6},{8,9},{9,8},{10,11... | collective-permute-start | bytes 221192 | tf_op jit(solution)/shard_map/ppermute | solution.py:574
  33.2 1.3 %collective-permute-start.6 = (f32[72,256]{1,0:T(8,128)S(1)}, f32[72,256]{1,0:T(8,128)S(1)}, u32[]{:S(2)}, u32[]{:S(2)}) collective-permute-start(f32[72,256]{1,0:T(8,128)S(1)} %collective-permute-done.5.refs_1_), channel_id=1, source_target_pairs={{0,1},{1,0},{2,3},{3,2},{4,5},{5,4},{6,7},{7,6},{8,9},{9,8},{10,11... | collective-permute-start | bytes 221192 | tf_op jit(solution)/shard_map/ppermute | solution.py:574
  36.0 6.0 %collective-permute-start.13 = (f32[144,256]{1,0:T(8,128)S(1)}, f32[144,256]{1,0:T(8,128)S(1)}, u32[]{:S(2)}, u32[]{:S(2)}) collective-permute-start(f32[144,256]{1,0:T(8,128)S(1)} %get-tuple-element.76.own_ref), channel_id=1, source_target_pairs={{0,8},{1,9},{2,10},{3,11},{4,12},{5,13},{6,14},{7,15},{8,0},{9,1},... | collective-permute-start | bytes 442376 | tf_op jit(solution)/shard_map/ppermute | solution.py:574
  37.7 4.3 %collective-permute-start.12 = (f32[128,256]{1,0:T(8,128)S(1)}, f32[128,256]{1,0:T(8,128)S(1)}, u32[]{:S(2)}, u32[]{:S(2)}) collective-permute-start(f32[128,256]{1,0:T(8,128)S(1)} %collective-permute-done.11.refs_0_.r_ref), channel_id=1, source_target_pairs={{0,1},{1,0},{2,3},{3,2},{4,5},{5,4},{6,7},{7,6},{8,9},{9,8},{10,11... | collective-permute-start | bytes 393224 | tf_op jit(solution)/shard_map/ppermute | solution.py:574
  42.5 5.6 %collective-permute-start.14 = (f32[72,256]{1,0:T(8,128)S(1)}, f32[72,256]{1,0:T(8,128)S(1)}, u32[]{:S(2)}, u32[]{:S(2)}) collective-permute-start(f32[72,256]{1,0:T(8,128)S(1)} %level.1), channel_id=1, source_target_pairs={{0,16},{1,17},{2,18},{3,19},{4,20},{5,21},{6,22},{7,23},{8,24},{9,... | collective-permute-start | bytes 221192 | tf_op jit(solution)/shard_map/ppermute | solution.py:574
  48.1 1.3 %collective-permute-start.15 = (f32[72,256]{1,0:T(8,128)S(1)}, f32[72,256]{1,0:T(8,128)S(1)}, u32[]{:S(2)}, u32[]{:S(2)}) collective-permute-start(f32[72,256]{1,0:T(8,128)S(1)} %collective-permute-done.14.r_ref), channel_id=1, source_target_pairs={{0,1},{1,0},{2,3},{3,2},{4,5},{5,4},{6,7},{7,6},{8,9},{9,8},{10,11... | collective-permute-start | bytes 221192 | tf_op jit(solution)/shard_map/ppermute | solution.py:574
